TPU v7x, 32 devices: a whole 2x2x4 slice. The times are simulated.
32 devices in a mesh: section: 16 (over z, y, core), tp: 2 (over x).
Axes of the slice: x: 2, y: 2, z: 4, core: 2. Of those that a mesh axis runs over, the one named last changes fastest.
Arguments:
- block_input: bfloat16 [16, 2, 128, 4096], P('section', None, None, 'tp'), may hold values from -6 to 6
- incoming: bfloat16 [16, 2, 128, 4096], P('section', None, None, 'tp'), may hold values from -6 to 6
- in_weight: bfloat16 [16, 4096, 3, 4096], P('section', None, None, 'tp'), may hold values from -0.09375 to 0.09375
- short_taps: float32 [16, 7, 3, 4096], P('section', None, None, 'tp'), may hold values from -2.5 to 2.5
- medium_taps: float32 [16, 128, 256], P('section', None, 'tp'), may hold values from -0.625 to 0.625
- skip_weight: float32 [16, 4096], P('section', 'tp'), may hold values from 0.5 to 1.5
Outputs:
- passed: bfloat16 [16, 2, 128, 4096], P('section', None, None, 'tp')
All inputs are finite; a program needn't handle non-finite values.
Results may differ from a plain program's by a relative error of at most 0.0049.
Values may be sent and summed in bfloat16 or wider, within the bound.
No kernel may reach another device: no remote copies, remote signals or barrier semaphores. Data moves between devices by JAX's collectives and lax.ppermute only.
A program may use at most 192 MiB of HBM per device.

v0:
```python
import jax
import jax.numpy as jnp
from jax import lax
from jax.sharding import PartitionSpec as P


def shifted(value, axis, steps):
    count = lax.axis_size(axis)
    pairs = [(source, (source + steps) % count) for source in range(count)]
    return lax.ppermute(value, axis, pairs)


def causal_taps(series, taps):
    length = series.shape[1]
    reach = taps.shape[0]
    padded = jnp.pad(series, ((0, 0), (reach - 1, 0), (0, 0), (0, 0)))
    result = jnp.zeros(series.shape, jnp.float32)
    for offset in range(reach):
        first = reach - 1 - offset
        result = result + taps[offset] * padded[:, first : first + length]
    return result


def anti_taps(series, taps):
    length = series.shape[1]
    reach = taps.shape[0]
    padded = jnp.pad(series, ((0, 0), (0, reach - 1), (0, 0), (0, 0)))
    result = jnp.zeros(series.shape, jnp.float32)
    for offset in range(reach):
        result = result + taps[offset] * padded[:, offset : offset + length]
    return result


def toeplitz_of(medium, length):
    reach = medium.shape[0]
    places = jnp.arange(length, dtype=jnp.int32)
    lag_table = places[:, None] - places[None, :]
    inside = (lag_table >= 0) & (lag_table < reach)
    lag_index = jnp.clip(lag_table, 0, reach - 1)
    looked = jnp.take(medium.T, lag_index, axis=1)
    return jnp.where(inside[None, :, :], looked, jnp.zeros((), jnp.float32))


def time_last(series, groups):
    micro_count, length, channels = series.shape
    turned = jnp.transpose(series, (0, 2, 1))
    return turned.reshape(micro_count, groups, channels // groups, length)


def time_back(series):
    micro_count, groups, members, length = series.shape
    merged = series.reshape(micro_count, groups * members, length)
    return jnp.transpose(merged, (0, 2, 1))


def section_backward(block_input, incoming, weights, short_taps, toeplitz_mat, skip_weight):
    micro_count = block_input.shape[1]
    length = block_input.shape[2]
    channels = skip_weight.shape[0]
    groups = toeplitz_mat.shape[0]
    portion = lax.all_gather(block_input, "tp", axis=3, tiled=True)
    slab_rows = weights
    flattened = portion.reshape(micro_count * length, portion.shape[3])
    projected = jnp.dot(flattened, slab_rows, preferred_element_type=jnp.float32)
    projected = projected.reshape(micro_count, length, 3, channels)
    featured = causal_taps(projected, short_taps)
    query = featured[:, :, 0]
    key_part = featured[:, :, 1]
    value_part = featured[:, :, 2]
    product = key_part * value_part
    grouped = time_last(product, groups)
    mixed = jnp.einsum("gts,bgcs->bgct", toeplitz_mat, grouped, precision=lax.Precision.HIGHEST)
    mixed = time_back(mixed) + skip_weight * product
    upstream = incoming[0].astype(jnp.float32)
    query_grad = upstream * mixed
    mixed_grad = upstream * query
    grouped_grad = time_last(mixed_grad, groups)
    product_grad = jnp.einsum(
        "gts,bgct->bgcs", toeplitz_mat, grouped_grad, precision=lax.Precision.HIGHEST
    )
    product_grad = time_back(product_grad) + skip_weight * mixed_grad
    stream_grad = jnp.stack(
        [query_grad, product_grad * value_part, product_grad * key_part], axis=2
    )
    conv_grad = anti_taps(stream_grad, short_taps).astype(jnp.bfloat16)
    conv_flat = conv_grad.reshape(micro_count * length, 3 * channels)
    slab_rows = weights
    own_share = lax.psum_scatter(
        lax.dot_general(
            slab_rows, conv_flat, (((1,), (1,)), ((), ())), preferred_element_type=jnp.float32
        ),
        "tp",
        scatter_dimension=0,
        tiled=True,
    )
    summed = upstream + own_share.T.reshape(micro_count, length, channels)
    result = summed.astype(jnp.bfloat16)[None]
    return shifted(result, "section", -1)


def local(block_input, incoming, in_weight, short_taps, medium_taps, skip_weight):
    model_width = in_weight.shape[1]
    channels = in_weight.shape[3]
    weights = in_weight[0].reshape(model_width, 3 * channels)
    toeplitz_mat = toeplitz_of(medium_taps[0], block_input.shape[2])
    return section_backward(
        block_input, incoming, weights, short_taps[0], toeplitz_mat, skip_weight[0]
    )


def solution(mesh):
    in_specs = (
        P("section", None, None, "tp"),
        P("section", None, None, "tp"),
        P("section", None, None, "tp"),
        P("section", None, None, "tp"),
        P("section", None, "tp"),
        P("section", "tp"),
    )
    out_specs = P("section", None, None, "tp")
    return jax.shard_map(local, mesh=mesh, in_specs=in_specs, out_specs=out_specs, check_vma=False)
```

profile of v0, /device:TPU:1, one launch (start us, length us, event | category | flops | bytes accessed | tf_op | source)
XLA Modules:
  0.0 352.6 jit_solution(3633009456991187988)
XLA Ops:
  6.5 0.0 copy-start
  6.5 0.0 all-gather.2.cloned.1.call-start
  6.5 0.7 all-gather.2.cloned.1.call-update
  7.3 0.0 reduce-scatter.2.cloned.1.call-start
  7.3 0.9 fusion.55
  8.2 62.6 %copy.22 = bf16[1,4096,3,2048]{1,3,2,0:T(8,128)(2,1)} copy(bf16[1,4096,3,2048]{3,1,2,0:T(8,128)(2,1)} %param.8) | data formatting | bytes 100663296 | tf_op args[2]
  70.9 0.0 copy-done
  70.9 54.4 %gather_fusion = f32[16384,128]{1,0:T(8,128)} fusion(f32[128,128]{0,1:T(8,128)S(1)} %bitcast.146, s32[16384]{0:T(1024)S(1)} %fusion.44), kind=kCustom, calls=%fused_computation | custom fusion | bytes 16842752 | tf_op jit(solution)/shard_map/jit(_take)/gather | solution.py:40
  125.3 9.3 %copy.34 = f32[128,128,128]{1,0,2:T(8,128)} copy(f32[128,128,128]{2,1,0:T(8,128)} %bitcast.148) | data formatting | bytes 16777216 | tf_op jit(solution)/shard_map/jit(_take)/gather | solution.py:40
  134.7 0.0 all-gather.2.cloned.1.call-done
  134.8 22.9 %fusion = f32[2,128,3,2048]{3,1,2,0:T(8,128)} fusion(bf16[1,4096,3,2048]{1,3,2,0:T(8,128)(2,1)} %copy.22, bf16[1,2,128,4096]{3,2,1,0:T(8,128)(2,1)} %all-gather.2.cloned.1.call-done), kind=kOutput, calls=%fused_computation.1 | convolution fusion | flops 12884901888 | bytes 58720256 | tf_op jit(solution)/shard_map/dot_general | solution.py:64
  157.7 0.0 copy-start.2
  157.7 22.6 %pad_slice_fusion.4 = (f32[2,128,3,2048]{3,1,2,0:T(8,128)S(1)}, f32[2,128,3,2048]{3,1,2,0:T(8,128)}, f32[2,128,3,2048]{3,1,2,0:T(8,128)}, f32[2,128,3,2048]{3,1,2,0:T(8,128)}, f32[2,128,3,2048]{3,1,2,0:T(8,128)}) fusion(f32[2,128,3,2048]{3,1,2,0:T(8,128)} %fusion), kind=kLoop, calls=%fused_computation.28 | loop fusion | bytes 37748736 | tf_op jit(solution)/shard_map/slice | solution.py:20
  180.3 0.0 copy-done.2
  180.3 0.0 copy-start.4
  180.3 10.8 %copy_add_fusion = f32[2,128,3,2048]{3,1,2,0:T(8,128)S(1)} fusion(f32[2,128,3,2048]{3,1,2,0:T(8,128)S(1)} %copy-done.2, f32[3,2048]{1,0:T(4,128)S(1)} %get-tuple-element.22, f32[2,128,3,2048]{3,1,2,0:T(8,128)} %get-tuple-element.14, f32[2,128,3,2048]{3,1,2,0:T(8,128)} %get-tuple-element.13, f32[2,128,3,2048]{3,1,2,0:T(8,128)} %get-tuple-element.12, ...), kind=kLoop, calls=%fused_computation.19 | loop fusion | flops 20447232 | bytes 50561024 | tf_op jit(solution)/shard_map/add | solution.py:20
  191.1 0.0 copy-start.3
  191.1 2.7 copy-done.3
  193.9 0.0 copy-done.4
  193.9 2.1 fusion.42
  196.0 1.8 copy.33
  197.8 15.7 %fusion.31 = f32[2,128,16,128]{3,2,0,1:T(8,128)S(1)} fusion(f32[128,128,128]{1,0,2:T(8,128)} %copy.34, pred[128,128]{1,0:T(8,128)(4,1)S(1)} %get-tuple-element.29, pred[128,128]{1,0:T(8,128)(4,1)S(1)} %get-tuple-element.28, f32[2,128,16,128]{3,2,1,0:T(8,128)} %bitcast.153), kind=kOutput, calls=%fused_computation.58 | convolution fusion | flops 809500672 | bytes 12615680 | tf_op jit(solution)/shard_map/gts,bgcs->bgct/dot_general | solution.py:72
  213.5 0.2 copy.36
  213.6 1.8 copy.37
  215.5 1.9 copy.38
  217.4 9.8 %fusion.36 = f32[2,128,16,128]{3,2,0,1:T(8,128)S(1)} fusion(f32[128,128,128]{1,0,2:T(8,128)} %copy.34, pred[128,128]{1,0:T(8,128)(4,1)S(1)} %get-tuple-element.29, pred[128,128]{1,0:T(8,128)(4,1)S(1)} %get-tuple-element.28, f32[2,128,16,128]{3,2,1,0:T(8,128)S(1)} %bitcast.152), kind=kOutput, calls=%fused_computation.59 | convolution fusion | flops 809500672 | bytes 12615680 | tf_op jit(solution)/shard_map/gts,bgct->bgcs/dot_general | solution.py:78
  227.2 0.0 copy-start.5
  227.2 0.0 copy-start.6
  227.2 0.2 copy.40
  227.4 1.8 copy.41
  229.2 0.0 copy-done.5
  229.2 0.0 copy-done.6
  229.2 5.4 %multiply_bitcast_fusion.1 = (f32[2,128,1,2048]{3,1,0,2:T(8,128)S(1)}, f32[2,128,1,2048]{3,1,0,2:T(8,128)S(1)}, f32[2,128,1,2048]{3,1,0,2:T(8,128)S(1)}) fusion(f32[2,128,3,2048]{3,1,2,0:T(8,128)} %copy-done.3, bf16[1,2,128,2048]{3,2,1,0:T(8,128)(2,1)S(1)} %copy-done.5, f32[2048]{0:T(1024)S(1)} %bitcast.157, f32[2,2048,128]{1,2,0:T(8,128)} %copy.41, ...), kind=kLoop, calls=%fused_computation.56 | loop fusion | flops 5242880 | bytes 17833984 | tf_op jit(solution)/shard_map/stack | solution.py:82
  234.6 0.8 pad_maximum_fusion
  235.4 6.4 %add_convert_fusion = bf16[2,128,3,2048]{3,1,0,2:T(8,128)(2,1)} fusion(f32[2,128,3,2048]{3,1,0,2:T(8,128)S(1)} %pad_maximum_fusion, f32[3,2048]{1,0:T(4,128)S(1)} %get-tuple-element.22, f32[3,2048]{1,0:T(4,128)S(1)} %get-tuple-element.23, f32[3,2048]{1,0:T(4,128)S(1)} %get-tuple-element.24, f32[3,2048]{1,0:T(4,128)S(1)} %get-tuple-element.25, ...), kind=kLoop, calls=%fused_computation.21 | loop fusion | flops 22020096 | bytes 9609216 | tf_op jit(solution)/shard_map/convert_element_type | solution.py:85
  241.8 7.0 %copy.42 = bf16[2,128,3,2048]{1,0,3,2:T(2,128)(2,1)S(1)} copy(bf16[2,128,3,2048]{3,1,0,2:T(8,128)(2,1)} %add_convert_fusion) | data formatting | bytes 6291456 | tf_op jit(solution)/shard_map/convert_element_type | solution.py:85
  248.8 0.0 copy-start.1
  248.8 23.1 %convolution_bitcast_fusion = f32[4096,256]{0,1:T(8,128)} fusion(bf16[4096,6144]{0,1:T(8,128)(2,1)} %bitcast.147, bf16[768,8,2,128]{3,2,1,0:T(2,128)(2,1)S(1)} %bitcast.149), kind=kOutput, calls=%fused_computation.30 | convolution fusion | flops 12884901888 | bytes 57671680 | tf_op jit(solution)/shard_map/dot_general | solution.py:89
  271.9 0.0 reduce-scatter.2.cloned.1.call-update
  271.9 56.5 %reduce-scatter.2.cloned.1.call-done = f32[2048,256]{0,1:T(8,128)} async-done(((f32[4096,256]{0,1:T(8,128)}), f32[2048,256]{0,1:T(8,128)}) %reduce-scatter.2.cloned.1.call-update) | async-done | bytes 2097168 | tf_op jit(solution)/shard_map/reduce_scatter | solution.py:88
  328.4 2.1 fusion.26
  330.5 0.7 collective-permute-start
  331.3 13.5 %collective-permute-done = bf16[1,2,128,2048]{3,2,1,0:T(8,128)(2,1)S(1)} collective-permute-done((bf16[1,2,128,2048]{3,2,1,0:T(8,128)(2,1)S(1)}, bf16[1,2,128,2048]{3,2,1,0:T(8,128)(2,1)S(1)}, u32[]{:S(2)}, u32[]{:S(2)}) %collective-permute-start) | collective-permute-done | bytes 1048608 | tf_op jit(solution)/shard_map/ppermute | solution.py:10
  344.8 1.0 copy.116
  345.8 0.0 copy-done.1
  (6 shorter events, 0.2 us)
Async XLA Ops:
  6.5 64.3 %copy-start = (f32[1,128,128]{2,1,0:T(8,128)S(1)}, f32[1,128,128]{2,1,0:T(8,128)}, u32[]{:S(2)}) copy-start(f32[1,128,128]{2,1,0:T(8,128)} %param.10) | copy-start | bytes 196612
  6.5 128.2 %all-gather.2.cloned.1.call-start = ((), (), s32[]{:S(2)}) async-start(), calls=%async_computation.1 | async-start | bytes 3145728 | tf_op jit(solution)/shard_map/all_gather | solution.py:61
  7.3 321.1 %reduce-scatter.2.cloned.1.call-start = ((), (), s32[]{:S(2)}) async-start(), calls=%async_computation.2 | async-start | bytes 6291456 | tf_op jit(solution)/shard_map/reduce_scatter | solution.py:88
  157.7 22.6 %copy-start.2 = (f32[2,128,3,2048]{3,1,2,0:T(8,128)S(1)}, f32[2,128,3,2048]{3,1,2,0:T(8,128)}, u32[]{:S(2)}) copy-start(f32[2,128,3,2048]{3,1,2,0:T(8,128)} %fusion) | copy-start | bytes 18874372
  180.3 13.5 %copy-start.4 = (bf16[1,2,128,2048]{3,2,1,0:T(8,128)(2,1)S(1)}, bf16[1,2,128,2048]{3,2,1,0:T(8,128)(2,1)}, u32[]{:S(2)}) copy-start(bf16[1,2,128,2048]{3,2,1,0:T(8,128)(2,1)} %param.7) | copy-start | bytes 3145732
  191.1 2.7 copy-start.3
  227.2 2.0 copy-start.5
  227.2 2.0 copy-start.6
  248.8 97.0 %copy-start.1 = (f32[1,128,128]{2,1,0:T(8,128)S(1)}, f32[1,128,128]{2,1,0:T(8,128)}, u32[]{:S(2)}) copy-start(f32[1,128,128]{2,1,0:T(8,128)} %param.10) | copy-start | bytes 196612
  330.5 14.3 %collective-permute-start = (bf16[1,2,128,2048]{3,2,1,0:T(8,128)(2,1)S(1)}, bf16[1,2,128,2048]{3,2,1,0:T(8,128)(2,1)S(1)}, u32[]{:S(2)}, u32[]{:S(2)}) collective-permute-start(bf16[1,2,128,2048]{3,2,1,0:T(8,128)(2,1)S(1)} %fusion.26), channel_id=1, source_target_pairs={{0,30},{2,0},{4,2},{6,4},{8,6},{10,8},{12,10},{14,12},{16,14},{18,... | collective-permute-start | bytes 3145736 | tf_op jit(solution)/shard_map/ppermute | solution.py:10
Sparse Core Ops, SparseCore 0:
  8.9 35.1 all-gather.1
  272.1 56.2 reduce-scatter.1
where the time goes:
time: 357 us; the launch traced here: 353 us
  local copies, waits for them, and re-layouts  168 us (47%)
  matrix products  71.5 us (20%)
  waiting for transfers between devices  70.8 us (20%)
  other arithmetic  27.7 us (8%)
  between operations  13.6 us (4%)
    unnamed x20, local copies, waits for them, and re-layouts  66.5 us
    gather x2, local copies, waits for them, and re-layouts, toeplitz_of(): looked = jnp.take(medium.T, lag_index, axis=1)  63.7 us
    reduce_scatter x1, waiting for transfers between devices, section_backward(): lax.psum_scatter(lax.dot_general(slab_rows, conv_flat, (((1,), (1,)), (()...  56.5 us
    slice x2, local copies, waits for them, and re-layouts, causal_taps(): result = result + taps[offset] * padded[:, first:first + length]  23.5 us
    dot_general x1, matrix products, section_backward(): lax.dot_general(slab_rows, conv_flat, (((1,), (1,)), ((), ())), preferred...  23.1 us
    dot_general x1, matrix products, section_backward(): jnp.dot(flattened, slab_rows, preferred_element_type=jnp.float32)  22.9 us
    dot_general x1, matrix products, section_backward(): jnp.einsum('gts,bgcs->bgct', toeplitz_mat, grouped, precision=lax.Precisi...  15.7 us
    ppermute x1, waiting for transfers between devices, shifted(): return lax.ppermute(value, axis, pairs)  13.5 us
  transfers between devices with their start and end apart: 3, of which 2 were waited for; matrix products, arithmetic and copies ran while one was open for 36% of the time, Pallas kernels for 0%

commit v1 on v0

v1 whole, which is shorter than its diff:
```python
import functools

import jax
import jax.numpy as jnp
from jax import lax
from jax.experimental import pallas as pl
from jax.experimental.pallas import tpu as pltpu
from jax.sharding import PartitionSpec as P

F32 = jnp.float32
BF16 = jnp.bfloat16
LANES = 128
VMEM_LIMIT = 56 * 1024 * 1024


def params(semantics):
    return pltpu.CompilerParams(
        dimension_semantics=semantics, vmem_limit_bytes=VMEM_LIMIT
    )


def cost(flops, moved):
    return pl.CostEstimate(flops=flops, bytes_accessed=moved, transcendentals=0)


def project_kernel(owner_ref, x_ref, w_ref, *rest):
    out_ref = rest[-1]
    total = jnp.dot(x_ref[...], w_ref[0], preferred_element_type=F32)
    if len(rest) > 1:
        total = total + rest[0][0]
    out_ref[0] = total


def project(x, weights, owner, so_far=None):
    rows, depth = x.shape
    channels = weights.shape[2]
    width = min(512, channels)
    block = pl.BlockSpec((1, rows, width), lambda i, j, o: (i, 0, j))
    in_specs = [
        pl.BlockSpec((rows, depth), lambda i, j, o: (0, 0)),
        pl.BlockSpec((1, depth, width), lambda i, j, o: (i, o[0], j)),
    ]
    operands = [x, weights]
    if so_far is not None:
        in_specs.append(block)
        operands.append(so_far)
    return pl.pallas_call(
        project_kernel,
        grid_spec=pltpu.PrefetchScalarGridSpec(
            num_scalar_prefetch=1,
            grid=(3, channels // width),
            in_specs=in_specs,
            out_specs=block,
        ),
        out_shape=jax.ShapeDtypeStruct((3, rows, channels), F32),
        compiler_params=params(("arbitrary", "arbitrary")),
        cost_estimate=cost(6 * rows * depth * channels, 6 * depth * channels + 12 * rows * channels),
        name="project",
    )(owner, *operands)


def toeplitz_kernel(taps_ref, turned_ref, first_ref, second_ref):
    length = first_ref.shape[0]
    count = taps_ref.shape[0]
    rows = lax.broadcasted_iota(jnp.int32, (length, length), 0)
    columns = lax.broadcasted_iota(jnp.int32, (length, length), 1)
    for g in range(count):
        place = slice(g * length, (g + 1) * length)
        base = jnp.broadcast_to(turned_ref[g : g + 1, :], (length, length))
        rolled = pltpu.roll(base, 0, 1, stride=1, stride_axis=0)
        first_ref[:, place] = jnp.where(columns <= rows, rolled, 0.0).astype(BF16)
        base = jnp.broadcast_to(taps_ref[g : g + 1, :], (length, length))
        rolled = pltpu.roll(base, 0, 1, stride=1, stride_axis=0)
        second_ref[:, place] = jnp.where(columns >= rows, rolled, 0.0).astype(BF16)


def toeplitz_pair(medium):
    reach, groups = medium.shape
    taps = medium.T
    turned = jnp.concatenate([taps[:, :1], taps[:, :0:-1]], axis=1)
    step = 8
    shape = jax.ShapeDtypeStruct((reach, groups * reach), BF16)
    row = pl.BlockSpec((step, reach), lambda g: (g, 0))
    block = pl.BlockSpec((reach, step * reach), lambda g: (0, g))
    return pl.pallas_call(
        toeplitz_kernel,
        grid=(groups // step,),
        in_specs=[row, row],
        out_specs=[block, block],
        out_shape=[shape, shape],
        compiler_params=params(("arbitrary",)),
        cost_estimate=cost(0, 4 * groups * reach * reach),
        name="toeplitz",
    )(taps, turned)


def down(series, steps):
    moved = pltpu.roll(series, steps, 0)
    row = lax.broadcasted_iota(jnp.int32, (8, series.shape[1]), 0)
    return jnp.concatenate([jnp.where(row >= steps, moved[:8], 0.0), moved[8:]], axis=0)


def up(series, steps):
    length = series.shape[0]
    moved = pltpu.roll(series, length - steps, 0)
    row = lax.broadcasted_iota(jnp.int32, (8, series.shape[1]), 0)
    last = jnp.where(row < 8 - steps, moved[length - 8 :], 0.0)
    return jnp.concatenate([moved[: length - 8], last], axis=0)


def short_filter(series, taps, move):
    shifted = [series] + [move(series, steps) for steps in range(1, 4)]
    near = taps[0] * series
    far = None
    for lag in range(1, len(taps)):
        term = taps[lag] * shifted[lag % 4]
        if lag < 4:
            near = near + term
        else:
            far = term if far is None else far + term
    if far is None:
        return near
    return near + move(far, 4)


def group_masks(members, width):
    group = lax.broadcasted_iota(jnp.int32, (1, width), 1) % LANES // members
    return [jnp.where(group == g, 1.0, 0.0).astype(BF16) for g in range(LANES // members)]


def medium_filter(toeplitz, series, masks):
    rounded = series.astype(BF16)
    stacked = jnp.concatenate([rounded * mask for mask in masks], axis=0)
    return jnp.dot(toeplitz, stacked, preferred_element_type=F32)


def mixer_kernel(
    owner_ref, x_ref, w_ref, so_far_ref, first_ref, second_ref, taps_ref, skip_ref, grad_ref,
    out_ref, *, micro, members
):
    rows, width = out_ref.shape[1:]
    length = rows // micro
    spread = LANES // members * length
    masks = group_masks(members, micro * LANES)
    x = x_ref[...]
    projected = [
        jnp.dot(x, w_ref[i], preferred_element_type=F32) + so_far_ref[i] for i in range(3)
    ]
    for tile in range(width // LANES):
        lanes = slice(tile * LANES, (tile + 1) * LANES)
        taps = [[taps_ref[j, i : i + 1, lanes] for j in range(taps_ref.shape[0])] for i in range(3)]
        skip = skip_ref[0:1, lanes]
        window = slice(tile * spread, (tile + 1) * spread)
        query, key, value, upstream = [], [], [], []
        for b in range(micro):
            span = slice(b * length, (b + 1) * length)
            series = [short_filter(projected[i][span, lanes], taps[i], down) for i in range(3)]
            query.append(series[0])
            key.append(series[1])
            value.append(series[2])
            upstream.append(grad_ref[span, lanes].astype(F32))
        product = [k * v for k, v in zip(key, value)]
        mixed = medium_filter(first_ref[:, window], jnp.concatenate(product, axis=1), masks)
        mixed_grad = [u * q for u, q in zip(upstream, query)]
        product_grad = medium_filter(
            second_ref[:, window], jnp.concatenate(mixed_grad, axis=1), masks
        )
        for b in range(micro):
            span = slice(b * length, (b + 1) * length)
            part = slice(b * LANES, (b + 1) * LANES)
            back = product_grad[:, part] + skip * mixed_grad[b]
            grads = [
                upstream[b] * (mixed[:, part] + skip * product[b]),
                back * value[b],
                back * key[b],
            ]
            for i in range(3):
                out_ref[i, span, lanes] = short_filter(grads[i], taps[i], up).astype(BF16)


def mixer(x, weights, owner, so_far, first, second, taps, skip, grad, micro):
    rows, depth = x.shape
    channels = weights.shape[2]
    length = rows // micro
    groups = first.shape[1] // length
    members = channels // groups
    width = min(256, channels)
    spread = width // members * length
    block = pl.BlockSpec((3, rows, width), lambda j, o: (0, 0, j))
    matrix = pl.BlockSpec((length, spread), lambda j, o: (0, j))
    return pl.pallas_call(
        functools.partial(mixer_kernel, micro=micro, members=members),
        grid_spec=pltpu.PrefetchScalarGridSpec(
            num_scalar_prefetch=1,
            grid=(channels // width,),
            in_specs=[
                pl.BlockSpec((rows, depth), lambda j, o: (0, 0)),
                pl.BlockSpec((3, depth, width), lambda j, o: (0, o[0], j)),
                block,
                matrix,
                matrix,
                pl.BlockSpec((taps.shape[0], 3, width), lambda j, o: (0, 0, j)),
                pl.BlockSpec((1, width), lambda j, o: (0, j)),
                pl.BlockSpec((rows, width), lambda j, o: (0, j)),
            ],
            out_specs=block,
        ),
        out_shape=jax.ShapeDtypeStruct((3, rows, channels), BF16),
        compiler_params=params(("arbitrary",)),
        cost_estimate=cost(6 * rows * depth * channels, 6 * depth * channels + 18 * rows * channels),
        name="mixer",
    )(owner, x, weights, so_far, first, second, taps, skip, grad)


def input_grad_kernel(member_ref, conv_ref, w_ref, *rest):
    out_ref = rest[-1]
    total = rest[0][...].astype(F32) if len(rest) > 1 else None
    for i in range(3):
        term = lax.dot_general(
            conv_ref[i], w_ref[i], (((1,), (1,)), ((), ())), preferred_element_type=F32
        )
        total = term if total is None else total + term
    out_ref[...] = total.astype(BF16)


def input_grad(conv, weights, member, part, parts, depth, grad=None):
    rows, channels = conv.shape[1:]
    extent = depth // parts
    width = min(256, extent)
    steps = extent // width
    in_specs = [
        pl.BlockSpec((3, rows, channels), lambda j, m: (0, 0, 0)),
        pl.BlockSpec((3, width, channels), lambda j, m: (0, (m[0] * parts + part) * steps + j, 0)),
    ]
    operands = [conv, weights]
    if grad is not None:
        in_specs.append(pl.BlockSpec((rows, width), lambda j, m: (0, part * steps + j)))
        operands.append(grad)
    return pl.pallas_call(
        input_grad_kernel,
        grid_spec=pltpu.PrefetchScalarGridSpec(
            num_scalar_prefetch=1,
            grid=(steps,),
            in_specs=in_specs,
            out_specs=pl.BlockSpec((rows, width), lambda j, m: (0, j)),
        ),
        out_shape=jax.ShapeDtypeStruct((rows, extent), BF16),
        compiler_params=params(("arbitrary",)),
        cost_estimate=cost(6 * rows * extent * channels, 6 * extent * channels + 8 * rows * channels),
        name="input_grad",
    )(member, *operands)


def join(pieces):
    rows, extent = pieces[0][0].shape
    flat = [piece for part in pieces for piece in part]
    sources = len(pieces[0])

    def kernel(*refs):
        out_ref = refs[-1]
        for p in range(len(pieces)):
            total = refs[p * sources][...].astype(F32)
            for s in range(1, sources):
                total = total + refs[p * sources + s][...].astype(F32)
            out_ref[:, p * extent : (p + 1) * extent] = total.astype(BF16)

    return pl.pallas_call(
        kernel,
        out_shape=jax.ShapeDtypeStruct((rows, extent * len(pieces)), BF16),
        compiler_params=pltpu.CompilerParams(vmem_limit_bytes=VMEM_LIMIT),
        cost_estimate=cost(0, 2 * rows * extent * (len(flat) + len(pieces))),
        name="join",
    )(*flat)


PARTS = 2


def local(block_input, incoming, in_weight, short_taps, medium_taps, skip_weight):
    micro, length, depth = block_input.shape[1:]
    rows = micro * length
    members = lax.axis_size("tp")
    sections = lax.axis_size("section")
    me = lax.axis_index("tp")
    weights = jnp.transpose(in_weight[0], (1, 0, 2))
    x = block_input.reshape(rows, depth)
    grad = incoming.reshape(rows, depth)

    def owner(step):
        return jnp.full((1,), lax.rem(me + step, members), jnp.int32)

    from_member = [x]
    for k in range(1, members):
        pairs = [((m + k) % members, m) for m in range(members)]
        from_member.append(lax.ppermute(x, "tp", pairs))
    so_far = None
    for k in range(members - 1):
        so_far = project(from_member[k], weights, owner(k), so_far)
    first, second = toeplitz_pair(medium_taps[0])
    conv = mixer(
        from_member[-1], weights, owner(members - 1), so_far, first, second,
        short_taps[0], skip_weight, grad, micro,
    )
    pieces = [[None] * members for _ in range(PARTS)]
    for k in list(range(1, members)) + [0]:
        pairs = [
            (s * members + m, (s - 1) % sections * members + (m + k) % members)
            for s in range(sections)
            for m in range(members)
        ]
        for part in range(PARTS):
            share = input_grad(
                conv, weights, owner(k), part, PARTS, depth, grad if k == 0 else None
            )
            pieces[part][k] = lax.ppermute(share, ("section", "tp"), pairs)
    return join(pieces).reshape(block_input.shape)


def solution(mesh):
    in_specs = (
        P("section", None, None, "tp"),
        P("section", None, None, "tp"),
        P("section", None, None, "tp"),
        P("section", None, None, "tp"),
        P("section", None, "tp"),
        P("section", "tp"),
    )
    out_specs = P("section", None, None, "tp")
    return jax.shard_map(local, mesh=mesh, in_specs=in_specs, out_specs=out_specs, check_vma=False)
```

time: 357 us -> 132 us (0.37)
  the two profiles are of different devices: /device:TPU:1 before, /device:TPU:0 now
where the time goes in v1:
time: 132 us; the launch traced here: 131 us
  Pallas kernels  92.7 us (70%)
  waiting for transfers between devices  23.8 us (18%)
  starting transfers between devices  9.29 us (7%)
  local copies, waits for them, and re-layouts  4.7 us (4%)
    pallas_call x4, Pallas kernels, input_grad(): pl.pallas_call(input_grad_kernel, grid_spec=pltpu.PrefetchScalarGridSpec(...  35.3 us
    pallas_call x1, Pallas kernels, mixer(): pl.pallas_call(functools.partial(mixer_kernel, micro=micro, members=membe...  26.5 us
    ppermute x4, waiting for transfers between devices, local(): pieces[part][k] = lax.ppermute(share, ('section', 'tp'), pairs)  23.8 us
    pallas_call x1, Pallas kernels, project(): pl.pallas_call(project_kernel, grid_spec=pltpu.PrefetchScalarGridSpec(num...  17.7 us
    pallas_call x1, Pallas kernels, toeplitz_pair(): pl.pallas_call(toeplitz_kernel, grid=(groups // step,), in_specs=[row, ro...  10.5 us
    ppermute x4, starting transfers between devices, local(): pieces[part][k] = lax.ppermute(share, ('section', 'tp'), pairs)  6.36 us
    unnamed x20, local copies, waits for them, and re-layouts  3.72 us
    ppermute x1, starting transfers between devices, local(): from_member.append(lax.ppermute(x, 'tp', pairs))  2.94 us
  transfers between devices with their start and end apart: 5, of which 4 were waited for; matrix products, arithmetic and copies ran while one was open for 3% of the time, Pallas kernels for 21%

profile of v1, /device:TPU:0, one launch (start us, length us, event | category | flops | bytes accessed | tf_op | source)
XLA Modules:
  0.0 131.2 jit_solution(6438454188445231886)
XLA Ops:
  0.0 2.9 %collective-permute-start = (bf16[256,2048]{1,0:T(8,128)(2,1)}, bf16[256,2048]{1,0:T(8,128)(2,1)S(1)}, u32[]{:S(2)}, u32[]{:S(2)}) collective-permute-start(bf16[256,2048]{1,0:T(8,128)(2,1)} %bitcast.24), channel_id=1, source_target_pairs={{1,0},{0,1},{3,2},{2,3},{5,4},{4,5},{7,6},{6,7},{9,8},{8,9},{11,10... | collective-permute-start | bytes 3145736 | tf_op jit(solution)/shard_map/ppermute | solution.py:295
  2.9 0.9 copy.8
  3.9 0.0 copy-start.1
  3.9 0.1 slice.9
  4.0 0.1 rev.3
  4.0 1.0 copy.12
  5.0 0.8 copy.10.taps_ref
  5.9 0.7 pad_maximum_fusion.turned_ref
  6.6 0.0 copy-done.1
  6.6 10.5 %toeplitz.1 = (bf16[128,16384]{1,0:T(8,128)(2,1)}, bf16[128,16384]{1,0:T(8,128)(2,1)}) custom-call(f32[128,128]{1,0:T(8,128)} %bitcast.28, f32[128,128]{1,0:T(8,128)} %pad_maximum_fusion.turned_ref), custom_call_target="tpu_custom_call" | custom-call | bytes 8388608 | tf_op jit(solution)/shard_map/toeplitz/pallas_call | solution.py:85
  17.1 17.7 %project.1.so_far_ref = f32[3,256,2048]{2,1,0:T(8,128)} custom-call(s32[1]{0:T(128)} %bitcast.owner_ref.member_ref, bf16[256,2048]{1,0:T(8,128)(2,1)} %bitcast.25, bf16[3,4096,2048]{2,1,0:T(8,128)(2,1)} %bitcast.15), custom_call_target="tpu_custom_call" | custom-call | flops 6442450944 | bytes 31457280 | tf_op jit(solution)/shard_map/project/pallas_call | solution.py:47
  34.7 0.0 collective-permute-done.x_ref
  34.7 0.0 copy-start
  34.7 1.0 copy-done
  35.7 26.5 %mixer.1.conv_ref = bf16[3,256,2048]{2,1,0:T(8,128)(2,1)} custom-call(s32[1]{0:T(128)} %bitcast.1.owner_ref.member_ref, bf16[256,2048]{1,0:T(8,128)(2,1)} %copy-done, bf16[3,4096,2048]{2,1,0:T(8,128)(2,1)} %bitcast.16, f32[3,256,2048]{2,1,0:T(8,128)} %project.1.so_far_ref, bf16[128,16384]{1,0:T(8,128)(2,1)} %get-tuple-element.7.first_ref, ...), custom_call_target="tpu_custom_call" | custom-call | flops 6442450944 | bytes 34603008 | tf_op jit(solution)/shard_map/mixer/pallas_call | solution.py:191
  62.2 8.8 %input_grad.7 = bf16[256,1024]{1,0:T(8,128)(2,1)} custom-call(s32[1]{0:T(128)} %bitcast.1.owner_ref.member_ref, bf16[3,256,2048]{2,1,0:T(8,128)(2,1)} %mixer.1.conv_ref, bf16[3,4096,2048]{2,1,0:T(8,128)(2,1)} %bitcast.17), custom_call_target="tpu_custom_call" | custom-call | flops 3221225472 | bytes 16777216 | tf_op jit(solution)/shard_map/input_grad/pallas_call | solution.py:239
  71.0 8.8 %input_grad.5 = bf16[256,1024]{1,0:T(8,128)(2,1)} custom-call(s32[1]{0:T(128)} %bitcast.1.owner_ref.member_ref, bf16[3,256,2048]{2,1,0:T(8,128)(2,1)} %mixer.1.conv_ref, bf16[3,4096,2048]{2,1,0:T(8,128)(2,1)} %bitcast.18), custom_call_target="tpu_custom_call" | custom-call | flops 3221225472 | bytes 16777216 | tf_op jit(solution)/shard_map/input_grad/pallas_call | solution.py:239
  79.8 8.8 %input_grad.6 = bf16[256,1024]{1,0:T(8,128)(2,1)} custom-call(s32[1]{0:T(128)} %bitcast.owner_ref.member_ref, bf16[3,256,2048]{2,1,0:T(8,128)(2,1)} %mixer.1.conv_ref, bf16[3,4096,2048]{2,1,0:T(8,128)(2,1)} %bitcast.19, bf16[256,2048]{1,0:T(8,128)(2,1)} %bitcast.22), custom_call_target="tpu_custom_call" | custom-call | flops 3221225472 | bytes 16777216 | tf_op jit(solution)/shard_map/input_grad/pallas_call | solution.py:239
  88.6 0.0 copy-start.4
  88.6 0.0 copy-start.3
  88.6 0.0 copy-start.2
  88.6 8.9 %input_grad.4 = bf16[256,1024]{1,0:T(8,128)(2,1)} custom-call(s32[1]{0:T(128)} %bitcast.owner_ref.member_ref, bf16[3,256,2048]{2,1,0:T(8,128)(2,1)} %mixer.1.conv_ref, bf16[3,4096,2048]{2,1,0:T(8,128)(2,1)} %bitcast.20, bf16[256,2048]{1,0:T(8,128)(2,1)} %bitcast.23), custom_call_target="tpu_custom_call" | custom-call | flops 3221225472 | bytes 16777216 | tf_op jit(solution)/shard_map/input_grad/pallas_call | solution.py:239
  97.5 3.7 %collective-permute-start.1 = (bf16[256,1024]{1,0:T(8,128)(2,1)}, bf16[256,1024]{1,0:T(8,128)(2,1)S(1)}, u32[]{:S(2)}, u32[]{:S(2)}) collective-permute-start(bf16[256,1024]{1,0:T(8,128)(2,1)} %input_grad.4), channel_id=1, source_target_pairs={{0,30},{1,31},{2,0},{3,1},{4,2},{5,3},{6,4},{7,5},{8,6},{9,7},{10,... | collective-permute-start | bytes 1572872 | tf_op jit(solution)/shard_map/ppermute | solution.py:315
  101.2 0.0 copy-done.4
  101.3 1.0 collective-permute-start.3
  102.2 0.0 copy-done.3
  102.2 0.0 collective-permute-start.2
  102.2 0.0 copy-done.2
  102.2 1.7 %collective-permute-start.4 = (bf16[256,1024]{1,0:T(8,128)(2,1)S(1)}, bf16[256,1024]{1,0:T(8,128)(2,1)S(1)}, u32[]{:S(2)}, u32[]{:S(2)}) collective-permute-start(bf16[256,1024]{1,0:T(8,128)(2,1)S(1)} %copy-done.2), channel_id=1, source_target_pairs={{0,31},{1,30},{2,1},{3,0},{4,3},{5,2},{6,5},{7,4},{8,7},{9,6},{10,... | collective-permute-start | bytes 1572872 | tf_op jit(solution)/shard_map/ppermute | solution.py:315
  103.9 4.4 %collective-permute-done.1.refs_0_ = bf16[256,1024]{1,0:T(8,128)(2,1)S(1)} collective-permute-done((bf16[256,1024]{1,0:T(8,128)(2,1)}, bf16[256,1024]{1,0:T(8,128)(2,1)S(1)}, u32[]{:S(2)}, u32[]{:S(2)}) %collective-permute-start.1) | collective-permute-done | bytes 524320 | tf_op jit(solution)/shard_map/ppermute | solution.py:315
  108.3 0.0 copy-start.5
  108.3 5.5 %collective-permute-done.3.refs_2_ = bf16[256,1024]{1,0:T(8,128)(2,1)S(1)} collective-permute-done((bf16[256,1024]{1,0:T(8,128)(2,1)S(1)}, bf16[256,1024]{1,0:T(8,128)(2,1)S(1)}, u32[]{:S(2)}, u32[]{:S(2)}) %collective-permute-start.3) | collective-permute-done | bytes 524320 | tf_op jit(solution)/shard_map/ppermute | solution.py:315
  113.8 0.0 copy-start.6
  113.8 5.6 %collective-permute-done.2.refs_1_ = bf16[256,1024]{1,0:T(8,128)(2,1)S(1)} collective-permute-done((bf16[256,1024]{1,0:T(8,128)(2,1)S(1)}, bf16[256,1024]{1,0:T(8,128)(2,1)S(1)}, u32[]{:S(2)}, u32[]{:S(2)}) %collective-permute-start.2) | collective-permute-done | bytes 524320 | tf_op jit(solution)/shard_map/ppermute | solution.py:315
  119.4 0.0 copy-start.7
  119.4 8.3 %collective-permute-done.4.refs_3_ = bf16[256,1024]{1,0:T(8,128)(2,1)S(1)} collective-permute-done((bf16[256,1024]{1,0:T(8,128)(2,1)S(1)}, bf16[256,1024]{1,0:T(8,128)(2,1)S(1)}, u32[]{:S(2)}, u32[]{:S(2)}) %collective-permute-start.4) | collective-permute-done | bytes 524320 | tf_op jit(solution)/shard_map/ppermute | solution.py:315
  127.7 0.0 copy-done.5
  127.7 0.0 copy-done.6
  127.7 0.0 copy-done.7
  127.7 0.0 copy-start.8
  127.7 0.8 copy-done.8
  128.5 2.7 %join.1 = bf16[256,2048]{1,0:T(8,128)(2,1)} custom-call(bf16[256,1024]{1,0:T(8,128)(2,1)} %copy-done.5, bf16[256,1024]{1,0:T(8,128)(2,1)} %copy-done.7, bf16[256,1024]{1,0:T(8,128)(2,1)} %copy-done.6, bf16[256,1024]{1,0:T(8,128)(2,1)} %copy-done.8), custom_call_target="tpu_custom_call" | custom-call | bytes 3145728 | tf_op jit(solution)/shard_map/join/pallas_call | solution.py:267
Async XLA Ops:
  0.0 34.7 %collective-permute-start = (bf16[256,2048]{1,0:T(8,128)(2,1)}, bf16[256,2048]{1,0:T(8,128)(2,1)S(1)}, u32[]{:S(2)}, u32[]{:S(2)}) collective-permute-start(bf16[256,2048]{1,0:T(8,128)(2,1)} %bitcast.24), channel_id=1, source_target_pairs={{1,0},{0,1},{3,2},{2,3},{5,4},{4,5},{7,6},{6,7},{9,8},{8,9},{11,10... | collective-permute-start | bytes 3145736 | tf_op jit(solution)/shard_map/ppermute | solution.py:295
  3.9 2.7 %copy-start.1 = (f32[1,128,128]{1,2,0:T(8,128)}, f32[1,128,128]{1,2,0:T(8,128)S(1)}, u32[]{:S(2)}) copy-start(f32[1,128,128]{1,2,0:T(8,128)S(1)} %copy.8) | copy-start | bytes 196612
  34.7 1.0 copy-start
  88.6 12.7 %copy-start.4 = (bf16[256,1024]{1,0:T(8,128)(2,1)S(1)}, bf16[256,1024]{1,0:T(8,128)(2,1)}, u32[]{:S(2)}) copy-start(bf16[256,1024]{1,0:T(8,128)(2,1)} %input_grad.6) | copy-start | bytes 1572868
  88.6 13.6 %copy-start.3 = (bf16[256,1024]{1,0:T(8,128)(2,1)S(1)}, bf16[256,1024]{1,0:T(8,128)(2,1)}, u32[]{:S(2)}) copy-start(bf16[256,1024]{1,0:T(8,128)(2,1)} %input_grad.5) | copy-start | bytes 1572868
  88.6 13.7 %copy-start.2 = (bf16[256,1024]{1,0:T(8,128)(2,1)S(1)}, bf16[256,1024]{1,0:T(8,128)(2,1)}, u32[]{:S(2)}) copy-start(bf16[256,1024]{1,0:T(8,128)(2,1)} %input_grad.7) | copy-start | bytes 1572868
  97.5 10.7 %collective-permute-start.1 = (bf16[256,1024]{1,0:T(8,128)(2,1)}, bf16[256,1024]{1,0:T(8,128)(2,1)S(1)}, u32[]{:S(2)}, u32[]{:S(2)}) collective-permute-start(bf16[256,1024]{1,0:T(8,128)(2,1)} %input_grad.4), channel_id=1, source_target_pairs={{0,30},{1,31},{2,0},{3,1},{4,2},{5,3},{6,4},{7,5},{8,6},{9,7},{10,... | collective-permute-start | bytes 1572872 | tf_op jit(solution)/shard_map/ppermute | solution.py:315
  101.3 12.5 %collective-permute-start.3 = (bf16[256,1024]{1,0:T(8,128)(2,1)S(1)}, bf16[256,1024]{1,0:T(8,128)(2,1)S(1)}, u32[]{:S(2)}, u32[]{:S(2)}) collective-permute-start(bf16[256,1024]{1,0:T(8,128)(2,1)S(1)} %copy-done.4), channel_id=1, source_target_pairs={{0,30},{1,31},{2,0},{3,1},{4,2},{5,3},{6,4},{7,5},{8,6},{9,7},{10,... | collective-permute-start | bytes 1572872 | tf_op jit(solution)/shard_map/ppermute | solution.py:315
  102.2 17.2 %collective-permute-start.2 = (bf16[256,1024]{1,0:T(8,128)(2,1)S(1)}, bf16[256,1024]{1,0:T(8,128)(2,1)S(1)}, u32[]{:S(2)}, u32[]{:S(2)}) collective-permute-start(bf16[256,1024]{1,0:T(8,128)(2,1)S(1)} %copy-done.3), channel_id=1, source_target_pairs={{0,31},{1,30},{2,1},{3,0},{4,3},{5,2},{6,5},{7,4},{8,7},{9,6},{10,... | collective-permute-start | bytes 1572872 | tf_op jit(solution)/shard_map/ppermute | solution.py:315
  102.2 25.4 %collective-permute-start.4 = (bf16[256,1024]{1,0:T(8,128)(2,1)S(1)}, bf16[256,1024]{1,0:T(8,128)(2,1)S(1)}, u32[]{:S(2)}, u32[]{:S(2)}) collective-permute-start(bf16[256,1024]{1,0:T(8,128)(2,1)S(1)} %copy-done.2), channel_id=1, source_target_pairs={{0,31},{1,30},{2,1},{3,0},{4,3},{5,2},{6,5},{7,4},{8,7},{9,6},{10,... | collective-permute-start | bytes 1572872 | tf_op jit(solution)/shard_map/ppermute | solution.py:315
  108.3 19.4 %copy-start.5 = (bf16[256,1024]{1,0:T(8,128)(2,1)}, bf16[256,1024]{1,0:T(8,128)(2,1)S(1)}, u32[]{:S(2)}) copy-start(bf16[256,1024]{1,0:T(8,128)(2,1)S(1)} %collective-permute-done.1.refs_0_) | copy-start | bytes 1572868
  113.8 13.9 %copy-start.6 = (bf16[256,1024]{1,0:T(8,128)(2,1)}, bf16[256,1024]{1,0:T(8,128)(2,1)S(1)}, u32[]{:S(2)}) copy-start(bf16[256,1024]{1,0:T(8,128)(2,1)S(1)} %collective-permute-done.3.refs_2_) | copy-start | bytes 1572868
  119.4 8.3 %copy-start.7 = (bf16[256,1024]{1,0:T(8,128)(2,1)}, bf16[256,1024]{1,0:T(8,128)(2,1)S(1)}, u32[]{:S(2)}) copy-start(bf16[256,1024]{1,0:T(8,128)(2,1)S(1)} %collective-permute-done.2.refs_1_) | copy-start | bytes 1572868
  127.7 0.8 copy-start.8

commit v2 on v1

--- a/solution.py
+++ b/solution.py
@@ -23,11 +23,15 @@
     return pl.CostEstimate(flops=flops, bytes_accessed=moved, transcendentals=0)
 
 
-def project_kernel(owner_ref, x_ref, w_ref, *rest):
+def project_kernel(owner_ref, x_ref, *rest, spans):
     out_ref = rest[-1]
-    total = jnp.dot(x_ref[...], w_ref[0], preferred_element_type=F32)
-    if len(rest) > 1:
-        total = total + rest[0][0]
+    depth = x_ref.shape[1] // spans
+    total = rest[spans][0] if len(rest) > spans + 1 else None
+    for k in range(spans):
+        term = jnp.dot(
+            x_ref[:, k * depth : (k + 1) * depth], rest[k][0], preferred_element_type=F32
+        )
+        total = term if total is None else total + term
     out_ref[0] = total
 
 
@@ -35,17 +39,22 @@
     rows, depth = x.shape
     channels = weights.shape[2]
     width = min(512, channels)
+    spans = 4 if depth >= 1024 else 1
     block = pl.BlockSpec((1, rows, width), lambda i, j, o: (i, 0, j))
-    in_specs = [
-        pl.BlockSpec((rows, depth), lambda i, j, o: (0, 0)),
-        pl.BlockSpec((1, depth, width), lambda i, j, o: (i, o[0], j)),
-    ]
-    operands = [x, weights]
+    in_specs = [pl.BlockSpec((rows, depth), lambda i, j, o: (0, 0))]
+    for k in range(spans):
+        in_specs.append(
+            pl.BlockSpec(
+                (1, depth // spans, width),
+                lambda i, j, o, k=k: (i, o[0] * spans + k, j),
+            )
+        )
+    operands = [x] + [weights] * spans
     if so_far is not None:
         in_specs.append(block)
         operands.append(so_far)
     return pl.pallas_call(
-        project_kernel,
+        functools.partial(project_kernel, spans=spans),
         grid_spec=pltpu.PrefetchScalarGridSpec(
             num_scalar_prefetch=1,
             grid=(3, channels // width),
@@ -135,8 +144,8 @@
 
 
 def mixer_kernel(
-    owner_ref, x_ref, w_ref, so_far_ref, first_ref, second_ref, taps_ref, skip_ref, grad_ref,
-    out_ref, *, micro, members
+    owner_ref, x_ref, w0_ref, w1_ref, w2_ref, so_far_ref, first_ref, second_ref, taps_ref,
+    skip_ref, grad_ref, out_ref, *, micro, members
 ):
     rows, width = out_ref.shape[1:]
     length = rows // micro
@@ -144,7 +153,8 @@
     masks = group_masks(members, micro * LANES)
     x = x_ref[...]
     projected = [
-        jnp.dot(x, w_ref[i], preferred_element_type=F32) + so_far_ref[i] for i in range(3)
+        jnp.dot(x, w_ref[0], preferred_element_type=F32) + so_far_ref[i]
+        for i, w_ref in enumerate((w0_ref, w1_ref, w2_ref))
     ]
     for tile in range(width // LANES):
         lanes = slice(tile * LANES, (tile + 1) * LANES)
@@ -195,7 +205,10 @@
             grid=(channels // width,),
             in_specs=[
                 pl.BlockSpec((rows, depth), lambda j, o: (0, 0)),
-                pl.BlockSpec((3, depth, width), lambda j, o: (0, o[0], j)),
+                *[
+                    pl.BlockSpec((1, depth, width), lambda j, o, i=i: (i, o[0], j))
+                    for i in range(3)
+                ],
                 block,
                 matrix,
                 matrix,
@@ -209,32 +222,39 @@
         compiler_params=params(("arbitrary",)),
         cost_estimate=cost(6 * rows * depth * channels, 6 * depth * channels + 18 * rows * channels),
         name="mixer",
-    )(owner, x, weights, so_far, first, second, taps, skip, grad)
-
-
-def input_grad_kernel(member_ref, conv_ref, w_ref, *rest):
+    )(owner, x, weights, weights, weights, so_far, first, second, taps, skip, grad)
+
+
+def input_grad_kernel(member_ref, conv_ref, w0_ref, w1_ref, w2_ref, *rest):
     out_ref = rest[-1]
-    total = rest[0][...].astype(F32) if len(rest) > 1 else None
+    total = None
+    for i, w_ref in enumerate((w0_ref, w1_ref, w2_ref)):
+        term = lax.dot_general(
+            w_ref[0], conv_ref[i], (((1,), (1,)), ((), ())), preferred_element_type=F32
+        )
+        total = term if total is None else total + term
+    total = total.T
+    if len(rest) > 1:
+        total = total + rest[0][...].astype(F32)
+    out_ref[...] = total.astype(BF16)
+
+
+def input_grad(conv, weights, member, first, extent, depth, grad=None):
+    rows, channels = conv.shape[1:]
+    width = SPAN
+    steps = extent // width
+    start = first // width
+    whole = depth // width
+    in_specs = [pl.BlockSpec((3, rows, channels), lambda j, m: (0, 0, 0))]
     for i in range(3):
-        term = lax.dot_general(
-            conv_ref[i], w_ref[i], (((1,), (1,)), ((), ())), preferred_element_type=F32
-        )
-        total = term if total is None else total + term
-    out_ref[...] = total.astype(BF16)
-
-
-def input_grad(conv, weights, member, part, parts, depth, grad=None):
-    rows, channels = conv.shape[1:]
-    extent = depth // parts
-    width = min(256, extent)
-    steps = extent // width
-    in_specs = [
-        pl.BlockSpec((3, rows, channels), lambda j, m: (0, 0, 0)),
-        pl.BlockSpec((3, width, channels), lambda j, m: (0, (m[0] * parts + part) * steps + j, 0)),
-    ]
-    operands = [conv, weights]
+        in_specs.append(
+            pl.BlockSpec(
+                (1, width, channels), lambda j, m, i=i: (i, m[0] * whole + start + j, 0)
+            )
+        )
+    operands = [conv, weights, weights, weights]
     if grad is not None:
-        in_specs.append(pl.BlockSpec((rows, width), lambda j, m: (0, part * steps + j)))
+        in_specs.append(pl.BlockSpec((rows, width), lambda j, m: (0, start + j)))
         operands.append(grad)
     return pl.pallas_call(
         input_grad_kernel,
@@ -246,34 +266,47 @@
         ),
         out_shape=jax.ShapeDtypeStruct((rows, extent), BF16),
         compiler_params=params(("arbitrary",)),
-        cost_estimate=cost(6 * rows * extent * channels, 6 * extent * channels + 8 * rows * channels),
+        cost_estimate=cost(1, 1),
         name="input_grad",
     )(member, *operands)
 
 
-def join(pieces):
-    rows, extent = pieces[0][0].shape
-    flat = [piece for part in pieces for piece in part]
-    sources = len(pieces[0])
+def join(pieces, depth):
+    rows = pieces[0][1].shape[0]
 
     def kernel(*refs):
         out_ref = refs[-1]
-        for p in range(len(pieces)):
-            total = refs[p * sources][...].astype(F32)
-            for s in range(1, sources):
-                total = total + refs[p * sources + s][...].astype(F32)
-            out_ref[:, p * extent : (p + 1) * extent] = total.astype(BF16)
+        for start in range(0, depth, SPAN):
+            total = None
+            for (first, piece), ref in zip(pieces, refs):
+                if first <= start < first + piece.shape[1]:
+                    term = ref[:, start - first : start - first + SPAN].astype(F32)
+                    total = term if total is None else total + term
+            out_ref[:, start : start + SPAN] = total.astype(BF16)
 
     return pl.pallas_call(
         kernel,
-        out_shape=jax.ShapeDtypeStruct((rows, extent * len(pieces)), BF16),
+        out_shape=jax.ShapeDtypeStruct((rows, depth), BF16),
         compiler_params=pltpu.CompilerParams(vmem_limit_bytes=VMEM_LIMIT),
-        cost_estimate=cost(0, 2 * rows * extent * (len(flat) + len(pieces))),
+        cost_estimate=cost(0, 6 * rows * depth),
         name="join",
-    )(*flat)
-
-
-PARTS = 2
+    )(*[piece for _, piece in pieces])
+
+
+SPAN = 256
+AWAY_CUTS = (8,)
+OWN_CUTS = (4, 4)
+
+
+def cuts_of(eighths, depth):
+    step = depth // 8
+    if step % SPAN:
+        return [(0, depth)]
+    first, spans = 0, []
+    for count in eighths:
+        spans.append((first, count * step))
+        first += count * step
+    return spans
 
 
 def local(block_input, incoming, in_weight, short_taps, medium_taps, skip_weight):
@@ -301,19 +334,19 @@
         from_member[-1], weights, owner(members - 1), so_far, first, second,
         short_taps[0], skip_weight, grad, micro,
     )
-    pieces = [[None] * members for _ in range(PARTS)]
+    pieces = []
     for k in list(range(1, members)) + [0]:
         pairs = [
             (s * members + m, (s - 1) % sections * members + (m + k) % members)
             for s in range(sections)
             for m in range(members)
         ]
-        for part in range(PARTS):
+        for first_column, extent in cuts_of(AWAY_CUTS if k else OWN_CUTS, depth):
             share = input_grad(
-                conv, weights, owner(k), part, PARTS, depth, grad if k == 0 else None
+                conv, weights, owner(k), first_column, extent, depth, None if k else grad
             )
-            pieces[part][k] = lax.ppermute(share, ("section", "tp"), pairs)
-    return join(pieces).reshape(block_input.shape)
+            pieces.append((first_column, lax.ppermute(share, ("section", "tp"), pairs)))
+    return join(pieces, depth).reshape(block_input.shape)
 
 
 def solution(mesh):

time: 132 us -> 115 us (0.87)
  the two profiles are of different devices: /device:TPU:0 before, /device:TPU:1 now
where the time goes in v2:
time: 115 us; the launch traced here: 114 us
  Pallas kernels  92.2 us (80%)
  starting transfers between devices  7.81 us (7%)
  waiting for transfers between devices  7.69 us (7%)
  local copies, waits for them, and re-layouts  5.61 us (5%)
    pallas_call x3, Pallas kernels, input_grad(): pl.pallas_call(input_grad_kernel, grid_spec=pltpu.PrefetchScalarGridSpec(...  34.1 us
    pallas_call x1, Pallas kernels, mixer(): pl.pallas_call(functools.partial(mixer_kernel, micro=micro, members=membe...  27.4 us
    pallas_call x1, Pallas kernels, project(): pl.pallas_call(functools.partial(project_kernel, spans=spans), grid_spec=...  17.4 us
    pallas_call x1, Pallas kernels, toeplitz_pair(): pl.pallas_call(toeplitz_kernel, grid=(groups // step,), in_specs=[row, ro...  10.5 us
    ppermute x3, waiting for transfers between devices, local(): pieces.append((first_column, lax.ppermute(share, ('section', 'tp'), pairs)))  7.69 us
    ppermute x3, starting transfers between devices, local(): pieces.append((first_column, lax.ppermute(share, ('section', 'tp'), pairs)))  5.77 us
    unnamed x12, local copies, waits for them, and re-layouts  4.64 us
    pallas_call x1, Pallas kernels, join(): pl.pallas_call(kernel, out_shape=jax.ShapeDtypeStruct((rows, depth), BF16...  2.75 us
  transfers between devices with their start and end apart: 4, of which 2 were waited for; matrix products, arithmetic and copies ran while one was open for 3% of the time, Pallas kernels for 41%

profile of v2, /device:TPU:1, one launch (start us, length us, event | category | flops | bytes accessed | tf_op | source)
XLA Modules:
  0.0 114.1 jit_solution(10063362134196446503)
XLA Ops:
  0.0 2.0 %collective-permute-start = (bf16[256,2048]{1,0:T(8,128)(2,1)}, bf16[256,2048]{1,0:T(8,128)(2,1)S(1)}, u32[]{:S(2)}, u32[]{:S(2)}) collective-permute-start(bf16[256,2048]{1,0:T(8,128)(2,1)} %bitcast.34), channel_id=1, source_target_pairs={{1,0},{0,1},{3,2},{2,3},{5,4},{4,5},{7,6},{6,7},{9,8},{8,9},{11,10... | collective-permute-start | bytes 3145736 | tf_op jit(solution)/shard_map/ppermute | solution.py:328
  2.0 0.9 copy.8
  3.0 0.0 copy-start.2
  3.0 0.1 slice.9
  3.1 0.1 rev.3
  3.1 1.0 copy.12
  4.1 0.8 copy.10.taps_ref
  5.0 0.7 pad_maximum_fusion.turned_ref
  5.7 0.0 copy-done.2
  5.7 10.5 %toeplitz.1 = (bf16[128,16384]{1,0:T(8,128)(2,1)}, bf16[128,16384]{1,0:T(8,128)(2,1)}) custom-call(f32[128,128]{1,0:T(8,128)} %bitcast.38, f32[128,128]{1,0:T(8,128)} %pad_maximum_fusion.turned_ref), custom_call_target="tpu_custom_call" | custom-call | bytes 8388608 | tf_op jit(solution)/shard_map/toeplitz/pallas_call | solution.py:94
  16.2 17.4 %project.1.so_far_ref = f32[3,256,2048]{2,1,0:T(8,128)} custom-call(s32[1]{0:T(128)} %bitcast.4.owner_ref.member_ref, bf16[256,2048]{1,0:T(8,128)(2,1)} %bitcast.35, bf16[3,4096,2048]{2,1,0:T(8,128)(2,1)} %bitcast.15, bf16[3,4096,2048]{2,1,0:T(8,128)(2,1)} %bitcast.16, bf16[3,4096,2048]{2,1,0:T(8,128)(2,1)} %bitcast.17, bf16[3,4096,2048]{2,1,0:T(8,128)(2,1)} %bitcast.18), custom_call_target="tpu_custom_call" | custom-call | flops 6442450944 | bytes 31457280 | tf_op jit(solution)/shard_map/project/pallas_call | solution.py:56
  33.6 0.0 collective-permute-done.x_ref
  33.6 0.0 copy-start
  33.6 1.0 copy-done
  34.6 27.4 %mixer.1.conv_ref = bf16[3,256,2048]{2,1,0:T(8,128)(2,1)} custom-call(s32[1]{0:T(128)} %bitcast.owner_ref.member_ref, bf16[256,2048]{1,0:T(8,128)(2,1)} %copy-done, bf16[3,4096,2048]{2,1,0:T(8,128)(2,1)} %bitcast.19, bf16[3,4096,2048]{2,1,0:T(8,128)(2,1)} %bitcast.20, bf16[3,4096,2048]{2,1,0:T(8,128)(2,1)} %bitcast.21, f32[3,256,2048]{2,1,0:T(8,128)} %project.1.so_far_ref, ...), custom_call_target="tpu_custom_call" | custom-call | flops 6442450944 | bytes 34603008 | tf_op jit(solution)/shard_map/mixer/pallas_call | solution.py:201
  62.0 15.5 %input_grad.3 = bf16[256,2048]{1,0:T(8,128)(2,1)} custom-call(s32[1]{0:T(128)} %bitcast.owner_ref.member_ref, bf16[3,256,2048]{2,1,0:T(8,128)(2,1)} %mixer.1.conv_ref, bf16[3,4096,2048]{2,1,0:T(8,128)(2,1)} %bitcast.22, bf16[3,4096,2048]{2,1,0:T(8,128)(2,1)} %bitcast.23, bf16[3,4096,2048]{2,1,0:T(8,128)(2,1)} %bitcast.24), custom_call_target="tpu_custom_call" | custom-call | flops 1 | bytes 1 | tf_op jit(solution)/shard_map/input_grad/pallas_call | solution.py:259
  77.5 0.6 collective-permute-start.1
  78.1 9.3 %input_grad.4 = bf16[256,1024]{1,0:T(8,128)(2,1)} custom-call(s32[1]{0:T(128)} %bitcast.4.owner_ref.member_ref, bf16[3,256,2048]{2,1,0:T(8,128)(2,1)} %mixer.1.conv_ref, bf16[3,4096,2048]{2,1,0:T(8,128)(2,1)} %bitcast.25, bf16[3,4096,2048]{2,1,0:T(8,128)(2,1)} %bitcast.26, bf16[3,4096,2048]{2,1,0:T(8,128)(2,1)} %bitcast.27, bf16[256,2048]{1,0:T(8,128)(2,1)} %bitcast.32), custom_call_target="tpu_custom_call" | custom-call | flops 1 | bytes 1 | tf_op jit(solution)/shard_map/input_grad/pallas_call | solution.py:259
  87.4 4.1 %collective-permute-start.2 = (bf16[256,1024]{1,0:T(8,128)(2,1)}, bf16[256,1024]{1,0:T(8,128)(2,1)S(1)}, u32[]{:S(2)}, u32[]{:S(2)}) collective-permute-start(bf16[256,1024]{1,0:T(8,128)(2,1)} %input_grad.4), channel_id=1, source_target_pairs={{0,30},{1,31},{2,0},{3,1},{4,2},{5,3},{6,4},{7,5},{8,6},{9,7},{10,... | collective-permute-start | bytes 1572872 | tf_op jit(solution)/shard_map/ppermute | solution.py:348
  91.4 9.3 %input_grad.5 = bf16[256,1024]{1,0:T(8,128)(2,1)} custom-call(s32[1]{0:T(128)} %bitcast.4.owner_ref.member_ref, bf16[3,256,2048]{2,1,0:T(8,128)(2,1)} %mixer.1.conv_ref, bf16[3,4096,2048]{2,1,0:T(8,128)(2,1)} %bitcast.28, bf16[3,4096,2048]{2,1,0:T(8,128)(2,1)} %bitcast.29, bf16[3,4096,2048]{2,1,0:T(8,128)(2,1)} %bitcast.30, bf16[256,2048]{1,0:T(8,128)(2,1)} %bitcast.33), custom_call_target="tpu_custom_call" | custom-call | flops 1 | bytes 1 | tf_op jit(solution)/shard_map/input_grad/pallas_call | solution.py:259
  100.8 1.1 collective-permute-start.3
  101.9 0.2 collective-permute-done.2.refs_1_
  102.1 0.0 copy-start.3
  102.1 7.5 %collective-permute-done.3.refs_2_ = bf16[256,1024]{1,0:T(8,128)(2,1)S(1)} collective-permute-done((bf16[256,1024]{1,0:T(8,128)(2,1)}, bf16[256,1024]{1,0:T(8,128)(2,1)S(1)}, u32[]{:S(2)}, u32[]{:S(2)}) %collective-permute-start.3) | collective-permute-done | bytes 524320 | tf_op jit(solution)/shard_map/ppermute | solution.py:348
  109.6 0.0 copy-start.4
  109.6 0.0 collective-permute-done.1.refs_0_
  109.6 0.0 copy-done.3
  109.6 0.8 copy-done.4
  110.4 0.0 copy-start.1
  110.4 1.0 copy-done.1
  111.3 2.8 %join.1 = bf16[256,2048]{1,0:T(8,128)(2,1)} custom-call(bf16[256,2048]{1,0:T(8,128)(2,1)} %copy-done.1, bf16[256,1024]{1,0:T(8,128)(2,1)} %copy-done.3, bf16[256,1024]{1,0:T(8,128)(2,1)} %copy-done.4), custom_call_target="tpu_custom_call" | custom-call | bytes 3145728 | tf_op jit(solution)/shard_map/join/pallas_call | solution.py:287
Async XLA Ops:
  0.0 33.6 %collective-permute-start = (bf16[256,2048]{1,0:T(8,128)(2,1)}, bf16[256,2048]{1,0:T(8,128)(2,1)S(1)}, u32[]{:S(2)}, u32[]{:S(2)}) collective-permute-start(bf16[256,2048]{1,0:T(8,128)(2,1)} %bitcast.34), channel_id=1, source_target_pairs={{1,0},{0,1},{3,2},{2,3},{5,4},{4,5},{7,6},{6,7},{9,8},{8,9},{11,10... | collective-permute-start | bytes 3145736 | tf_op jit(solution)/shard_map/ppermute | solution.py:328
  3.0 2.7 %copy-start.2 = (f32[1,128,128]{1,2,0:T(8,128)}, f32[1,128,128]{1,2,0:T(8,128)S(1)}, u32[]{:S(2)}) copy-start(f32[1,128,128]{1,2,0:T(8,128)S(1)} %copy.8) | copy-start | bytes 196612
  33.6 1.0 copy-start
  77.5 32.1 %collective-permute-start.1 = (bf16[256,2048]{1,0:T(8,128)(2,1)}, bf16[256,2048]{1,0:T(8,128)(2,1)S(1)}, u32[]{:S(2)}, u32[]{:S(2)}) collective-permute-start(bf16[256,2048]{1,0:T(8,128)(2,1)} %input_grad.3), channel_id=1, source_target_pairs={{0,31},{1,30},{2,1},{3,0},{4,3},{5,2},{6,5},{7,4},{8,7},{9,6},{10,... | collective-permute-start | bytes 3145736 | tf_op jit(solution)/shard_map/ppermute | solution.py:348
  87.4 14.7 %collective-permute-start.2 = (bf16[256,1024]{1,0:T(8,128)(2,1)}, bf16[256,1024]{1,0:T(8,128)(2,1)S(1)}, u32[]{:S(2)}, u32[]{:S(2)}) collective-permute-start(bf16[256,1024]{1,0:T(8,128)(2,1)} %input_grad.4), channel_id=1, source_target_pairs={{0,30},{1,31},{2,0},{3,1},{4,2},{5,3},{6,4},{7,5},{8,6},{9,7},{10,... | collective-permute-start | bytes 1572872 | tf_op jit(solution)/shard_map/ppermute | solution.py:348
  100.8 8.8 %collective-permute-start.3 = (bf16[256,1024]{1,0:T(8,128)(2,1)}, bf16[256,1024]{1,0:T(8,128)(2,1)S(1)}, u32[]{:S(2)}, u32[]{:S(2)}) collective-permute-start(bf16[256,1024]{1,0:T(8,128)(2,1)} %input_grad.5), channel_id=1, source_target_pairs={{0,30},{1,31},{2,0},{3,1},{4,2},{5,3},{6,4},{7,5},{8,6},{9,7},{10,... | collective-permute-start | bytes 1572872 | tf_op jit(solution)/shard_map/ppermute | solution.py:348
  102.1 7.5 %copy-start.3 = (bf16[256,1024]{1,0:T(8,128)(2,1)}, bf16[256,1024]{1,0:T(8,128)(2,1)S(1)}, u32[]{:S(2)}) copy-start(bf16[256,1024]{1,0:T(8,128)(2,1)S(1)} %collective-permute-done.2.refs_1_) | copy-start | bytes 1572868
  109.6 0.8 copy-start.4
  110.4 1.0 copy-start.1

commit v3 on v2

v3 whole, which is shorter than its diff:
```python
import functools

import jax
import jax.numpy as jnp
from jax import lax
from jax.experimental import pallas as pl
from jax.experimental.pallas import tpu as pltpu
from jax.sharding import PartitionSpec as P

F32 = jnp.float32
BF16 = jnp.bfloat16
LANES = 128
MIB = 1024 * 1024
VMEM_LIMIT = 8 * MIB
SPAN = 256
AWAY_CUTS = (8,)
OWN_CUTS = (4, 4)

IN_VMEM = pl.BlockSpec(memory_space=pltpu.VMEM)
IN_SMEM = pl.BlockSpec(memory_space=pltpu.SMEM)
ANYWHERE = pl.BlockSpec(memory_space=pl.ANY)


def params():
    return pltpu.CompilerParams(vmem_limit_bytes=VMEM_LIMIT)


def cost(flops, moved):
    return pl.CostEstimate(flops=flops, bytes_accessed=moved, transcendentals=0)


def held(array):
    return pltpu.with_memory_space_constraint(array, pltpu.VMEM)


def load_kernel(
    me_ref, x_ref, w_ref, medium_ref, held_ref, so_far_ref, first_ref, second_ref,
    sums, matrices, turned_ref, own_sem, rest_sem, sums_sem, first_sem, second_sem,
    *, members, width, rest_rows
):
    rows, depth = x_ref.shape
    channels = w_ref.shape[2]
    length, groups = medium_ref.shape
    me = me_ref[0]
    own_row = pl.multiple_of(me * depth, depth)
    blocks = channels // width

    def own_copy(n):
        place = (
            n // blocks,
            pl.ds(own_row, depth),
            pl.ds(pl.multiple_of(n % blocks * width, width), width),
        )
        return pltpu.make_async_copy(w_ref.at[place], held_ref.at[place], own_sem.at[n])

    rest = []
    for k in range(1, members):
        row = pl.multiple_of(lax.rem(me + k, members) * depth, depth)
        for i in range(3):
            for part in range(depth // rest_rows):
                place = (i, pl.ds(pl.multiple_of(row + part * rest_rows, rest_rows), rest_rows))
                rest.append(
                    pltpu.make_async_copy(
                        w_ref.at[place], held_ref.at[place], rest_sem.at[len(rest)]
                    )
                )
    for n in range(3 * blocks):
        own_copy(n).start()
    for copy in rest:
        copy.start()

    places = lax.broadcasted_iota(jnp.int32, (length, length), 0)
    lags = lax.broadcasted_iota(jnp.int32, (length, length), 1)
    medium = medium_ref[...].astype(BF16)
    turns = (places == lags, (places + lags) % length == 0)
    for n, turn in enumerate(turns):
        turned_ref[n] = lax.dot_general(
            medium,
            jnp.where(turn, 1.0, 0.0).astype(BF16),
            (((0,), (0,)), ((), ())),
            preferred_element_type=F32,
        )
    step = 8
    keeps = (lags >= places, lags <= places)
    targets = (second_ref, first_ref)
    target_sems = (second_sem, first_sem)

    def matrix_copy(n, turn):
        slot = n % 2
        lanes = pl.ds(pl.multiple_of(n * step * length, step * length), step * length)
        return pltpu.make_async_copy(
            matrices.at[turn, slot], targets[turn].at[:, lanes], target_sems[turn].at[slot]
        )

    def matrix_step(n, carry):
        for turn in range(2):
            @pl.when(n >= 2)
            def _():
                matrix_copy(n - 2, turn).wait()

            lines = turned_ref[turn, pl.ds(pl.multiple_of(n * step, step), step), :]
            for g in range(step):
                base = jnp.broadcast_to(lines[g : g + 1], (length, length))
                rolled = pltpu.roll(base, 0, 1, stride=1, stride_axis=0)
                matrices[turn, n % 2, :, g * length : (g + 1) * length] = jnp.where(
                    keeps[turn], rolled, 0.0
                ).astype(BF16)
            matrix_copy(n, turn).start()
        return carry

    matrix_steps = groups // step
    lax.fori_loop(0, matrix_steps, matrix_step, 0)
    for n in range(max(matrix_steps - 2, 0), matrix_steps):
        for turn in range(2):
            matrix_copy(n, turn).wait()

    def sums_copy(n):
        slot = n % 2
        lanes = pl.ds(pl.multiple_of(n % blocks * width, width), width)
        return pltpu.make_async_copy(
            sums.at[slot], so_far_ref.at[n // blocks, :, lanes], sums_sem.at[slot]
        )

    def sums_step(n, carry):
        own_copy(n).wait()

        @pl.when(n >= 2)
        def _():
            sums_copy(n - 2).wait()

        lanes = pl.ds(pl.multiple_of(n % blocks * width, width), width)
        sums[n % 2] = jnp.dot(
            x_ref[...],
            held_ref[n // blocks, pl.ds(own_row, depth), lanes],
            preferred_element_type=F32,
        )
        sums_copy(n).start()
        return carry

    lax.fori_loop(0, 3 * blocks, sums_step, 0)
    for n in range(3 * blocks - 2, 3 * blocks):
        sums_copy(n).wait()
    for copy in rest:
        copy.wait()


def load(me, x, weights, medium, members):
    rows, depth = x.shape
    channels = weights.shape[2]
    length, groups = medium.shape
    width = min(512, channels)
    rest_rows = min(512, depth)
    matrix = jax.ShapeDtypeStruct((length, groups * length), BF16)
    return pl.pallas_call(
        functools.partial(load_kernel, members=members, width=width, rest_rows=rest_rows),
        in_specs=[IN_SMEM, IN_VMEM, ANYWHERE, IN_VMEM],
        out_specs=[IN_VMEM, ANYWHERE, ANYWHERE, ANYWHERE],
        out_shape=[
            pltpu.VMEM(weights.shape, BF16),
            jax.ShapeDtypeStruct((3, rows, channels), F32),
            matrix,
            matrix,
        ],
        scratch_shapes=[
            pltpu.VMEM((2, rows, width), F32),
            pltpu.VMEM((2, 2, length, 8 * length), BF16),
            pltpu.VMEM((2, groups, length), F32),
            pltpu.SemaphoreType.DMA((3 * channels // width,)),
            pltpu.SemaphoreType.DMA(((members - 1) * 3 * depth // rest_rows,)),
            pltpu.SemaphoreType.DMA((2,)),
            pltpu.SemaphoreType.DMA((2,)),
            pltpu.SemaphoreType.DMA((2,)),
        ],
        compiler_params=params(),
        cost_estimate=cost(6 * rows * depth * channels, 2 * weights.size),
        name="load",
    )(me, x, weights, medium)


def down(series, steps):
    moved = pltpu.roll(series, steps, 0)
    row = lax.broadcasted_iota(jnp.int32, (8, series.shape[1]), 0)
    return jnp.concatenate([jnp.where(row >= steps, moved[:8], 0.0), moved[8:]], axis=0)


def up(series, steps):
    length = series.shape[0]
    moved = pltpu.roll(series, length - steps, 0)
    row = lax.broadcasted_iota(jnp.int32, (8, series.shape[1]), 0)
    last = jnp.where(row < 8 - steps, moved[length - 8 :], 0.0)
    return jnp.concatenate([moved[: length - 8], last], axis=0)


def short_filter(series, taps, move):
    shifted = [series] + [move(series, steps) for steps in range(1, 4)]
    near = taps[0] * series
    far = None
    for lag in range(1, len(taps)):
        term = taps[lag] * shifted[lag % 4]
        if lag < 4:
            near = near + term
        else:
            far = term if far is None else far + term
    if far is None:
        return near
    return near + move(far, 4)


def group_masks(members, width):
    group = lax.broadcasted_iota(jnp.int32, (1, width), 1) % LANES // members
    return [jnp.where(group == g, 1.0, 0.0).astype(BF16) for g in range(LANES // members)]


def medium_filter(toeplitz, series, masks):
    rounded = series.astype(BF16)
    stacked = jnp.concatenate([rounded * mask for mask in masks], axis=0)
    return jnp.dot(toeplitz, stacked, preferred_element_type=F32)


def mixer_kernel(
    me_ref, w_ref, taps_ref, skip_ref, grad_ref, so_far_ref, first_ref, second_ref, *rest,
    members, micro, group, width
):
    x_refs = rest[: members - 1]
    out_ref, so_far, first, second, so_far_sem, first_sem, second_sem = rest[members - 1 :]
    rows = out_ref.shape[1]
    channels = out_ref.shape[2]
    length = rows // micro
    depth = x_refs[0].shape[1]
    reach = taps_ref.shape[0] * LANES // 3 // channels
    tiles = channels // LANES
    spread = LANES // group * length
    window = width // group * length
    blocks = channels // width
    me = me_ref[0]
    masks = group_masks(group, micro * LANES)

    def copies(n):
        slot = n % 2
        lanes = pl.ds(pl.multiple_of(n * width, width), width)
        wide = pl.ds(pl.multiple_of(n * window, window), window)
        return (
            pltpu.make_async_copy(
                so_far_ref.at[:, :, lanes], so_far.at[slot], so_far_sem.at[slot]
            ),
            pltpu.make_async_copy(first_ref.at[:, wide], first.at[slot], first_sem.at[slot]),
            pltpu.make_async_copy(second_ref.at[:, wide], second.at[slot], second_sem.at[slot]),
        )

    for copy in copies(0):
        copy.start()

    def step(n, carry):
        slot = n % 2

        @pl.when(n + 1 < blocks)
        def _():
            for copy in copies(n + 1):
                copy.start()

        for copy in copies(n):
            copy.wait()
        lanes_all = pl.ds(pl.multiple_of(n * width, width), width)
        projected = []
        for i in range(3):
            total = so_far[slot, i]
            for k, x_ref in enumerate(x_refs):
                row = pl.multiple_of(lax.rem(me + k + 1, members) * depth, depth)
                total = total + jnp.dot(
                    x_ref[...],
                    w_ref[i, pl.ds(row, depth), lanes_all],
                    preferred_element_type=F32,
                )
            projected.append(total)
        for tile in range(width // LANES):
            inner = slice(tile * LANES, (tile + 1) * LANES)
            lanes = pl.ds(pl.multiple_of(n * width + tile * LANES, LANES), LANES)
            line = n * (width // LANES) + tile
            taps = [
                [taps_ref[pl.ds((j * 3 + i) * tiles + line, 1), :] for j in range(reach)]
                for i in range(3)
            ]
            skip = skip_ref[0:1, lanes]
            places = slice(tile * spread, (tile + 1) * spread)
            query, key, value, upstream = [], [], [], []
            for b in range(micro):
                span = slice(b * length, (b + 1) * length)
                series = [short_filter(projected[i][span, inner], taps[i], down) for i in range(3)]
                query.append(series[0])
                key.append(series[1])
                value.append(series[2])
                upstream.append(grad_ref[span, lanes].astype(F32))
            product = [k * v for k, v in zip(key, value)]
            mixed = medium_filter(first[slot, :, places], jnp.concatenate(product, axis=1), masks)
            mixed_grad = [u * q for u, q in zip(upstream, query)]
            product_grad = medium_filter(
                second[slot, :, places], jnp.concatenate(mixed_grad, axis=1), masks
            )
            for b in range(micro):
                span = slice(b * length, (b + 1) * length)
                part = slice(b * LANES, (b + 1) * LANES)
                back = product_grad[:, part] + skip * mixed_grad[b]
                grads = [
                    upstream[b] * (mixed[:, part] + skip * product[b]),
                    back * value[b],
                    back * key[b],
                ]
                for i in range(3):
                    out_ref[i, span, lanes] = short_filter(grads[i], taps[i], up).astype(BF16)
        return carry

    lax.fori_loop(0, blocks, step, 0)


def mixer(me, weights, taps, skip, grad, so_far, first, second, others, micro):
    rows, depth = others[0].shape
    members = len(others) + 1
    channels = weights.shape[2]
    length = rows // micro
    groups = first.shape[1] // length
    group = channels // groups
    width = min(256, channels)
    window = width // group * length
    return pl.pallas_call(
        functools.partial(
            mixer_kernel, members=members, micro=micro, group=group, width=width
        ),
        in_specs=[IN_SMEM, IN_VMEM, IN_VMEM, IN_VMEM, IN_VMEM]
        + [ANYWHERE] * 3
        + [IN_VMEM] * len(others),
        out_specs=IN_VMEM,
        out_shape=pltpu.VMEM((3, rows, channels), BF16),
        scratch_shapes=[
            pltpu.VMEM((2, 3, rows, width), F32),
            pltpu.VMEM((2, length, window), BF16),
            pltpu.VMEM((2, length, window), BF16),
            pltpu.SemaphoreType.DMA((2,)),
            pltpu.SemaphoreType.DMA((2,)),
            pltpu.SemaphoreType.DMA((2,)),
        ],
        compiler_params=params(),
        cost_estimate=cost(6 * rows * depth * channels, 18 * rows * channels),
        name="mixer",
    )(me, held(weights), taps, skip, grad, so_far, first, second, *map(held, others))


def input_grad_kernel(member_ref, conv_ref, w_ref, *rest, first, depth, width):
    out_ref = rest[-1]
    start = member_ref[0] * depth + first
    for step in range(out_ref.shape[1] // width):
        place = slice(step * width, (step + 1) * width)
        row = pl.multiple_of(start + step * width, width)
        total = None
        for i in range(3):
            term = lax.dot_general(
                w_ref[i, pl.ds(row, width), :],
                conv_ref[i],
                (((1,), (1,)), ((), ())),
                preferred_element_type=F32,
            )
            total = term if total is None else total + term
        total = total.T
        if len(rest) > 1:
            total = total + rest[0][:, first + step * width : first + (step + 1) * width].astype(F32)
        out_ref[:, place] = total.astype(BF16)


def input_grad(conv, weights, member, first, extent, depth, grad=None):
    rows = conv.shape[1]
    operands = [conv, weights] + ([] if grad is None else [grad])
    return pl.pallas_call(
        functools.partial(input_grad_kernel, first=first, depth=depth, width=SPAN),
        in_specs=[IN_SMEM] + [IN_VMEM] * len(operands),
        out_specs=IN_VMEM,
        out_shape=jax.ShapeDtypeStruct((rows, extent), BF16),
        compiler_params=params(),
        cost_estimate=cost(1, 1),
        name="input_grad",
    )(member, held(conv), held(weights), *operands[2:])


def join(pieces, depth):
    rows = pieces[0][1].shape[0]

    def kernel(*refs):
        out_ref = refs[-1]
        for start in range(0, depth, SPAN):
            total = None
            for (first, piece), ref in zip(pieces, refs):
                if first <= start < first + piece.shape[1]:
                    term = ref[:, start - first : start - first + SPAN].astype(F32)
                    total = term if total is None else total + term
            out_ref[:, start : start + SPAN] = total.astype(BF16)

    return pl.pallas_call(
        kernel,
        out_shape=jax.ShapeDtypeStruct((rows, depth), BF16),
        compiler_params=params(),
        cost_estimate=cost(0, 6 * rows * depth),
        name="join",
    )(*[piece for _, piece in pieces])


def cuts_of(eighths, depth):
    step = depth // 8
    if step % SPAN:
        return [(0, depth)]
    first, spans = 0, []
    for count in eighths:
        spans.append((first, count * step))
        first += count * step
    return spans


def local(block_input, incoming, in_weight, short_taps, medium_taps, skip_weight):
    micro, length, depth = block_input.shape[1:]
    rows = micro * length
    members = lax.axis_size("tp")
    sections = lax.axis_size("section")
    me = lax.axis_index("tp")
    weights = jnp.transpose(in_weight[0], (1, 0, 2))
    x = block_input.reshape(rows, depth)
    grad = incoming.reshape(rows, depth)

    def owner(step):
        return jnp.full((1,), lax.rem(me + step, members), jnp.int32)

    others = []
    for k in range(1, members):
        pairs = [((m + k) % members, m) for m in range(members)]
        others.append(lax.ppermute(x, "tp", pairs))
    weights, so_far, first, second = load(owner(0), x, weights, medium_taps[0], members)
    conv = mixer(
        owner(0), weights, short_taps.reshape(-1, LANES), skip_weight, grad, so_far, first,
        second, others, micro,
    )
    pieces = []
    for k in list(range(1, members)) + [0]:
        pairs = [
            (s * members + m, (s - 1) % sections * members + (m + k) % members)
            for s in range(sections)
            for m in range(members)
        ]
        for first_column, extent in cuts_of(AWAY_CUTS if k else OWN_CUTS, depth):
            share = input_grad(
                conv, weights, owner(k), first_column, extent, depth, None if k else grad
            )
            pieces.append((first_column, lax.ppermute(share, ("section", "tp"), pairs)))
    return join(pieces, depth).reshape(block_input.shape)


def solution(mesh):
    in_specs = (
        P("section", None, None, "tp"),
        P("section", None, None, "tp"),
        P("section", None, None, "tp"),
        P("section", None, None, "tp"),
        P("section", None, "tp"),
        P("section", "tp"),
    )
    out_specs = P("section", None, None, "tp")
    return jax.shard_map(local, mesh=mesh, in_specs=in_specs, out_specs=out_specs, check_vma=False)
```

time: 115 us -> 91.2 us (0.79)
  Pallas kernels: 92.2 us -> 68.6 us
  local copies, waits for them, and re-layouts: 5.61 us -> 0 us
  waiting for transfers between devices: 7.69 us -> 13 us
  starting transfers between devices: 7.81 us -> 9.28 us
    pallas_call x6 -> x5, Pallas kernels: 89.5 us -> 67.4 us  [the longest x1 26.1 us: mixer(): pl.pallas_call(functools.partial(mixer_kernel, members=members, micro=mic...]
    unnamed x12 -> x0, local copies, waits for them, and re-layouts: 4.64 us -> none
    ppermute x3, waiting for transfers between devices: 7.69 us -> 12.2 us  [local(): pieces.append((first_column, lax.ppermute(share, ('section', 'tp'), pairs)))]
    pallas_call x1, Pallas kernels: 2.75 us -> 1.24 us  [join(): pl.pallas_call(kernel, out_shape=jax.ShapeDtypeStruct((rows, depth), BF16...]
    ppermute x3, starting transfers between devices: 5.77 us -> 7.24 us  [local(): pieces.append((first_column, lax.ppermute(share, ('section', 'tp'), pairs)))]
  transfers between devices with their start and end apart: 4 -> 4, of which waited for: 2 -> 3; matrix products, arithmetic and copies ran while one was open for 3% -> 0% of each run, Pallas kernels for 41% -> 37%
where the time goes in v3:
time: 91.2 us; the launch traced here: 91 us
  Pallas kernels  68.6 us (75%)
  waiting for transfers between devices  13 us (14%)
  starting transfers between devices  9.28 us (10%)
    pallas_call x1, Pallas kernels, mixer(): pl.pallas_call(functools.partial(mixer_kernel, members=members, micro=mic...  26.1 us
    pallas_call x1, Pallas kernels, load(): pl.pallas_call(functools.partial(load_kernel, members=members, width=widt...  22.2 us
    pallas_call x3, Pallas kernels, input_grad(): pl.pallas_call(functools.partial(input_grad_kernel, first=first, depth=de...  19 us
    ppermute x3, waiting for transfers between devices, local(): pieces.append((first_column, lax.ppermute(share, ('section', 'tp'), pairs)))  12.2 us
    ppermute x3, starting transfers between devices, local(): pieces.append((first_column, lax.ppermute(share, ('section', 'tp'), pairs)))  7.24 us
    ppermute x1, starting transfers between devices, local(): others.append(lax.ppermute(x, 'tp', pairs))  2.04 us
  transfers between devices with their start and end apart: 4, of which 3 were waited for; matrix products, arithmetic and copies ran while one was open for 0% of the time, Pallas kernels for 37%

profile of v3, /device:TPU:1, one launch (start us, length us, event | category | flops | bytes accessed | tf_op | source)
XLA Modules:
  0.0 91.0 jit_solution(5111988434790087577)
XLA Ops:
  0.0 2.0 %collective-permute-start = (bf16[256,2048]{1,0:T(8,128)(2,1)}, bf16[256,2048]{1,0:T(8,128)(2,1)S(1)}, u32[]{:S(2)}, u32[]{:S(2)}) collective-permute-start(bf16[256,2048]{1,0:T(8,128)(2,1)} %bitcast.14), channel_id=1, source_target_pairs={{1,0},{0,1},{3,2},{2,3},{5,4},{4,5},{7,6},{6,7},{9,8},{8,9},{11,10... | collective-permute-start | bytes 3145736 | tf_op jit(solution)/shard_map/ppermute | solution.py:431
  2.0 22.2 %load.1 = (bf16[3,4096,2048]{2,1,0:T(8,128)(2,1)S(1)}, f32[3,256,2048]{2,1,0:T(8,128)}, bf16[128,16384]{1,0:T(8,128)(2,1)}, bf16[128,16384]{1,0:T(8,128)(2,1)}) custom-call(s32[1]{0:T(128)} %bitcast.1.me_ref.member_ref, bf16[256,2048]{1,0:T(8,128)(2,1)} %bitcast.15, bf16[3,4096,2048]{2,1,0:T(8,128)(2,1)} %bitcast.10, f32[128,128]{1,0:T(8,128)} %bitcast.17), custom_call_target="tpu_custom_call" | custom-call | flops 6442450944 | bytes 50331648 | tf_op jit(solution)/shard_map/load/pallas_call | solution.py:154
  24.3 0.8 collective-permute-done.rest_0_
  25.1 26.1 %mixer.1.conv_ref = bf16[3,256,2048]{2,1,0:T(8,128)(2,1)S(1)} custom-call(s32[1]{0:T(128)} %bitcast.1.me_ref.member_ref, bf16[3,4096,2048]{2,1,0:T(8,128)(2,1)S(1)} %get-tuple-element.9.w_ref, f32[336,128]{1,0:T(8,128)} %bitcast.16, f32[1,2048]{1,0:T(1,128)} %skip_ref.1, bf16[256,2048]{1,0:T(8,128)(2,1)} %bitcast.11, ...), custom_call_target="tpu_custom_call" | custom-call | flops 6442450944 | bytes 9437184 | tf_op jit(solution)/shard_map/mixer/pallas_call | solution.py:324
  51.3 7.8 %input_grad.3 = bf16[256,2048]{1,0:T(8,128)(2,1)} custom-call(s32[1]{0:T(128)} %bitcast.member_ref, bf16[3,256,2048]{2,1,0:T(8,128)(2,1)S(1)} %mixer.1.conv_ref, bf16[3,4096,2048]{2,1,0:T(8,128)(2,1)S(1)} %get-tuple-element.9.w_ref), custom_call_target="tpu_custom_call" | custom-call | flops 1 | bytes 1 | tf_op jit(solution)/shard_map/input_grad/pallas_call | solution.py:371
  59.0 2.6 %collective-permute-start.1 = (bf16[256,2048]{1,0:T(8,128)(2,1)}, bf16[256,2048]{1,0:T(8,128)(2,1)S(1)}, u32[]{:S(2)}, u32[]{:S(2)}) collective-permute-start(bf16[256,2048]{1,0:T(8,128)(2,1)} %input_grad.3), channel_id=1, source_target_pairs={{0,31},{1,30},{2,1},{3,0},{4,3},{5,2},{6,5},{7,4},{8,7},{9,6},{10,... | collective-permute-start | bytes 3145736 | tf_op jit(solution)/shard_map/ppermute | solution.py:448
  61.6 5.6 %input_grad.4 = bf16[256,1024]{1,0:T(8,128)(2,1)} custom-call(s32[1]{0:T(128)} %bitcast.1.me_ref.member_ref, bf16[3,256,2048]{2,1,0:T(8,128)(2,1)S(1)} %mixer.1.conv_ref, bf16[3,4096,2048]{2,1,0:T(8,128)(2,1)S(1)} %get-tuple-element.9.w_ref, bf16[256,2048]{1,0:T(8,128)(2,1)} %bitcast.12), custom_call_target="tpu_custom_call" | custom-call | flops 1 | bytes 1 | tf_op jit(solution)/shard_map/input_grad/pallas_call | solution.py:371
  67.2 3.0 %collective-permute-start.2 = (bf16[256,1024]{1,0:T(8,128)(2,1)}, bf16[256,1024]{1,0:T(8,128)(2,1)S(1)}, u32[]{:S(2)}, u32[]{:S(2)}) collective-permute-start(bf16[256,1024]{1,0:T(8,128)(2,1)} %input_grad.4), channel_id=1, source_target_pairs={{0,30},{1,31},{2,0},{3,1},{4,2},{5,3},{6,4},{7,5},{8,6},{9,7},{10,... | collective-permute-start | bytes 1572872 | tf_op jit(solution)/shard_map/ppermute | solution.py:448
  70.2 5.6 %input_grad.5 = bf16[256,1024]{1,0:T(8,128)(2,1)} custom-call(s32[1]{0:T(128)} %bitcast.1.me_ref.member_ref, bf16[3,256,2048]{2,1,0:T(8,128)(2,1)S(1)} %mixer.1.conv_ref, bf16[3,4096,2048]{2,1,0:T(8,128)(2,1)S(1)} %get-tuple-element.9.w_ref, bf16[256,2048]{1,0:T(8,128)(2,1)} %bitcast.13), custom_call_target="tpu_custom_call" | custom-call | flops 1 | bytes 1 | tf_op jit(solution)/shard_map/input_grad/pallas_call | solution.py:371
  75.8 1.7 %collective-permute-start.3 = (bf16[256,1024]{1,0:T(8,128)(2,1)}, bf16[256,1024]{1,0:T(8,128)(2,1)S(1)}, u32[]{:S(2)}, u32[]{:S(2)}) collective-permute-start(bf16[256,1024]{1,0:T(8,128)(2,1)} %input_grad.5), channel_id=1, source_target_pairs={{0,30},{1,31},{2,0},{3,1},{4,2},{5,3},{6,4},{7,5},{8,6},{9,7},{10,... | collective-permute-start | bytes 1572872 | tf_op jit(solution)/shard_map/ppermute | solution.py:448
  77.5 4.4 %collective-permute-done.2.refs_1_ = bf16[256,1024]{1,0:T(8,128)(2,1)S(1)} collective-permute-done((bf16[256,1024]{1,0:T(8,128)(2,1)}, bf16[256,1024]{1,0:T(8,128)(2,1)S(1)}, u32[]{:S(2)}, u32[]{:S(2)}) %collective-permute-start.2) | collective-permute-done | bytes 524320 | tf_op jit(solution)/shard_map/ppermute | solution.py:448
  82.0 7.8 %collective-permute-done.3.refs_2_ = bf16[256,1024]{1,0:T(8,128)(2,1)S(1)} collective-permute-done((bf16[256,1024]{1,0:T(8,128)(2,1)}, bf16[256,1024]{1,0:T(8,128)(2,1)S(1)}, u32[]{:S(2)}, u32[]{:S(2)}) %collective-permute-start.3) | collective-permute-done | bytes 524320 | tf_op jit(solution)/shard_map/ppermute | solution.py:448
  89.7 0.0 collective-permute-done.1.refs_0_
  89.7 1.2 %join.1 = bf16[256,2048]{1,0:T(8,128)(2,1)} custom-call(bf16[256,2048]{1,0:T(8,128)(2,1)S(1)} %collective-permute-done.1.refs_0_, bf16[256,1024]{1,0:T(8,128)(2,1)S(1)} %collective-permute-done.2.refs_1_, bf16[256,1024]{1,0:T(8,128)(2,1)S(1)} %collective-permute-done.3.refs_2_), custom_call_target="tpu_custom_call" | custom-call | bytes 3145728 | tf_op jit(solution)/shard_map/join/pallas_call | solution.py:395
Async XLA Ops:
  0.0 25.1 %collective-permute-start = (bf16[256,2048]{1,0:T(8,128)(2,1)}, bf16[256,2048]{1,0:T(8,128)(2,1)S(1)}, u32[]{:S(2)}, u32[]{:S(2)}) collective-permute-start(bf16[256,2048]{1,0:T(8,128)(2,1)} %bitcast.14), channel_id=1, source_target_pairs={{1,0},{0,1},{3,2},{2,3},{5,4},{4,5},{7,6},{6,7},{9,8},{8,9},{11,10... | collective-permute-start | bytes 3145736 | tf_op jit(solution)/shard_map/ppermute | solution.py:431
  59.0 30.7 %collective-permute-start.1 = (bf16[256,2048]{1,0:T(8,128)(2,1)}, bf16[256,2048]{1,0:T(8,128)(2,1)S(1)}, u32[]{:S(2)}, u32[]{:S(2)}) collective-permute-start(bf16[256,2048]{1,0:T(8,128)(2,1)} %input_grad.3), channel_id=1, source_target_pairs={{0,31},{1,30},{2,1},{3,0},{4,3},{5,2},{6,5},{7,4},{8,7},{9,6},{10,... | collective-permute-start | bytes 3145736 | tf_op jit(solution)/shard_map/ppermute | solution.py:448
  67.2 14.7 %collective-permute-start.2 = (bf16[256,1024]{1,0:T(8,128)(2,1)}, bf16[256,1024]{1,0:T(8,128)(2,1)S(1)}, u32[]{:S(2)}, u32[]{:S(2)}) collective-permute-start(bf16[256,1024]{1,0:T(8,128)(2,1)} %input_grad.4), channel_id=1, source_target_pairs={{0,30},{1,31},{2,0},{3,1},{4,2},{5,3},{6,4},{7,5},{8,6},{9,7},{10,... | collective-permute-start | bytes 1572872 | tf_op jit(solution)/shard_map/ppermute | solution.py:448
  75.8 13.9 %collective-permute-start.3 = (bf16[256,1024]{1,0:T(8,128)(2,1)}, bf16[256,1024]{1,0:T(8,128)(2,1)S(1)}, u32[]{:S(2)}, u32[]{:S(2)}) collective-permute-start(bf16[256,1024]{1,0:T(8,128)(2,1)} %input_grad.5), channel_id=1, source_target_pairs={{0,30},{1,31},{2,0},{3,1},{4,2},{5,3},{6,4},{7,5},{8,6},{9,7},{10,... | collective-permute-start | bytes 1572872 | tf_op jit(solution)/shard_map/ppermute | solution.py:448

commit v4 on v3

--- a/solution.py
+++ b/solution.py
@@ -21,8 +21,8 @@
 ANYWHERE = pl.BlockSpec(memory_space=pl.ANY)
 
 
-def params():
-    return pltpu.CompilerParams(vmem_limit_bytes=VMEM_LIMIT)
+def params(limit=VMEM_LIMIT):
+    return pltpu.CompilerParams(vmem_limit_bytes=limit)
 
 
 def cost(flops, moved):
@@ -177,44 +177,40 @@
     )(me, x, weights, medium)
 
 
-def down(series, steps):
-    moved = pltpu.roll(series, steps, 0)
-    row = lax.broadcasted_iota(jnp.int32, (8, series.shape[1]), 0)
-    return jnp.concatenate([jnp.where(row >= steps, moved[:8], 0.0), moved[8:]], axis=0)
-
-
-def up(series, steps):
-    length = series.shape[0]
-    moved = pltpu.roll(series, length - steps, 0)
-    row = lax.broadcasted_iota(jnp.int32, (8, series.shape[1]), 0)
-    last = jnp.where(row < 8 - steps, moved[length - 8 :], 0.0)
-    return jnp.concatenate([moved[: length - 8], last], axis=0)
-
-
-def short_filter(series, taps, move):
-    shifted = [series] + [move(series, steps) for steps in range(1, 4)]
-    near = taps[0] * series
-    far = None
-    for lag in range(1, len(taps)):
-        term = taps[lag] * shifted[lag % 4]
-        if lag < 4:
-            near = near + term
-        else:
-            far = term if far is None else far + term
-    if far is None:
-        return near
-    return near + move(far, 4)
+STRIP = 8
+NEAR = 4
+
+
+def strip_filter(strip, taps, passed, back):
+    row = lax.broadcasted_iota(jnp.int32, strip.shape, 0)
+
+    def moved(series, lag):
+        return pltpu.roll(series, STRIP - lag if back else lag, 0)
+
+    def joined(own, before, lag):
+        outside = row >= STRIP - lag if back else row < lag
+        return jnp.where(outside, 0.0 if before is None else before, own)
+
+    turned = [moved(strip, lag) for lag in range(1, NEAR)]
+    lagged = [strip] + [
+        joined(own, None if passed is None else passed[0][n], n + 1)
+        for n, own in enumerate(turned)
+    ]
+    near, far = (
+        functools.reduce(
+            lambda total, term: total + term,
+            [tap * series for tap, series in zip(span, lagged)],
+        )
+        for span in (taps[:NEAR], taps[NEAR:])
+    )
+    far = moved(far, NEAR)
+    result = near + joined(far, None if passed is None else passed[1], NEAR)
+    return result, (turned, far)
 
 
 def group_masks(members, width):
     group = lax.broadcasted_iota(jnp.int32, (1, width), 1) % LANES // members
     return [jnp.where(group == g, 1.0, 0.0).astype(BF16) for g in range(LANES // members)]
-
-
-def medium_filter(toeplitz, series, masks):
-    rounded = series.astype(BF16)
-    stacked = jnp.concatenate([rounded * mask for mask in masks], axis=0)
-    return jnp.dot(toeplitz, stacked, preferred_element_type=F32)
 
 
 def mixer_kernel(
@@ -222,7 +218,10 @@
     members, micro, group, width
 ):
     x_refs = rest[: members - 1]
-    out_ref, so_far, first, second, so_far_sem, first_sem, second_sem = rest[members - 1 :]
+    (
+        out_ref, so_far, first, second, coming, projected, keys, values, mixed_grads, rounded,
+        so_far_sem, first_sem, second_sem,
+    ) = rest[members - 1 :]
     rows = out_ref.shape[1]
     channels = out_ref.shape[2]
     length = rows // micro
@@ -232,81 +231,157 @@
     spread = LANES // group * length
     window = width // group * length
     blocks = channels // width
+    pairs = length // (2 * STRIP)
     me = me_ref[0]
     masks = group_masks(group, micro * LANES)
 
-    def copies(n):
+    def sums_copy(n):
+        lanes = pl.ds(pl.multiple_of(n * width, width), width)
+        return pltpu.make_async_copy(so_far_ref.at[:, :, lanes], so_far, so_far_sem)
+
+    def matrix_copies(n):
         slot = n % 2
-        lanes = pl.ds(pl.multiple_of(n * width, width), width)
         wide = pl.ds(pl.multiple_of(n * window, window), window)
         return (
-            pltpu.make_async_copy(
-                so_far_ref.at[:, :, lanes], so_far.at[slot], so_far_sem.at[slot]
-            ),
             pltpu.make_async_copy(first_ref.at[:, wide], first.at[slot], first_sem.at[slot]),
             pltpu.make_async_copy(second_ref.at[:, wide], second.at[slot], second_sem.at[slot]),
         )
 
-    for copy in copies(0):
+    def project(n, i):
+        lanes = pl.ds(pl.multiple_of(n * width, width), width)
+        total = None
+        for k, x_ref in enumerate(x_refs):
+            row = pl.multiple_of(lax.rem(me + k + 1, members) * depth, depth)
+            term = jnp.dot(
+                x_ref[...], w_ref[i, pl.ds(row, depth), lanes], preferred_element_type=F32
+            )
+            total = term if total is None else total + term
+        coming[i] = total
+
+    def take_over():
+        for i in range(3):
+            projected[i] = coming[i] + so_far[i]
+
+    def forward(n, tile, taps):
+        inner = slice(tile * LANES, (tile + 1) * LANES)
+        lanes = pl.ds(pl.multiple_of(n * width + tile * LANES, LANES), LANES)
+        for b in range(micro):
+            place = slice(b * LANES, (b + 1) * LANES)
+            passed = [None] * 3
+            for pair in range(pairs):
+                start = b * length + pair * 2 * STRIP
+                upstream = grad_ref[start : start + 2 * STRIP, lanes].astype(F32)
+                products, backs = [], []
+                for half in range(2):
+                    span = slice(start + half * STRIP, start + (half + 1) * STRIP)
+                    series = [None] * 3
+                    for i in range(3):
+                        series[i], passed[i] = strip_filter(
+                            projected[i, span, inner], taps[i], passed[i], False
+                        )
+                    query, key, value = series
+                    mixed_grad = upstream[half * STRIP : (half + 1) * STRIP] * query
+                    keys[span, inner] = key
+                    values[span, inner] = value
+                    mixed_grads[span, inner] = mixed_grad
+                    products.append(key * value)
+                    backs.append(mixed_grad)
+                held_rows = slice(pair * 2 * STRIP, (pair + 1) * 2 * STRIP)
+                rounded[0, tile, held_rows, place] = jnp.concatenate(products, axis=0).astype(BF16)
+                rounded[1, tile, held_rows, place] = jnp.concatenate(backs, axis=0).astype(BF16)
+
+    def medium(n, tile):
+        places = slice(tile * spread, (tile + 1) * spread)
+        return [
+            jnp.dot(
+                matrix[n % 2, :, places],
+                jnp.concatenate([rounded[turn, tile] * mask for mask in masks], axis=0),
+                preferred_element_type=F32,
+            )
+            for turn, matrix in enumerate((first, second))
+        ]
+
+    def backward(n, tile, taps, mixed, product_grad):
+        inner = slice(tile * LANES, (tile + 1) * LANES)
+        lanes = pl.ds(pl.multiple_of(n * width + tile * LANES, LANES), LANES)
+        skip = jnp.broadcast_to(skip_ref[0:1, lanes], (STRIP, LANES))
+        for b in range(micro):
+            place = slice(b * LANES, (b + 1) * LANES)
+            passed = [None] * 3
+            for pair in reversed(range(pairs)):
+                start = b * length + pair * 2 * STRIP
+                upstream = grad_ref[start : start + 2 * STRIP, lanes].astype(F32)
+                results = [[None] * 2 for _ in range(3)]
+                for half in (1, 0):
+                    span = slice(start + half * STRIP, start + (half + 1) * STRIP)
+                    own = slice(
+                        pair * 2 * STRIP + half * STRIP, pair * 2 * STRIP + (half + 1) * STRIP
+                    )
+                    key, value = keys[span, inner], values[span, inner]
+                    back = product_grad[own, place] + skip * mixed_grads[span, inner]
+                    grads = [
+                        upstream[half * STRIP : (half + 1) * STRIP]
+                        * (mixed[own, place] + skip * (key * value)),
+                        back * value,
+                        back * key,
+                    ]
+                    for i in range(3):
+                        results[i][half], passed[i] = strip_filter(
+                            grads[i], taps[i], passed[i], True
+                        )
+                for i in range(3):
+                    out_ref[i, start : start + 2 * STRIP, lanes] = jnp.concatenate(
+                        results[i], axis=0
+                    ).astype(BF16)
+
+    sums_copy(0).start()
+    for copy in matrix_copies(0):
         copy.start()
+    for i in range(3):
+        project(0, i)
+    sums_copy(0).wait()
+    take_over()
 
     def step(n, carry):
-        slot = n % 2
+        following = jnp.minimum(n + 1, blocks - 1)
 
         @pl.when(n + 1 < blocks)
         def _():
-            for copy in copies(n + 1):
+            for copy in matrix_copies(n + 1):
                 copy.start()
-
-        for copy in copies(n):
+            sums_copy(n + 1).start()
+
+        for copy in matrix_copies(n):
             copy.wait()
-        lanes_all = pl.ds(pl.multiple_of(n * width, width), width)
-        projected = []
-        for i in range(3):
-            total = so_far[slot, i]
-            for k, x_ref in enumerate(x_refs):
-                row = pl.multiple_of(lax.rem(me + k + 1, members) * depth, depth)
-                total = total + jnp.dot(
-                    x_ref[...],
-                    w_ref[i, pl.ds(row, depth), lanes_all],
-                    preferred_element_type=F32,
-                )
-            projected.append(total)
+        taps = []
         for tile in range(width // LANES):
-            inner = slice(tile * LANES, (tile + 1) * LANES)
-            lanes = pl.ds(pl.multiple_of(n * width + tile * LANES, LANES), LANES)
             line = n * (width // LANES) + tile
-            taps = [
-                [taps_ref[pl.ds((j * 3 + i) * tiles + line, 1), :] for j in range(reach)]
+            taps.append([
+                [
+                    jnp.broadcast_to(
+                        taps_ref[pl.ds((j * 3 + i) * tiles + line, 1), :], (STRIP, LANES)
+                    )
+                    for j in range(reach)
+                ]
                 for i in range(3)
-            ]
-            skip = skip_ref[0:1, lanes]
-            places = slice(tile * spread, (tile + 1) * spread)
-            query, key, value, upstream = [], [], [], []
-            for b in range(micro):
-                span = slice(b * length, (b + 1) * length)
-                series = [short_filter(projected[i][span, inner], taps[i], down) for i in range(3)]
-                query.append(series[0])
-                key.append(series[1])
-                value.append(series[2])
-                upstream.append(grad_ref[span, lanes].astype(F32))
-            product = [k * v for k, v in zip(key, value)]
-            mixed = medium_filter(first[slot, :, places], jnp.concatenate(product, axis=1), masks)
-            mixed_grad = [u * q for u, q in zip(upstream, query)]
-            product_grad = medium_filter(
-                second[slot, :, places], jnp.concatenate(mixed_grad, axis=1), masks
-            )
-            for b in range(micro):
-                span = slice(b * length, (b + 1) * length)
-                part = slice(b * LANES, (b + 1) * LANES)
-                back = product_grad[:, part] + skip * mixed_grad[b]
-                grads = [
-                    upstream[b] * (mixed[:, part] + skip * product[b]),
-                    back * value[b],
-                    back * key[b],
-                ]
-                for i in range(3):
-                    out_ref[i, span, lanes] = short_filter(grads[i], taps[i], up).astype(BF16)
+            ])
+        work = [functools.partial(project, following, i) for i in range(3)]
+        for tile in range(width // LANES):
+            if work:
+                work.pop(0)()
+            forward(n, tile, taps[tile])
+        for tile in range(width // LANES):
+            if work:
+                work.pop(0)()
+            backward(n, tile, taps[tile], *medium(n, tile))
+        for late in work:
+            late()
+
+        @pl.when(n + 1 < blocks)
+        def _():
+            sums_copy(n + 1).wait()
+            take_over()
+
         return carry
 
     lax.fori_loop(0, blocks, step, 0)
@@ -331,14 +406,20 @@
         out_specs=IN_VMEM,
         out_shape=pltpu.VMEM((3, rows, channels), BF16),
         scratch_shapes=[
-            pltpu.VMEM((2, 3, rows, width), F32),
+            pltpu.VMEM((3, rows, width), F32),
             pltpu.VMEM((2, length, window), BF16),
             pltpu.VMEM((2, length, window), BF16),
-            pltpu.SemaphoreType.DMA((2,)),
+            pltpu.VMEM((3, rows, width), F32),
+            pltpu.VMEM((3, rows, width), F32),
+            pltpu.VMEM((rows, width), F32),
+            pltpu.VMEM((rows, width), F32),
+            pltpu.VMEM((rows, width), F32),
+            pltpu.VMEM((2, width // LANES, length, micro * LANES), BF16),
+            pltpu.SemaphoreType.DMA,
             pltpu.SemaphoreType.DMA((2,)),
             pltpu.SemaphoreType.DMA((2,)),
         ],
-        compiler_params=params(),
+        compiler_params=params(10 * MIB),
         cost_estimate=cost(6 * rows * depth * channels, 18 * rows * channels),
         name="mixer",
     )(me, held(weights), taps, skip, grad, so_far, first, second, *map(held, others))

time: 91.2 us -> 108 us (1.18)
  local copies, waits for them, and re-layouts: 0 us -> 15.4 us
  Pallas kernels: 68.6 us -> 69.8 us
    unnamed x0 -> x4, local copies, waits for them, and re-layouts: none -> 15.4 us
    pallas_call x1, Pallas kernels: 26.1 us -> 27.4 us  [mixer(): pl.pallas_call(functools.partial(mixer_kernel, members=members, micro=mic...]
  transfers between devices with their start and end apart: 4 -> 4, of which waited for: 3 -> 3; matrix products, arithmetic and copies ran while one was open for 0% -> 0% of each run, Pallas kernels for 37% -> 31%
where the time goes in v4:
time: 108 us; the launch traced here: 107 us
  Pallas kernels  69.8 us (65%)
  local copies, waits for them, and re-layouts  15.4 us (14%)
  waiting for transfers between devices  12.8 us (12%)
  starting transfers between devices  9.28 us (9%)
    pallas_call x1, Pallas kernels, mixer(): pl.pallas_call(functools.partial(mixer_kernel, members=members, micro=mic...  27.4 us
    pallas_call x1, Pallas kernels, load(): pl.pallas_call(functools.partial(load_kernel, members=members, width=widt...  22.2 us
    pallas_call x3, Pallas kernels, input_grad(): pl.pallas_call(functools.partial(input_grad_kernel, first=first, depth=de...  19 us
    unnamed x4, local copies, waits for them, and re-layouts  15.4 us
    ppermute x3, waiting for transfers between devices, local(): pieces.append((first_column, lax.ppermute(share, ('section', 'tp'), pairs)))  12 us
    ppermute x3, starting transfers between devices, local(): pieces.append((first_column, lax.ppermute(share, ('section', 'tp'), pairs)))  7.23 us
  transfers between devices with their start and end apart: 4, of which 3 were waited for; matrix products, arithmetic and copies ran while one was open for 0% of the time, Pallas kernels for 31%

profile of v4, /device:TPU:1, one launch (start us, length us, event | category | flops | bytes accessed | tf_op | source)
XLA Modules:
  0.0 107.4 jit_solution(12568187044017195596)
XLA Ops:
  0.0 2.0 %collective-permute-start = (bf16[256,2048]{1,0:T(8,128)(2,1)}, bf16[256,2048]{1,0:T(8,128)(2,1)S(1)}, u32[]{:S(2)}, u32[]{:S(2)}) collective-permute-start(bf16[256,2048]{1,0:T(8,128)(2,1)} %bitcast.14), channel_id=1, source_target_pairs={{1,0},{0,1},{3,2},{2,3},{5,4},{4,5},{7,6},{6,7},{9,8},{8,9},{11,10... | collective-permute-start | bytes 3145736 | tf_op jit(solution)/shard_map/ppermute | solution.py:512
  2.0 22.2 %load.1 = (bf16[3,4096,2048]{2,1,0:T(8,128)(2,1)S(1)}, f32[3,256,2048]{2,1,0:T(8,128)}, bf16[128,16384]{1,0:T(8,128)(2,1)}, bf16[128,16384]{1,0:T(8,128)(2,1)}) custom-call(s32[1]{0:T(128)} %bitcast.1.me_ref.member_ref, bf16[256,2048]{1,0:T(8,128)(2,1)} %bitcast.15, bf16[3,4096,2048]{2,1,0:T(8,128)(2,1)} %bitcast.10, f32[128,128]{1,0:T(8,128)} %bitcast.17), custom_call_target="tpu_custom_call" | custom-call | flops 6442450944 | bytes 50331648 | tf_op jit(solution)/shard_map/load/pallas_call | solution.py:154
  24.3 0.0 copy-start
  24.3 0.8 collective-permute-done.rest_0_
  25.1 27.4 %mixer.1.conv_ref = bf16[3,256,2048]{2,1,0:T(8,128)(2,1)S(1)} custom-call(s32[1]{0:T(128)} %bitcast.1.me_ref.member_ref, bf16[3,4096,2048]{2,1,0:T(8,128)(2,1)S(1)} %get-tuple-element.9.w_ref, f32[336,128]{1,0:T(8,128)} %bitcast.16, f32[1,2048]{1,0:T(1,128)} %skip_ref.1, bf16[256,2048]{1,0:T(8,128)(2,1)} %bitcast.11, ...), custom_call_target="tpu_custom_call" | custom-call | flops 6442450944 | bytes 9437184 | tf_op jit(solution)/shard_map/mixer/pallas_call | solution.py:399
  52.5 0.0 copy-done
  52.5 0.0 copy-start.1
  52.5 15.4 %copy-done.1 = bf16[3,4096,2048]{2,1,0:T(8,128)(2,1)S(1)} copy-done((bf16[3,4096,2048]{2,1,0:T(8,128)(2,1)S(1)}, bf16[3,4096,2048]{2,1,0:T(8,128)(2,1)}, u32[]{:S(2)}) %copy-start.1) | copy-done | bytes 50331672
  68.0 7.8 %input_grad.3 = bf16[256,2048]{1,0:T(8,128)(2,1)} custom-call(s32[1]{0:T(128)} %bitcast.member_ref, bf16[3,256,2048]{2,1,0:T(8,128)(2,1)S(1)} %mixer.1.conv_ref, bf16[3,4096,2048]{2,1,0:T(8,128)(2,1)S(1)} %copy-done.1), custom_call_target="tpu_custom_call" | custom-call | flops 1 | bytes 1 | tf_op jit(solution)/shard_map/input_grad/pallas_call | solution.py:452
  75.8 2.2 %collective-permute-start.1 = (bf16[256,2048]{1,0:T(8,128)(2,1)}, bf16[256,2048]{1,0:T(8,128)(2,1)S(1)}, u32[]{:S(2)}, u32[]{:S(2)}) collective-permute-start(bf16[256,2048]{1,0:T(8,128)(2,1)} %input_grad.3), channel_id=1, source_target_pairs={{0,31},{1,30},{2,1},{3,0},{4,3},{5,2},{6,5},{7,4},{8,7},{9,6},{10,... | collective-permute-start | bytes 3145736 | tf_op jit(solution)/shard_map/ppermute | solution.py:529
  77.9 5.6 %input_grad.4 = bf16[256,1024]{1,0:T(8,128)(2,1)} custom-call(s32[1]{0:T(128)} %bitcast.1.me_ref.member_ref, bf16[3,256,2048]{2,1,0:T(8,128)(2,1)S(1)} %mixer.1.conv_ref, bf16[3,4096,2048]{2,1,0:T(8,128)(2,1)S(1)} %copy-done.1, bf16[256,2048]{1,0:T(8,128)(2,1)} %bitcast.12), custom_call_target="tpu_custom_call" | custom-call | flops 1 | bytes 1 | tf_op jit(solution)/shard_map/input_grad/pallas_call | solution.py:452
  83.5 3.3 %collective-permute-start.2 = (bf16[256,1024]{1,0:T(8,128)(2,1)}, bf16[256,1024]{1,0:T(8,128)(2,1)S(1)}, u32[]{:S(2)}, u32[]{:S(2)}) collective-permute-start(bf16[256,1024]{1,0:T(8,128)(2,1)} %input_grad.4), channel_id=1, source_target_pairs={{0,30},{1,31},{2,0},{3,1},{4,2},{5,3},{6,4},{7,5},{8,6},{9,7},{10,... | collective-permute-start | bytes 1572872 | tf_op jit(solution)/shard_map/ppermute | solution.py:529
  86.9 5.6 %input_grad.5 = bf16[256,1024]{1,0:T(8,128)(2,1)} custom-call(s32[1]{0:T(128)} %bitcast.1.me_ref.member_ref, bf16[3,256,2048]{2,1,0:T(8,128)(2,1)S(1)} %mixer.1.conv_ref, bf16[3,4096,2048]{2,1,0:T(8,128)(2,1)S(1)} %copy-done.1, bf16[256,2048]{1,0:T(8,128)(2,1)} %bitcast.13), custom_call_target="tpu_custom_call" | custom-call | flops 1 | bytes 1 | tf_op jit(solution)/shard_map/input_grad/pallas_call | solution.py:452
  92.5 1.7 %collective-permute-start.3 = (bf16[256,1024]{1,0:T(8,128)(2,1)}, bf16[256,1024]{1,0:T(8,128)(2,1)S(1)}, u32[]{:S(2)}, u32[]{:S(2)}) collective-permute-start(bf16[256,1024]{1,0:T(8,128)(2,1)} %input_grad.5), channel_id=1, source_target_pairs={{0,30},{1,31},{2,0},{3,1},{4,2},{5,3},{6,4},{7,5},{8,6},{9,7},{10,... | collective-permute-start | bytes 1572872 | tf_op jit(solution)/shard_map/ppermute | solution.py:529
  94.2 4.1 %collective-permute-done.2.refs_1_ = bf16[256,1024]{1,0:T(8,128)(2,1)S(1)} collective-permute-done((bf16[256,1024]{1,0:T(8,128)(2,1)}, bf16[256,1024]{1,0:T(8,128)(2,1)S(1)}, u32[]{:S(2)}, u32[]{:S(2)}) %collective-permute-start.2) | collective-permute-done | bytes 524320 | tf_op jit(solution)/shard_map/ppermute | solution.py:529
  98.3 7.9 %collective-permute-done.3.refs_2_ = bf16[256,1024]{1,0:T(8,128)(2,1)S(1)} collective-permute-done((bf16[256,1024]{1,0:T(8,128)(2,1)}, bf16[256,1024]{1,0:T(8,128)(2,1)S(1)}, u32[]{:S(2)}, u32[]{:S(2)}) %collective-permute-start.3) | collective-permute-done | bytes 524320 | tf_op jit(solution)/shard_map/ppermute | solution.py:529
  106.2 0.0 collective-permute-done.1.refs_0_
  106.2 1.2 %join.1 = bf16[256,2048]{1,0:T(8,128)(2,1)} custom-call(bf16[256,2048]{1,0:T(8,128)(2,1)S(1)} %collective-permute-done.1.refs_0_, bf16[256,1024]{1,0:T(8,128)(2,1)S(1)} %collective-permute-done.2.refs_1_, bf16[256,1024]{1,0:T(8,128)(2,1)S(1)} %collective-permute-done.3.refs_2_), custom_call_target="tpu_custom_call" | custom-call | bytes 3145728 | tf_op jit(solution)/shard_map/join/pallas_call | solution.py:476
Async XLA Ops:
  0.0 25.1 %collective-permute-start = (bf16[256,2048]{1,0:T(8,128)(2,1)}, bf16[256,2048]{1,0:T(8,128)(2,1)S(1)}, u32[]{:S(2)}, u32[]{:S(2)}) collective-permute-start(bf16[256,2048]{1,0:T(8,128)(2,1)} %bitcast.14), channel_id=1, source_target_pairs={{1,0},{0,1},{3,2},{2,3},{5,4},{4,5},{7,6},{6,7},{9,8},{8,9},{11,10... | collective-permute-start | bytes 3145736 | tf_op jit(solution)/shard_map/ppermute | solution.py:512
  24.3 28.2 %copy-start = (bf16[3,4096,2048]{2,1,0:T(8,128)(2,1)}, bf16[3,4096,2048]{2,1,0:T(8,128)(2,1)S(1)}, u32[]{:S(2)}) copy-start(bf16[3,4096,2048]{2,1,0:T(8,128)(2,1)S(1)} %get-tuple-element.9.w_ref) | copy-start | bytes 150994944
  52.5 15.4 %copy-start.1 = (bf16[3,4096,2048]{2,1,0:T(8,128)(2,1)S(1)}, bf16[3,4096,2048]{2,1,0:T(8,128)(2,1)}, u32[]{:S(2)}) copy-start(bf16[3,4096,2048]{2,1,0:T(8,128)(2,1)} %copy-done) | copy-start | bytes 150994944
  75.8 30.4 %collective-permute-start.1 = (bf16[256,2048]{1,0:T(8,128)(2,1)}, bf16[256,2048]{1,0:T(8,128)(2,1)S(1)}, u32[]{:S(2)}, u32[]{:S(2)}) collective-permute-start(bf16[256,2048]{1,0:T(8,128)(2,1)} %input_grad.3), channel_id=1, source_target_pairs={{0,31},{1,30},{2,1},{3,0},{4,3},{5,2},{6,5},{7,4},{8,7},{9,6},{10,... | collective-permute-start | bytes 3145736 | tf_op jit(solution)/shard_map/ppermute | solution.py:529
  83.5 14.7 %collective-permute-start.2 = (bf16[256,1024]{1,0:T(8,128)(2,1)}, bf16[256,1024]{1,0:T(8,128)(2,1)S(1)}, u32[]{:S(2)}, u32[]{:S(2)}) collective-permute-start(bf16[256,1024]{1,0:T(8,128)(2,1)} %input_grad.4), channel_id=1, source_target_pairs={{0,30},{1,31},{2,0},{3,1},{4,2},{5,3},{6,4},{7,5},{8,6},{9,7},{10,... | collective-permute-start | bytes 1572872 | tf_op jit(solution)/shard_map/ppermute | solution.py:529
  92.5 13.7 %collective-permute-start.3 = (bf16[256,1024]{1,0:T(8,128)(2,1)}, bf16[256,1024]{1,0:T(8,128)(2,1)S(1)}, u32[]{:S(2)}, u32[]{:S(2)}) collective-permute-start(bf16[256,1024]{1,0:T(8,128)(2,1)} %input_grad.5), channel_id=1, source_target_pairs={{0,30},{1,31},{2,0},{3,1},{4,2},{5,3},{6,4},{7,5},{8,6},{9,7},{10,... | collective-permute-start | bytes 1572872 | tf_op jit(solution)/shard_map/ppermute | solution.py:529

commit v5 on v4

--- a/solution.py
+++ b/solution.py
@@ -1,4 +1,5 @@
 import functools
+import math
 
 import jax
 import jax.numpy as jnp
@@ -13,6 +14,7 @@
 MIB = 1024 * 1024
 VMEM_LIMIT = 8 * MIB
 SPAN = 256
+SHARE_CUTS = (6, 2)
 AWAY_CUTS = (8,)
 OWN_CUTS = (4, 4)
 
@@ -21,8 +23,8 @@
 ANYWHERE = pl.BlockSpec(memory_space=pl.ANY)
 
 
-def params(limit=VMEM_LIMIT):
-    return pltpu.CompilerParams(vmem_limit_bytes=limit)
+def params():
+    return pltpu.CompilerParams(vmem_limit_bytes=VMEM_LIMIT)
 
 
 def cost(flops, moved):
@@ -177,6 +179,71 @@
     )(me, x, weights, medium)
 
 
+def project_kernel(
+    member_ref, x_ref, w_ref, sums_ref, out_ref, before, after, before_sem, after_sem,
+    *, depth, first, width
+):
+    rows, extent = x_ref.shape
+    blocks = w_ref.shape[2] // width
+    row = pl.multiple_of(member_ref[0] * depth + first, math.gcd(depth, first))
+
+    def lanes(n):
+        return pl.ds(pl.multiple_of(n % blocks * width, width), width)
+
+    def before_copy(n):
+        source = sums_ref.at[n // blocks, :, lanes(n)]
+        return pltpu.make_async_copy(source, before.at[n % 2], before_sem.at[n % 2])
+
+    def after_copy(n):
+        target = out_ref.at[n // blocks, :, lanes(n)]
+        return pltpu.make_async_copy(after.at[n % 2], target, after_sem.at[n % 2])
+
+    before_copy(0).start()
+
+    def step(n, carry):
+        @pl.when(n + 1 < 3 * blocks)
+        def _():
+            before_copy(n + 1).start()
+
+        @pl.when(n >= 2)
+        def _():
+            after_copy(n - 2).wait()
+
+        before_copy(n).wait()
+        after[n % 2] = before[n % 2] + jnp.dot(
+            x_ref[...],
+            w_ref[n // blocks, pl.ds(row, extent), lanes(n)],
+            preferred_element_type=F32,
+        )
+        after_copy(n).start()
+        return carry
+
+    lax.fori_loop(0, 3 * blocks, step, 0)
+    for n in range(3 * blocks - 2, 3 * blocks):
+        after_copy(n).wait()
+
+
+def project(member, x, first, depth, weights, sums):
+    rows, extent = x.shape
+    channels = weights.shape[2]
+    width = min(512, channels)
+    return pl.pallas_call(
+        functools.partial(project_kernel, depth=depth, first=first, width=width),
+        in_specs=[IN_SMEM, IN_VMEM, IN_VMEM, ANYWHERE],
+        out_specs=ANYWHERE,
+        out_shape=jax.ShapeDtypeStruct(sums.shape, F32),
+        scratch_shapes=[
+            pltpu.VMEM((2, rows, width), F32),
+            pltpu.VMEM((2, rows, width), F32),
+            pltpu.SemaphoreType.DMA((2,)),
+            pltpu.SemaphoreType.DMA((2,)),
+        ],
+        compiler_params=params(),
+        cost_estimate=cost(6 * rows * extent * channels, 24 * rows * channels),
+        name="project",
+    )(member, held(x), held(weights), sums)
+
+
 STRIP = 8
 NEAR = 4
 
@@ -214,53 +281,33 @@
 
 
 def mixer_kernel(
-    me_ref, w_ref, taps_ref, skip_ref, grad_ref, so_far_ref, first_ref, second_ref, *rest,
-    members, micro, group, width
+    w_ref, taps_ref, skip_ref, grad_ref, sums_ref, first_ref, second_ref, out_ref,
+    projected, first, second, keys, values, mixed_grads, rounded,
+    sums_sem, first_sem, second_sem, *, micro, group, width
 ):
-    x_refs = rest[: members - 1]
-    (
-        out_ref, so_far, first, second, coming, projected, keys, values, mixed_grads, rounded,
-        so_far_sem, first_sem, second_sem,
-    ) = rest[members - 1 :]
+    del w_ref
     rows = out_ref.shape[1]
     channels = out_ref.shape[2]
     length = rows // micro
-    depth = x_refs[0].shape[1]
     reach = taps_ref.shape[0] * LANES // 3 // channels
     tiles = channels // LANES
     spread = LANES // group * length
     window = width // group * length
     blocks = channels // width
     pairs = length // (2 * STRIP)
-    me = me_ref[0]
     masks = group_masks(group, micro * LANES)
 
-    def sums_copy(n):
+    def copies(n):
+        slot = n % 2
         lanes = pl.ds(pl.multiple_of(n * width, width), width)
-        return pltpu.make_async_copy(so_far_ref.at[:, :, lanes], so_far, so_far_sem)
-
-    def matrix_copies(n):
-        slot = n % 2
         wide = pl.ds(pl.multiple_of(n * window, window), window)
         return (
+            pltpu.make_async_copy(
+                sums_ref.at[:, :, lanes], projected.at[slot], sums_sem.at[slot]
+            ),
             pltpu.make_async_copy(first_ref.at[:, wide], first.at[slot], first_sem.at[slot]),
             pltpu.make_async_copy(second_ref.at[:, wide], second.at[slot], second_sem.at[slot]),
         )
-
-    def project(n, i):
-        lanes = pl.ds(pl.multiple_of(n * width, width), width)
-        total = None
-        for k, x_ref in enumerate(x_refs):
-            row = pl.multiple_of(lax.rem(me + k + 1, members) * depth, depth)
-            term = jnp.dot(
-                x_ref[...], w_ref[i, pl.ds(row, depth), lanes], preferred_element_type=F32
-            )
-            total = term if total is None else total + term
-        coming[i] = total
-
-    def take_over():
-        for i in range(3):
-            projected[i] = coming[i] + so_far[i]
 
     def forward(n, tile, taps):
         inner = slice(tile * LANES, (tile + 1) * LANES)
@@ -277,7 +324,7 @@
                     series = [None] * 3
                     for i in range(3):
                         series[i], passed[i] = strip_filter(
-                            projected[i, span, inner], taps[i], passed[i], False
+                            projected[n % 2, i, span, inner], taps[i], passed[i], False
                         )
                     query, key, value = series
                     mixed_grad = upstream[half * STRIP : (half + 1) * STRIP] * query
@@ -334,24 +381,16 @@
                         results[i], axis=0
                     ).astype(BF16)
 
-    sums_copy(0).start()
-    for copy in matrix_copies(0):
+    for copy in copies(0):
         copy.start()
-    for i in range(3):
-        project(0, i)
-    sums_copy(0).wait()
-    take_over()
 
     def step(n, carry):
-        following = jnp.minimum(n + 1, blocks - 1)
-
         @pl.when(n + 1 < blocks)
         def _():
-            for copy in matrix_copies(n + 1):
+            for copy in copies(n + 1):
                 copy.start()
-            sums_copy(n + 1).start()
-
-        for copy in matrix_copies(n):
+
+        for copy in copies(n):
             copy.wait()
         taps = []
         for tile in range(width // LANES):
@@ -365,64 +404,43 @@
                 ]
                 for i in range(3)
             ])
-        work = [functools.partial(project, following, i) for i in range(3)]
         for tile in range(width // LANES):
-            if work:
-                work.pop(0)()
             forward(n, tile, taps[tile])
         for tile in range(width // LANES):
-            if work:
-                work.pop(0)()
             backward(n, tile, taps[tile], *medium(n, tile))
-        for late in work:
-            late()
-
-        @pl.when(n + 1 < blocks)
-        def _():
-            sums_copy(n + 1).wait()
-            take_over()
-
         return carry
 
     lax.fori_loop(0, blocks, step, 0)
 
 
-def mixer(me, weights, taps, skip, grad, so_far, first, second, others, micro):
-    rows, depth = others[0].shape
-    members = len(others) + 1
-    channels = weights.shape[2]
+def mixer(weights, taps, skip, grad, sums, first, second, micro):
+    rows, channels = sums.shape[1:]
     length = rows // micro
     groups = first.shape[1] // length
     group = channels // groups
     width = min(256, channels)
     window = width // group * length
     return pl.pallas_call(
-        functools.partial(
-            mixer_kernel, members=members, micro=micro, group=group, width=width
-        ),
-        in_specs=[IN_SMEM, IN_VMEM, IN_VMEM, IN_VMEM, IN_VMEM]
-        + [ANYWHERE] * 3
-        + [IN_VMEM] * len(others),
+        functools.partial(mixer_kernel, micro=micro, group=group, width=width),
+        in_specs=[IN_VMEM] * 4 + [ANYWHERE] * 3,
         out_specs=IN_VMEM,
         out_shape=pltpu.VMEM((3, rows, channels), BF16),
         scratch_shapes=[
-            pltpu.VMEM((3, rows, width), F32),
+            pltpu.VMEM((2, 3, rows, width), F32),
             pltpu.VMEM((2, length, window), BF16),
             pltpu.VMEM((2, length, window), BF16),
-            pltpu.VMEM((3, rows, width), F32),
-            pltpu.VMEM((3, rows, width), F32),
             pltpu.VMEM((rows, width), F32),
             pltpu.VMEM((rows, width), F32),
             pltpu.VMEM((rows, width), F32),
             pltpu.VMEM((2, width // LANES, length, micro * LANES), BF16),
-            pltpu.SemaphoreType.DMA,
+            pltpu.SemaphoreType.DMA((2,)),
             pltpu.SemaphoreType.DMA((2,)),
             pltpu.SemaphoreType.DMA((2,)),
         ],
-        compiler_params=params(10 * MIB),
-        cost_estimate=cost(6 * rows * depth * channels, 18 * rows * channels),
+        compiler_params=params(),
+        cost_estimate=cost(0, 18 * rows * channels),
         name="mixer",
-    )(me, held(weights), taps, skip, grad, so_far, first, second, *map(held, others))
+    )(held(weights), taps, skip, grad, sums, first, second)
 
 
 def input_grad_kernel(member_ref, conv_ref, w_ref, *rest, first, depth, width):
@@ -509,11 +527,14 @@
     others = []
     for k in range(1, members):
         pairs = [((m + k) % members, m) for m in range(members)]
-        others.append(lax.ppermute(x, "tp", pairs))
-    weights, so_far, first, second = load(owner(0), x, weights, medium_taps[0], members)
+        for first_column, extent in cuts_of(SHARE_CUTS, depth):
+            sent = x[:, first_column : first_column + extent]
+            others.append((k, first_column, lax.ppermute(sent, "tp", pairs)))
+    weights, sums, first, second = load(owner(0), x, weights, medium_taps[0], members)
+    for k, first_column, share in others:
+        sums = project(owner(k), share, first_column, depth, weights, sums)
     conv = mixer(
-        owner(0), weights, short_taps.reshape(-1, LANES), skip_weight, grad, so_far, first,
-        second, others, micro,
+        weights, short_taps.reshape(-1, LANES), skip_weight, grad, sums, first, second, micro
     )
     pieces = []
     for k in list(range(1, members)) + [0]:

time: 108 us -> 107 us (level)
  local copies, waits for them, and re-layouts: 15.4 us -> 2.15 us
  Pallas kernels: 69.8 us -> 82.4 us
    unnamed x4 -> x0, local copies, waits for them, and re-layouts: 15.4 us -> none
    pallas_call x1 -> x3, Pallas kernels: 27.4 us -> 39.9 us  [the longest x2 22.8 us: project(): pl.pallas_call(functools.partial(project_kernel, depth=depth, first=first...]
    slice x0 -> x2, local copies, waits for them, and re-layouts: none -> 2.15 us  [local(): sent = x[:, first_column:first_column + extent]]
    ppermute x1 -> x2, starting transfers between devices: 2.04 us -> 2.19 us  [local(): others.append((k, first_column, lax.ppermute(sent, 'tp', pairs)))]
  transfers between devices with their start and end apart: 4 -> 5, of which waited for: 3 -> 2; matrix products, arithmetic and copies ran while one was open for 0% -> 1% of each run, Pallas kernels for 31% -> 43%
where the time goes in v5:
time: 107 us; the launch traced here: 106 us
  Pallas kernels  82.4 us (77%)
  waiting for transfers between devices  12.2 us (11%)
  starting transfers between devices  9.38 us (9%)
  local copies, waits for them, and re-layouts  2.15 us (2%)
    pallas_call x2, Pallas kernels, project(): pl.pallas_call(functools.partial(project_kernel, depth=depth, first=first...  22.8 us
    pallas_call x1, Pallas kernels, load(): pl.pallas_call(functools.partial(load_kernel, members=members, width=widt...  22.3 us
    pallas_call x3, Pallas kernels, input_grad(): pl.pallas_call(functools.partial(input_grad_kernel, first=first, depth=de...  19 us
    pallas_call x1, Pallas kernels, mixer(): pl.pallas_call(functools.partial(mixer_kernel, micro=micro, group=group,...  17.1 us
    ppermute x3, waiting for transfers between devices, local(): pieces.append((first_column, lax.ppermute(share, ('section', 'tp'), pairs)))  12.2 us
    ppermute x3, starting transfers between devices, local(): pieces.append((first_column, lax.ppermute(share, ('section', 'tp'), pairs)))  7.19 us
    ppermute x2, starting transfers between devices, local(): others.append((k, first_column, lax.ppermute(sent, 'tp', pairs)))  2.19 us
    slice x2, local copies, waits for them, and re-layouts, local(): sent = x[:, first_column:first_column + extent]  2.15 us
  transfers between devices with their start and end apart: 5, of which 2 were waited for; matrix products, arithmetic and copies ran while one was open for 1% of the time, Pallas kernels for 43%

profile of v5, /device:TPU:1, one launch (start us, length us, event | category | flops | bytes accessed | tf_op | source)
XLA Modules:
  0.0 106.2 jit_solution(6815463001925850400)
XLA Ops:
  0.0 1.2 %slice.9 = bf16[256,1536]{1,0:T(8,128)(2,1)S(1)} slice(bf16[256,2048]{1,0:T(8,128)(2,1)} %bitcast.14), slice={[0:256], [0:1536]} | slice | bytes 1572864 | tf_op jit(solution)/shard_map/slice | solution.py:531
  1.2 2.1 %collective-permute-start.1 = (bf16[256,1536]{1,0:T(8,128)(2,1)S(1)}, bf16[256,1536]{1,0:T(8,128)(2,1)S(1)}, u32[]{:S(2)}, u32[]{:S(2)}) collective-permute-start(bf16[256,1536]{1,0:T(8,128)(2,1)S(1)} %slice.9), channel_id=1, source_target_pairs={{1,0},{0,1},{3,2},{2,3},{5,4},{4,5},{7,6},{6,7},{9,8},{8,9},{11,10... | collective-permute-start | bytes 2359304 | tf_op jit(solution)/shard_map/ppermute | solution.py:532
  3.3 1.0 slice.8
  4.3 0.1 collective-permute-start
  4.3 22.3 %load.1 = (bf16[3,4096,2048]{2,1,0:T(8,128)(2,1)S(1)}, f32[3,256,2048]{2,1,0:T(8,128)}, bf16[128,16384]{1,0:T(8,128)(2,1)}, bf16[128,16384]{1,0:T(8,128)(2,1)}) custom-call(s32[1]{0:T(128)} %bitcast.1.me_ref.member_ref, bf16[256,2048]{1,0:T(8,128)(2,1)} %bitcast.16, bf16[3,4096,2048]{2,1,0:T(8,128)(2,1)} %bitcast.10, f32[128,128]{1,0:T(8,128)} %bitcast.18), custom_call_target="tpu_custom_call" | custom-call | flops 6442450944 | bytes 50331648 | tf_op jit(solution)/shard_map/load/pallas_call | solution.py:156
  26.6 0.0 collective-permute-done.1.x_ref
  26.6 12.3 %project.2.sums_ref = f32[3,256,2048]{2,1,0:T(8,128)} custom-call(s32[1]{0:T(128)} %bitcast.member_ref, bf16[256,1536]{1,0:T(8,128)(2,1)S(1)} %collective-permute-done.1.x_ref, bf16[3,4096,2048]{2,1,0:T(8,128)(2,1)S(1)} %get-tuple-element.9.w_ref, f32[3,256,2048]{2,1,0:T(8,128)} %get-tuple-element.10.sums_ref), custom_call_target="tpu_custom_call" | custom-call | flops 4831838208 | bytes 12582912 | tf_op jit(solution)/shard_map/project/pallas_call | solution.py:230
  39.0 0.0 collective-permute-done.x_ref
  39.0 10.4 %project.3.sums_ref = f32[3,256,2048]{2,1,0:T(8,128)} custom-call(s32[1]{0:T(128)} %bitcast.member_ref, bf16[256,512]{1,0:T(8,128)(2,1)S(1)} %collective-permute-done.x_ref, bf16[3,4096,2048]{2,1,0:T(8,128)(2,1)S(1)} %get-tuple-element.9.w_ref, f32[3,256,2048]{2,1,0:T(8,128)} %project.2.sums_ref), custom_call_target="tpu_custom_call" | custom-call | flops 1610612736 | bytes 12582912 | tf_op jit(solution)/shard_map/project/pallas_call | solution.py:230
  49.4 17.1 %mixer.1.conv_ref = bf16[3,256,2048]{2,1,0:T(8,128)(2,1)S(1)} custom-call(bf16[3,4096,2048]{2,1,0:T(8,128)(2,1)S(1)} %get-tuple-element.9.w_ref, f32[336,128]{1,0:T(8,128)} %bitcast.17, f32[1,2048]{1,0:T(1,128)} %skip_ref.1, bf16[256,2048]{1,0:T(8,128)(2,1)} %bitcast.11, f32[3,256,2048]{2,1,0:T(8,128)} %project.3.sums_ref, ...), custom_call_target="tpu_custom_call" | custom-call | bytes 9437184 | tf_op jit(solution)/shard_map/mixer/pallas_call | solution.py:423
  66.5 7.8 %input_grad.3 = bf16[256,2048]{1,0:T(8,128)(2,1)} custom-call(s32[1]{0:T(128)} %bitcast.member_ref, bf16[3,256,2048]{2,1,0:T(8,128)(2,1)S(1)} %mixer.1.conv_ref, bf16[3,4096,2048]{2,1,0:T(8,128)(2,1)S(1)} %get-tuple-element.9.w_ref), custom_call_target="tpu_custom_call" | custom-call | flops 1 | bytes 1 | tf_op jit(solution)/shard_map/input_grad/pallas_call | solution.py:470
  74.3 2.5 %collective-permute-start.2 = (bf16[256,2048]{1,0:T(8,128)(2,1)}, bf16[256,2048]{1,0:T(8,128)(2,1)S(1)}, u32[]{:S(2)}, u32[]{:S(2)}) collective-permute-start(bf16[256,2048]{1,0:T(8,128)(2,1)} %input_grad.3), channel_id=1, source_target_pairs={{0,31},{1,30},{2,1},{3,0},{4,3},{5,2},{6,5},{7,4},{8,7},{9,6},{10,... | collective-permute-start | bytes 3145736 | tf_op jit(solution)/shard_map/ppermute | solution.py:550
  76.9 5.6 %input_grad.5 = bf16[256,1024]{1,0:T(8,128)(2,1)} custom-call(s32[1]{0:T(128)} %bitcast.1.me_ref.member_ref, bf16[3,256,2048]{2,1,0:T(8,128)(2,1)S(1)} %mixer.1.conv_ref, bf16[3,4096,2048]{2,1,0:T(8,128)(2,1)S(1)} %get-tuple-element.9.w_ref, bf16[256,2048]{1,0:T(8,128)(2,1)} %bitcast.12), custom_call_target="tpu_custom_call" | custom-call | flops 1 | bytes 1 | tf_op jit(solution)/shard_map/input_grad/pallas_call | solution.py:470
  82.5 3.3 %collective-permute-start.4 = (bf16[256,1024]{1,0:T(8,128)(2,1)}, bf16[256,1024]{1,0:T(8,128)(2,1)S(1)}, u32[]{:S(2)}, u32[]{:S(2)}) collective-permute-start(bf16[256,1024]{1,0:T(8,128)(2,1)} %input_grad.5), channel_id=1, source_target_pairs={{0,30},{1,31},{2,0},{3,1},{4,2},{5,3},{6,4},{7,5},{8,6},{9,7},{10,... | collective-permute-start | bytes 1572872 | tf_op jit(solution)/shard_map/ppermute | solution.py:550
  85.7 5.6 %input_grad.4 = bf16[256,1024]{1,0:T(8,128)(2,1)} custom-call(s32[1]{0:T(128)} %bitcast.1.me_ref.member_ref, bf16[3,256,2048]{2,1,0:T(8,128)(2,1)S(1)} %mixer.1.conv_ref, bf16[3,4096,2048]{2,1,0:T(8,128)(2,1)S(1)} %get-tuple-element.9.w_ref, bf16[256,2048]{1,0:T(8,128)(2,1)} %bitcast.13), custom_call_target="tpu_custom_call" | custom-call | flops 1 | bytes 1 | tf_op jit(solution)/shard_map/input_grad/pallas_call | solution.py:470
  91.3 1.4 %collective-permute-start.3 = (bf16[256,1024]{1,0:T(8,128)(2,1)}, bf16[256,1024]{1,0:T(8,128)(2,1)S(1)}, u32[]{:S(2)}, u32[]{:S(2)}) collective-permute-start(bf16[256,1024]{1,0:T(8,128)(2,1)} %input_grad.4), channel_id=1, source_target_pairs={{0,30},{1,31},{2,0},{3,1},{4,2},{5,3},{6,4},{7,5},{8,6},{9,7},{10,... | collective-permute-start | bytes 1572872 | tf_op jit(solution)/shard_map/ppermute | solution.py:550
  92.7 4.5 %collective-permute-done.4.refs_2_ = bf16[256,1024]{1,0:T(8,128)(2,1)S(1)} collective-permute-done((bf16[256,1024]{1,0:T(8,128)(2,1)}, bf16[256,1024]{1,0:T(8,128)(2,1)S(1)}, u32[]{:S(2)}, u32[]{:S(2)}) %collective-permute-start.4) | collective-permute-done | bytes 524320 | tf_op jit(solution)/shard_map/ppermute | solution.py:550
  97.2 7.7 %collective-permute-done.3.refs_1_ = bf16[256,1024]{1,0:T(8,128)(2,1)S(1)} collective-permute-done((bf16[256,1024]{1,0:T(8,128)(2,1)}, bf16[256,1024]{1,0:T(8,128)(2,1)S(1)}, u32[]{:S(2)}, u32[]{:S(2)}) %collective-permute-start.3) | collective-permute-done | bytes 524320 | tf_op jit(solution)/shard_map/ppermute | solution.py:550
  104.9 0.0 collective-permute-done.2.refs_0_
  104.9 1.2 %join.1 = bf16[256,2048]{1,0:T(8,128)(2,1)} custom-call(bf16[256,2048]{1,0:T(8,128)(2,1)S(1)} %collective-permute-done.2.refs_0_, bf16[256,1024]{1,0:T(8,128)(2,1)S(1)} %collective-permute-done.3.refs_1_, bf16[256,1024]{1,0:T(8,128)(2,1)S(1)} %collective-permute-done.4.refs_2_), custom_call_target="tpu_custom_call" | custom-call | bytes 3145728 | tf_op jit(solution)/shard_map/join/pallas_call | solution.py:494
Async XLA Ops:
  1.2 25.4 %collective-permute-start.1 = (bf16[256,1536]{1,0:T(8,128)(2,1)S(1)}, bf16[256,1536]{1,0:T(8,128)(2,1)S(1)}, u32[]{:S(2)}, u32[]{:S(2)}) collective-permute-start(bf16[256,1536]{1,0:T(8,128)(2,1)S(1)} %slice.9), channel_id=1, source_target_pairs={{1,0},{0,1},{3,2},{2,3},{5,4},{4,5},{7,6},{6,7},{9,8},{8,9},{11,10... | collective-permute-start | bytes 2359304 | tf_op jit(solution)/shard_map/ppermute | solution.py:532
  4.3 34.7 %collective-permute-start = (bf16[256,512]{1,0:T(8,128)(2,1)S(1)}, bf16[256,512]{1,0:T(8,128)(2,1)S(1)}, u32[]{:S(2)}, u32[]{:S(2)}) collective-permute-start(bf16[256,512]{1,0:T(8,128)(2,1)S(1)} %slice.8), channel_id=1, source_target_pairs={{1,0},{0,1},{3,2},{2,3},{5,4},{4,5},{7,6},{6,7},{9,8},{8,9},{11,10... | collective-permute-start | bytes 786440 | tf_op jit(solution)/shard_map/ppermute | solution.py:532
  74.3 30.6 %collective-permute-start.2 = (bf16[256,2048]{1,0:T(8,128)(2,1)}, bf16[256,2048]{1,0:T(8,128)(2,1)S(1)}, u32[]{:S(2)}, u32[]{:S(2)}) collective-permute-start(bf16[256,2048]{1,0:T(8,128)(2,1)} %input_grad.3), channel_id=1, source_target_pairs={{0,31},{1,30},{2,1},{3,0},{4,3},{5,2},{6,5},{7,4},{8,7},{9,6},{10,... | collective-permute-start | bytes 3145736 | tf_op jit(solution)/shard_map/ppermute | solution.py:550
  82.5 14.7 %collective-permute-start.4 = (bf16[256,1024]{1,0:T(8,128)(2,1)}, bf16[256,1024]{1,0:T(8,128)(2,1)S(1)}, u32[]{:S(2)}, u32[]{:S(2)}) collective-permute-start(bf16[256,1024]{1,0:T(8,128)(2,1)} %input_grad.5), channel_id=1, source_target_pairs={{0,30},{1,31},{2,0},{3,1},{4,2},{5,3},{6,4},{7,5},{8,6},{9,7},{10,... | collective-permute-start | bytes 1572872 | tf_op jit(solution)/shard_map/ppermute | solution.py:550
  91.3 13.6 %collective-permute-start.3 = (bf16[256,1024]{1,0:T(8,128)(2,1)}, bf16[256,1024]{1,0:T(8,128)(2,1)S(1)}, u32[]{:S(2)}, u32[]{:S(2)}) collective-permute-start(bf16[256,1024]{1,0:T(8,128)(2,1)} %input_grad.4), channel_id=1, source_target_pairs={{0,30},{1,31},{2,0},{3,1},{4,2},{5,3},{6,4},{7,5},{8,6},{9,7},{10,... | collective-permute-start | bytes 1572872 | tf_op jit(solution)/shard_map/ppermute | solution.py:550

commit v6 on v4

--- a/solution.py
+++ b/solution.py
@@ -13,7 +13,7 @@
 MIB = 1024 * 1024
 VMEM_LIMIT = 8 * MIB
 SPAN = 256
-AWAY_CUTS = (8,)
+AWAY_CUTS = (2, 6)
 OWN_CUTS = (4, 4)
 
 IN_VMEM = pl.BlockSpec(memory_space=pltpu.VMEM)
@@ -21,8 +21,8 @@
 ANYWHERE = pl.BlockSpec(memory_space=pl.ANY)
 
 
-def params(limit=VMEM_LIMIT):
-    return pltpu.CompilerParams(vmem_limit_bytes=limit)
+def params():
+    return pltpu.CompilerParams(vmem_limit_bytes=VMEM_LIMIT)
 
 
 def cost(flops, moved):
@@ -178,34 +178,15 @@
 
 
 STRIP = 8
-NEAR = 4
-
-
-def strip_filter(strip, taps, passed, back):
-    row = lax.broadcasted_iota(jnp.int32, strip.shape, 0)
-
-    def moved(series, lag):
-        return pltpu.roll(series, STRIP - lag if back else lag, 0)
-
-    def joined(own, before, lag):
-        outside = row >= STRIP - lag if back else row < lag
-        return jnp.where(outside, 0.0 if before is None else before, own)
-
-    turned = [moved(strip, lag) for lag in range(1, NEAR)]
-    lagged = [strip] + [
-        joined(own, None if passed is None else passed[0][n], n + 1)
-        for n, own in enumerate(turned)
-    ]
-    near, far = (
-        functools.reduce(
-            lambda total, term: total + term,
-            [tap * series for tap, series in zip(span, lagged)],
-        )
-        for span in (taps[:NEAR], taps[NEAR:])
-    )
-    far = moved(far, NEAR)
-    result = near + joined(far, None if passed is None else passed[1], NEAR)
-    return result, (turned, far)
+
+
+def strip_filter(scratch, i, start, taps, micro, back):
+    total = None
+    for lag, tap in enumerate(taps):
+        first = start + micro * (lag if back else -lag)
+        term = tap * scratch[i, pl.ds(first, STRIP, stride=micro), :]
+        total = term if total is None else total + term
+    return total
 
 
 def group_masks(members, width):
@@ -219,82 +200,92 @@
 ):
     x_refs = rest[: members - 1]
     (
-        out_ref, so_far, first, second, coming, projected, keys, values, mixed_grads, rounded,
-        so_far_sem, first_sem, second_sem,
+        out_ref, so_far, grads, first, second, lagged, keys, values, mixed_grads, rounded,
+        so_far_sem, grads_sem, first_sem, second_sem,
     ) = rest[members - 1 :]
-    rows = out_ref.shape[1]
-    channels = out_ref.shape[2]
+    rows, channels = out_ref.shape[1:]
+    depth = x_refs[0].shape[1]
+    me = me_ref[0]
     length = rows // micro
-    depth = x_refs[0].shape[1]
     reach = taps_ref.shape[0] * LANES // 3 // channels
     tiles = channels // LANES
     spread = LANES // group * length
     window = width // group * length
     blocks = channels // width
     pairs = length // (2 * STRIP)
-    me = me_ref[0]
+    margin = micro * STRIP
     masks = group_masks(group, micro * LANES)
 
-    def sums_copy(n):
+    def block_copies(n):
+        slot = n % 2
         lanes = pl.ds(pl.multiple_of(n * width, width), width)
-        return pltpu.make_async_copy(so_far_ref.at[:, :, lanes], so_far, so_far_sem)
+        return (
+            pltpu.make_async_copy(
+                so_far_ref.at[:, :, lanes], so_far.at[slot], so_far_sem.at[slot]
+            ),
+            pltpu.make_async_copy(grad_ref.at[:, lanes], grads.at[slot], grads_sem.at[slot]),
+        )
 
     def matrix_copies(n):
-        slot = n % 2
         wide = pl.ds(pl.multiple_of(n * window, window), window)
         return (
-            pltpu.make_async_copy(first_ref.at[:, wide], first.at[slot], first_sem.at[slot]),
-            pltpu.make_async_copy(second_ref.at[:, wide], second.at[slot], second_sem.at[slot]),
-        )
-
-    def project(n, i):
+            pltpu.make_async_copy(first_ref.at[:, wide], first, first_sem),
+            pltpu.make_async_copy(second_ref.at[:, wide], second, second_sem),
+        )
+
+    def lanes_of(n, tile):
+        return pl.ds(pl.multiple_of(n * width + tile * LANES, LANES), LANES)
+
+    def project(n):
         lanes = pl.ds(pl.multiple_of(n * width, width), width)
-        total = None
-        for k, x_ref in enumerate(x_refs):
-            row = pl.multiple_of(lax.rem(me + k + 1, members) * depth, depth)
-            term = jnp.dot(
-                x_ref[...], w_ref[i, pl.ds(row, depth), lanes], preferred_element_type=F32
-            )
-            total = term if total is None else total + term
-        coming[i] = total
-
-    def take_over():
         for i in range(3):
-            projected[i] = coming[i] + so_far[i]
+            total = so_far[n % 2, i]
+            for k, x_ref in enumerate(x_refs):
+                row = pl.multiple_of(lax.rem(me + k + 1, members) * depth, depth)
+                total = total + jnp.dot(
+                    x_ref[...], w_ref[i, pl.ds(row, depth), lanes], preferred_element_type=F32
+                )
+            for tile in range(width // LANES):
+                for b in range(micro):
+                    for start in range(0, length, STRIP):
+                        first_row = margin + micro * start + b
+                        lagged[tile, i, pl.ds(first_row, STRIP, stride=micro), :] = total[
+                            b * length + start : b * length + start + STRIP,
+                            tile * LANES : (tile + 1) * LANES,
+                        ]
 
     def forward(n, tile, taps):
         inner = slice(tile * LANES, (tile + 1) * LANES)
-        lanes = pl.ds(pl.multiple_of(n * width + tile * LANES, LANES), LANES)
+        scratch = lagged.at[tile]
         for b in range(micro):
             place = slice(b * LANES, (b + 1) * LANES)
-            passed = [None] * 3
             for pair in range(pairs):
-                start = b * length + pair * 2 * STRIP
-                upstream = grad_ref[start : start + 2 * STRIP, lanes].astype(F32)
+                start = pair * 2 * STRIP
+                span = slice(b * length + start, b * length + start + 2 * STRIP)
+                upstream = grads[n % 2, span, inner].astype(F32)
                 products, backs = [], []
                 for half in range(2):
-                    span = slice(start + half * STRIP, start + (half + 1) * STRIP)
-                    series = [None] * 3
-                    for i in range(3):
-                        series[i], passed[i] = strip_filter(
-                            projected[i, span, inner], taps[i], passed[i], False
-                        )
-                    query, key, value = series
+                    time = start + half * STRIP
+                    query, key, value = (
+                        strip_filter(scratch, i, margin + micro * time + b, taps[i], micro, False)
+                        for i in range(3)
+                    )
                     mixed_grad = upstream[half * STRIP : (half + 1) * STRIP] * query
-                    keys[span, inner] = key
-                    values[span, inner] = value
-                    mixed_grads[span, inner] = mixed_grad
+                    own = slice(b * length + time, b * length + time + STRIP)
+                    keys[own, inner] = key
+                    values[own, inner] = value
+                    mixed_grads[own, inner] = mixed_grad
                     products.append(key * value)
                     backs.append(mixed_grad)
-                held_rows = slice(pair * 2 * STRIP, (pair + 1) * 2 * STRIP)
+                held_rows = slice(start, start + 2 * STRIP)
                 rounded[0, tile, held_rows, place] = jnp.concatenate(products, axis=0).astype(BF16)
                 rounded[1, tile, held_rows, place] = jnp.concatenate(backs, axis=0).astype(BF16)
 
-    def medium(n, tile):
+    def medium(tile):
         places = slice(tile * spread, (tile + 1) * spread)
         return [
             jnp.dot(
-                matrix[n % 2, :, places],
+                matrix[:, places],
                 jnp.concatenate([rounded[turn, tile] * mask for mask in masks], axis=0),
                 preferred_element_type=F32,
             )
@@ -303,55 +294,57 @@
 
     def backward(n, tile, taps, mixed, product_grad):
         inner = slice(tile * LANES, (tile + 1) * LANES)
-        lanes = pl.ds(pl.multiple_of(n * width + tile * LANES, LANES), LANES)
+        lanes = lanes_of(n, tile)
+        scratch = lagged.at[tile]
         skip = jnp.broadcast_to(skip_ref[0:1, lanes], (STRIP, LANES))
         for b in range(micro):
             place = slice(b * LANES, (b + 1) * LANES)
-            passed = [None] * 3
-            for pair in reversed(range(pairs)):
-                start = b * length + pair * 2 * STRIP
-                upstream = grad_ref[start : start + 2 * STRIP, lanes].astype(F32)
-                results = [[None] * 2 for _ in range(3)]
-                for half in (1, 0):
-                    span = slice(start + half * STRIP, start + (half + 1) * STRIP)
-                    own = slice(
-                        pair * 2 * STRIP + half * STRIP, pair * 2 * STRIP + (half + 1) * STRIP
-                    )
-                    key, value = keys[span, inner], values[span, inner]
-                    back = product_grad[own, place] + skip * mixed_grads[span, inner]
-                    grads = [
+            for pair in range(pairs):
+                start = pair * 2 * STRIP
+                span = slice(b * length + start, b * length + start + 2 * STRIP)
+                upstream = grads[n % 2, span, inner].astype(F32)
+                for half in range(2):
+                    time = start + half * STRIP
+                    own = slice(b * length + time, b * length + time + STRIP)
+                    here = slice(time, time + STRIP)
+                    key, value = keys[own, inner], values[own, inner]
+                    back = product_grad[here, place] + skip * mixed_grads[own, inner]
+                    streams = (
                         upstream[half * STRIP : (half + 1) * STRIP]
-                        * (mixed[own, place] + skip * (key * value)),
+                        * (mixed[here, place] + skip * (key * value)),
                         back * value,
                         back * key,
+                    )
+                    for i in range(3):
+                        first_row = margin + micro * time + b
+                        scratch[i, pl.ds(first_row, STRIP, stride=micro), :] = streams[i]
+        for b in range(micro):
+            for start in range(0, length, 2 * STRIP):
+                span = slice(b * length + start, b * length + start + 2 * STRIP)
+                for i in range(3):
+                    strips = [
+                        strip_filter(
+                            scratch, i, margin + micro * (start + half) + b, taps[i], micro, True
+                        )
+                        for half in (0, STRIP)
                     ]
-                    for i in range(3):
-                        results[i][half], passed[i] = strip_filter(
-                            grads[i], taps[i], passed[i], True
-                        )
-                for i in range(3):
-                    out_ref[i, start : start + 2 * STRIP, lanes] = jnp.concatenate(
-                        results[i], axis=0
-                    ).astype(BF16)
-
-    sums_copy(0).start()
-    for copy in matrix_copies(0):
+                    out_ref[i, span, lanes] = jnp.concatenate(strips, axis=0).astype(BF16)
+
+    for copy in block_copies(0):
         copy.start()
-    for i in range(3):
-        project(0, i)
-    sums_copy(0).wait()
-    take_over()
+    zeros = jnp.zeros((width // LANES, 3, margin, LANES), F32)
+    lagged[:, :, :margin, :] = zeros
+    lagged[:, :, margin + micro * length :, :] = zeros
 
     def step(n, carry):
-        following = jnp.minimum(n + 1, blocks - 1)
-
         @pl.when(n + 1 < blocks)
         def _():
-            for copy in matrix_copies(n + 1):
+            for copy in block_copies(n + 1):
                 copy.start()
-            sums_copy(n + 1).start()
 
         for copy in matrix_copies(n):
+            copy.start()
+        for copy in block_copies(n):
             copy.wait()
         taps = []
         for tile in range(width // LANES):
@@ -365,67 +358,56 @@
                 ]
                 for i in range(3)
             ])
-        work = [functools.partial(project, following, i) for i in range(3)]
+        project(n)
         for tile in range(width // LANES):
-            if work:
-                work.pop(0)()
             forward(n, tile, taps[tile])
+        for copy in matrix_copies(n):
+            copy.wait()
         for tile in range(width // LANES):
-            if work:
-                work.pop(0)()
-            backward(n, tile, taps[tile], *medium(n, tile))
-        for late in work:
-            late()
-
-        @pl.when(n + 1 < blocks)
-        def _():
-            sums_copy(n + 1).wait()
-            take_over()
-
+            backward(n, tile, taps[tile], *medium(tile))
         return carry
 
     lax.fori_loop(0, blocks, step, 0)
 
 
 def mixer(me, weights, taps, skip, grad, so_far, first, second, others, micro):
-    rows, depth = others[0].shape
+    rows, channels = so_far.shape[1:]
     members = len(others) + 1
-    channels = weights.shape[2]
     length = rows // micro
     groups = first.shape[1] // length
     group = channels // groups
     width = min(256, channels)
     window = width // group * length
+    tiles = width // LANES
     return pl.pallas_call(
         functools.partial(
             mixer_kernel, members=members, micro=micro, group=group, width=width
         ),
-        in_specs=[IN_SMEM, IN_VMEM, IN_VMEM, IN_VMEM, IN_VMEM]
-        + [ANYWHERE] * 3
-        + [IN_VMEM] * len(others),
+        in_specs=[IN_SMEM] + [IN_VMEM] * 3 + [ANYWHERE] * 4 + [IN_VMEM] * len(others),
         out_specs=IN_VMEM,
-        out_shape=pltpu.VMEM((3, rows, channels), BF16),
+        out_shape=pltpu.VMEM(so_far.shape, BF16),
         scratch_shapes=[
-            pltpu.VMEM((3, rows, width), F32),
-            pltpu.VMEM((2, length, window), BF16),
-            pltpu.VMEM((2, length, window), BF16),
-            pltpu.VMEM((3, rows, width), F32),
-            pltpu.VMEM((3, rows, width), F32),
+            pltpu.VMEM((2, 3, rows, width), F32),
+            pltpu.VMEM((2, rows, width), BF16),
+            pltpu.VMEM((length, window), BF16),
+            pltpu.VMEM((length, window), BF16),
+            pltpu.VMEM((tiles, 3, micro * (length + 2 * STRIP), LANES), F32),
             pltpu.VMEM((rows, width), F32),
             pltpu.VMEM((rows, width), F32),
             pltpu.VMEM((rows, width), F32),
-            pltpu.VMEM((2, width // LANES, length, micro * LANES), BF16),
-            pltpu.SemaphoreType.DMA,
+            pltpu.VMEM((2, tiles, length, micro * LANES), BF16),
             pltpu.SemaphoreType.DMA((2,)),
             pltpu.SemaphoreType.DMA((2,)),
+            pltpu.SemaphoreType.DMA,
+            pltpu.SemaphoreType.DMA,
         ],
-        compiler_params=params(10 * MIB),
-        cost_estimate=cost(6 * rows * depth * channels, 18 * rows * channels),
+        compiler_params=params(),
+        cost_estimate=cost(0, 18 * rows * channels),
         name="mixer",
     )(me, held(weights), taps, skip, grad, so_far, first, second, *map(held, others))
 
 
-def input_grad_kernel(member_ref, conv_ref, w_ref, *rest, first, depth, width):
+def input_grad_kernel(member_ref, conv_ref, w_ref, *rest, first, depth, width, with_grad):
     out_ref = rest[-1]
     start = member_ref[0] * depth + first
     for step in range(out_ref.shape[1] // width):
@@ -441,23 +423,25 @@
             )
             total = term if total is None else total + term
         total = total.T
-        if len(rest) > 1:
+        if with_grad:
             total = total + rest[0][:, first + step * width : first + (step + 1) * width].astype(F32)
         out_ref[:, place] = total.astype(BF16)
 
 
-def input_grad(conv, weights, member, first, extent, depth, grad=None):
+def input_grad(conv, weights, member, first, extent, depth, grad=None, after=()):
     rows = conv.shape[1]
     operands = [conv, weights] + ([] if grad is None else [grad])
     return pl.pallas_call(
-        functools.partial(input_grad_kernel, first=first, depth=depth, width=SPAN),
-        in_specs=[IN_SMEM] + [IN_VMEM] * len(operands),
+        functools.partial(
+            input_grad_kernel, first=first, depth=depth, width=SPAN, with_grad=grad is not None
+        ),
+        in_specs=[IN_SMEM] + [IN_VMEM] * (len(operands) + len(after)),
         out_specs=IN_VMEM,
         out_shape=jax.ShapeDtypeStruct((rows, extent), BF16),
         compiler_params=params(),
         cost_estimate=cost(1, 1),
         name="input_grad",
-    )(member, held(conv), held(weights), *operands[2:])
+    )(member, held(conv), held(weights), *operands[2:], *map(held, after))
 
 
 def join(pieces, depth):
@@ -522,9 +506,12 @@
             for s in range(sections)
             for m in range(members)
         ]
-        for first_column, extent in cuts_of(AWAY_CUTS if k else OWN_CUTS, depth):
+        cuts = cuts_of(AWAY_CUTS if k else OWN_CUTS, depth)
+        for first_column, extent in cuts:
+            last = k == 0 and first_column + extent == depth and members > 1
             share = input_grad(
-                conv, weights, owner(k), first_column, extent, depth, None if k else grad
+                conv, weights, owner(k), first_column, extent, depth,
+                None if k else grad, (pieces[0][1],) if last else (),
             )
             pieces.append((first_column, lax.ppermute(share, ("section", "tp"), pairs)))
     return join(pieces, depth).reshape(block_input.shape)

time: 108 us -> 88.3 us (0.82)
  local copies, waits for them, and re-layouts: 15.4 us -> 0 us
  Pallas kernels: 69.8 us -> 66.1 us
    unnamed x4 -> x0, local copies, waits for them, and re-layouts: 15.4 us -> none
    pallas_call x1, Pallas kernels: 27.4 us -> 22.7 us  [mixer(): pl.pallas_call(functools.partial(mixer_kernel, members=members, micro=mic...]
    pallas_call x3 -> x4, Pallas kernels: 19 us -> 19.9 us  [input_grad(): pl.pallas_call(functools.partial(input_grad_kernel, first=first, depth=de...]
    ppermute x3 -> x4, waiting for transfers between devices: 12 us -> 11.8 us  [local(): pieces.append((first_column, lax.ppermute(share, ('section', 'tp'), pairs)))]
    ppermute x3 -> x4, starting transfers between devices: 7.23 us -> 7.24 us  [local(): pieces.append((first_column, lax.ppermute(share, ('section', 'tp'), pairs)))]
  transfers between devices with their start and end apart: 4 -> 5, of which waited for: 3 -> 3; matrix products, arithmetic and copies ran while one was open for 0% -> 0% of each run, Pallas kernels for 31% -> 45%
where the time goes in v6:
time: 88.3 us; the launch traced here: 88.1 us
  Pallas kernels  66.1 us (75%)
  waiting for transfers between devices  12.6 us (14%)
  starting transfers between devices  9.28 us (11%)
    pallas_call x1, Pallas kernels, mixer(): pl.pallas_call(functools.partial(mixer_kernel, members=members, micro=mic...  22.7 us
    pallas_call x1, Pallas kernels, load(): pl.pallas_call(functools.partial(load_kernel, members=members, width=widt...  22.3 us
    pallas_call x4, Pallas kernels, input_grad(): pl.pallas_call(functools.partial(input_grad_kernel, first=first, depth=de...  19.9 us
    ppermute x4, waiting for transfers between devices, local(): pieces.append((first_column, lax.ppermute(share, ('section', 'tp'), pairs)))  11.8 us
    ppermute x4, starting transfers between devices, local(): pieces.append((first_column, lax.ppermute(share, ('section', 'tp'), pairs)))  7.24 us
    ppermute x1, starting transfers between devices, local(): others.append(lax.ppermute(x, 'tp', pairs))  2.04 us
  transfers between devices with their start and end apart: 5, of which 3 were waited for; matrix products, arithmetic and copies ran while one was open for 0% of the time, Pallas kernels for 45%

profile of v6, /device:TPU:1, one launch (start us, length us, event | category | flops | bytes accessed | tf_op | source)
XLA Modules:
  0.0 88.1 jit_solution(867997427682575986)
XLA Ops:
  0.0 2.0 %collective-permute-start = (bf16[256,2048]{1,0:T(8,128)(2,1)}, bf16[256,2048]{1,0:T(8,128)(2,1)S(1)}, u32[]{:S(2)}, u32[]{:S(2)}) collective-permute-start(bf16[256,2048]{1,0:T(8,128)(2,1)} %bitcast.14), channel_id=1, source_target_pairs={{1,0},{0,1},{3,2},{2,3},{5,4},{4,5},{7,6},{6,7},{9,8},{8,9},{11,10... | collective-permute-start | bytes 3145736 | tf_op jit(solution)/shard_map/ppermute | solution.py:496
  2.0 22.3 %load.1 = (bf16[3,4096,2048]{2,1,0:T(8,128)(2,1)S(1)}, f32[3,256,2048]{2,1,0:T(8,128)}, bf16[128,16384]{1,0:T(8,128)(2,1)}, bf16[128,16384]{1,0:T(8,128)(2,1)}) custom-call(s32[1]{0:T(128)} %bitcast.1.me_ref.member_ref, bf16[256,2048]{1,0:T(8,128)(2,1)} %bitcast.15, bf16[3,4096,2048]{2,1,0:T(8,128)(2,1)} %bitcast.10, f32[128,128]{1,0:T(8,128)} %bitcast.17), custom_call_target="tpu_custom_call" | custom-call | flops 6442450944 | bytes 50331648 | tf_op jit(solution)/shard_map/load/pallas_call | solution.py:154
  24.3 0.8 collective-permute-done.rest_0_
  25.1 22.7 %mixer.1.conv_ref = bf16[3,256,2048]{2,1,0:T(8,128)(2,1)S(1)} custom-call(s32[1]{0:T(128)} %bitcast.1.me_ref.member_ref, bf16[3,4096,2048]{2,1,0:T(8,128)(2,1)S(1)} %get-tuple-element.9.w_ref, f32[336,128]{1,0:T(8,128)} %bitcast.16, f32[1,2048]{1,0:T(1,128)} %skip_ref.1, bf16[256,2048]{1,0:T(8,128)(2,1)} %bitcast.11, ...), custom_call_target="tpu_custom_call" | custom-call | bytes 9437184 | tf_op jit(solution)/shard_map/mixer/pallas_call | solution.py:382
  47.9 2.6 %input_grad.4 = bf16[256,512]{1,0:T(8,128)(2,1)} custom-call(s32[1]{0:T(128)} %bitcast.member_ref, bf16[3,256,2048]{2,1,0:T(8,128)(2,1)S(1)} %mixer.1.conv_ref, bf16[3,4096,2048]{2,1,0:T(8,128)(2,1)S(1)} %get-tuple-element.9.w_ref), custom_call_target="tpu_custom_call" | custom-call | flops 1 | bytes 1 | tf_op jit(solution)/shard_map/input_grad/pallas_call | solution.py:434
  50.5 2.6 %collective-permute-start.1 = (bf16[256,512]{1,0:T(8,128)(2,1)}, bf16[256,512]{1,0:T(8,128)(2,1)S(1)}, u32[]{:S(2)}, u32[]{:S(2)}) collective-permute-start(bf16[256,512]{1,0:T(8,128)(2,1)} %input_grad.4), channel_id=1, source_target_pairs={{0,31},{1,30},{2,1},{3,0},{4,3},{5,2},{6,5},{7,4},{8,7},{9,6},{10,... | collective-permute-start | bytes 786440 | tf_op jit(solution)/shard_map/ppermute | solution.py:516
  53.1 6.0 %input_grad.5 = bf16[256,1536]{1,0:T(8,128)(2,1)} custom-call(s32[1]{0:T(128)} %bitcast.member_ref, bf16[3,256,2048]{2,1,0:T(8,128)(2,1)S(1)} %mixer.1.conv_ref, bf16[3,4096,2048]{2,1,0:T(8,128)(2,1)S(1)} %get-tuple-element.9.w_ref), custom_call_target="tpu_custom_call" | custom-call | flops 1 | bytes 1 | tf_op jit(solution)/shard_map/input_grad/pallas_call | solution.py:434
  59.2 3.1 %collective-permute-start.2 = (bf16[256,1536]{1,0:T(8,128)(2,1)}, bf16[256,1536]{1,0:T(8,128)(2,1)S(1)}, u32[]{:S(2)}, u32[]{:S(2)}) collective-permute-start(bf16[256,1536]{1,0:T(8,128)(2,1)} %input_grad.5), channel_id=1, source_target_pairs={{0,31},{1,30},{2,1},{3,0},{4,3},{5,2},{6,5},{7,4},{8,7},{9,6},{10,... | collective-permute-start | bytes 2359304 | tf_op jit(solution)/shard_map/ppermute | solution.py:516
  62.3 5.6 %input_grad.6 = bf16[256,1024]{1,0:T(8,128)(2,1)} custom-call(s32[1]{0:T(128)} %bitcast.1.me_ref.member_ref, bf16[3,256,2048]{2,1,0:T(8,128)(2,1)S(1)} %mixer.1.conv_ref, bf16[3,4096,2048]{2,1,0:T(8,128)(2,1)S(1)} %get-tuple-element.9.w_ref, bf16[256,2048]{1,0:T(8,128)(2,1)} %bitcast.12), custom_call_target="tpu_custom_call" | custom-call | flops 1 | bytes 1 | tf_op jit(solution)/shard_map/input_grad/pallas_call | solution.py:434
  67.9 1.6 %collective-permute-start.3 = (bf16[256,1024]{1,0:T(8,128)(2,1)}, bf16[256,1024]{1,0:T(8,128)(2,1)S(1)}, u32[]{:S(2)}, u32[]{:S(2)}) collective-permute-start(bf16[256,1024]{1,0:T(8,128)(2,1)} %input_grad.6), channel_id=1, source_target_pairs={{0,30},{1,31},{2,0},{3,1},{4,2},{5,3},{6,4},{7,5},{8,6},{9,7},{10,... | collective-permute-start | bytes 1572872 | tf_op jit(solution)/shard_map/ppermute | solution.py:516
  69.4 0.0 collective-permute-done.1.rest_1_.refs_0_
  69.4 5.6 %input_grad.7 = bf16[256,1024]{1,0:T(8,128)(2,1)} custom-call(s32[1]{0:T(128)} %bitcast.1.me_ref.member_ref, bf16[3,256,2048]{2,1,0:T(8,128)(2,1)S(1)} %mixer.1.conv_ref, bf16[3,4096,2048]{2,1,0:T(8,128)(2,1)S(1)} %get-tuple-element.9.w_ref, bf16[256,2048]{1,0:T(8,128)(2,1)} %bitcast.13, bf16[256,512]{1,0:T(8,128)(2,1)S(1)} %collective-permute-done.1.rest_1_.refs_0_), custom_call_target="tpu_custom_call" | custom-call | flops 1 | bytes 1 | tf_op jit(solution)/shard_map/input_grad/pallas_call | solution.py:434
  75.0 0.0 collective-permute-start.4
  75.0 6.3 %collective-permute-done.3.refs_2_ = bf16[256,1024]{1,0:T(8,128)(2,1)S(1)} collective-permute-done((bf16[256,1024]{1,0:T(8,128)(2,1)}, bf16[256,1024]{1,0:T(8,128)(2,1)S(1)}, u32[]{:S(2)}, u32[]{:S(2)}) %collective-permute-start.3) | collective-permute-done | bytes 524320 | tf_op jit(solution)/shard_map/ppermute | solution.py:516
  81.4 5.5 %collective-permute-done.4.refs_3_ = bf16[256,1024]{1,0:T(8,128)(2,1)S(1)} collective-permute-done((bf16[256,1024]{1,0:T(8,128)(2,1)}, bf16[256,1024]{1,0:T(8,128)(2,1)S(1)}, u32[]{:S(2)}, u32[]{:S(2)}) %collective-permute-start.4) | collective-permute-done | bytes 524320 | tf_op jit(solution)/shard_map/ppermute | solution.py:516
  86.8 0.0 collective-permute-done.2.refs_1_
  86.8 1.2 %join.1 = bf16[256,2048]{1,0:T(8,128)(2,1)} custom-call(bf16[256,512]{1,0:T(8,128)(2,1)S(1)} %collective-permute-done.1.rest_1_.refs_0_, bf16[256,1536]{1,0:T(8,128)(2,1)S(1)} %collective-permute-done.2.refs_1_, bf16[256,1024]{1,0:T(8,128)(2,1)S(1)} %collective-permute-done.3.refs_2_, bf16[256,1024]{1,0:T(8,128)(2,1)S(1)} %collective-permute-done.4.refs_3_), custom_call_target="tpu_custom_call" | custom-call | bytes 3145728 | tf_op jit(solution)/shard_map/join/pallas_call | solution.py:460
Async XLA Ops:
  0.0 25.1 %collective-permute-start = (bf16[256,2048]{1,0:T(8,128)(2,1)}, bf16[256,2048]{1,0:T(8,128)(2,1)S(1)}, u32[]{:S(2)}, u32[]{:S(2)}) collective-permute-start(bf16[256,2048]{1,0:T(8,128)(2,1)} %bitcast.14), channel_id=1, source_target_pairs={{1,0},{0,1},{3,2},{2,3},{5,4},{4,5},{7,6},{6,7},{9,8},{8,9},{11,10... | collective-permute-start | bytes 3145736 | tf_op jit(solution)/shard_map/ppermute | solution.py:496
  50.5 18.9 %collective-permute-start.1 = (bf16[256,512]{1,0:T(8,128)(2,1)}, bf16[256,512]{1,0:T(8,128)(2,1)S(1)}, u32[]{:S(2)}, u32[]{:S(2)}) collective-permute-start(bf16[256,512]{1,0:T(8,128)(2,1)} %input_grad.4), channel_id=1, source_target_pairs={{0,31},{1,30},{2,1},{3,0},{4,3},{5,2},{6,5},{7,4},{8,7},{9,6},{10,... | collective-permute-start | bytes 786440 | tf_op jit(solution)/shard_map/ppermute | solution.py:516
  59.2 27.7 %collective-permute-start.2 = (bf16[256,1536]{1,0:T(8,128)(2,1)}, bf16[256,1536]{1,0:T(8,128)(2,1)S(1)}, u32[]{:S(2)}, u32[]{:S(2)}) collective-permute-start(bf16[256,1536]{1,0:T(8,128)(2,1)} %input_grad.5), channel_id=1, source_target_pairs={{0,31},{1,30},{2,1},{3,0},{4,3},{5,2},{6,5},{7,4},{8,7},{9,6},{10,... | collective-permute-start | bytes 2359304 | tf_op jit(solution)/shard_map/ppermute | solution.py:516
  67.9 13.5 %collective-permute-start.3 = (bf16[256,1024]{1,0:T(8,128)(2,1)}, bf16[256,1024]{1,0:T(8,128)(2,1)S(1)}, u32[]{:S(2)}, u32[]{:S(2)}) collective-permute-start(bf16[256,1024]{1,0:T(8,128)(2,1)} %input_grad.6), channel_id=1, source_target_pairs={{0,30},{1,31},{2,0},{3,1},{4,2},{5,3},{6,4},{7,5},{8,6},{9,7},{10,... | collective-permute-start | bytes 1572872 | tf_op jit(solution)/shard_map/ppermute | solution.py:516
  75.0 11.8 %collective-permute-start.4 = (bf16[256,1024]{1,0:T(8,128)(2,1)}, bf16[256,1024]{1,0:T(8,128)(2,1)S(1)}, u32[]{:S(2)}, u32[]{:S(2)}) collective-permute-start(bf16[256,1024]{1,0:T(8,128)(2,1)} %input_grad.7), channel_id=1, source_target_pairs={{0,30},{1,31},{2,0},{3,1},{4,2},{5,3},{6,4},{7,5},{8,6},{9,7},{10,... | collective-permute-start | bytes 1572872 | tf_op jit(solution)/shard_map/ppermute | solution.py:516

commit v7 on v6

--- a/solution.py
+++ b/solution.py
@@ -13,8 +13,8 @@
 MIB = 1024 * 1024
 VMEM_LIMIT = 8 * MIB
 SPAN = 256
-AWAY_CUTS = (2, 6)
-OWN_CUTS = (4, 4)
+AWAY_CUTS = (3, 5)
+OWN_CUTS = (5, 3)
 
 IN_VMEM = pl.BlockSpec(memory_space=pltpu.VMEM)
 IN_SMEM = pl.BlockSpec(memory_space=pltpu.SMEM)
@@ -441,7 +441,7 @@
         compiler_params=params(),
         cost_estimate=cost(1, 1),
         name="input_grad",
-    )(member, held(conv), held(weights), *operands[2:], *map(held, after))
+    )(member, held(conv), held(weights), *map(held, operands[2:]), *map(held, after))
 
 
 def join(pieces, depth):

time: 88.3 us -> 89.6 us (1.015)
  Pallas kernels: 66.1 us -> 63.6 us
  local copies, waits for them, and re-layouts: 0 us -> 2.2 us
  waiting for transfers between devices: 12.6 us -> 14.3 us
    pallas_call x4, Pallas kernels: 19.9 us -> 17.4 us  [input_grad(): pl.pallas_call(functools.partial(input_grad_kernel, first=first, depth=de...]
    unnamed x0 -> x6, local copies, waits for them, and re-layouts: none -> 2.2 us
    ppermute x4, waiting for transfers between devices: 11.8 us -> 13.5 us  [local(): pieces.append((first_column, lax.ppermute(share, ('section', 'tp'), pairs)))]
  transfers between devices with their start and end apart: 5 -> 5, of which waited for: 3 -> 5; matrix products, arithmetic and copies ran while one was open for 0% -> 0% of each run, Pallas kernels for 45% -> 40%
where the time goes in v7:
time: 89.6 us; the launch traced here: 89.4 us
  Pallas kernels  63.6 us (71%)
  waiting for transfers between devices  14.3 us (16%)
  starting transfers between devices  9.27 us (10%)
  local copies, waits for them, and re-layouts  2.2 us (2%)
    pallas_call x1, Pallas kernels, mixer(): pl.pallas_call(functools.partial(mixer_kernel, members=members, micro=mic...  22.8 us
    pallas_call x1, Pallas kernels, load(): pl.pallas_call(functools.partial(load_kernel, members=members, width=widt...  22.2 us
    pallas_call x4, Pallas kernels, input_grad(): pl.pallas_call(functools.partial(input_grad_kernel, first=first, depth=de...  17.4 us
    ppermute x4, waiting for transfers between devices, local(): pieces.append((first_column, lax.ppermute(share, ('section', 'tp'), pairs)))  13.5 us
    ppermute x4, starting transfers between devices, local(): pieces.append((first_column, lax.ppermute(share, ('section', 'tp'), pairs)))  7.23 us
    unnamed x6, local copies, waits for them, and re-layouts  2.2 us
    ppermute x1, starting transfers between devices, local(): others.append(lax.ppermute(x, 'tp', pairs))  2.04 us
  transfers between devices with their start and end apart: 5, of which 5 were waited for; matrix products, arithmetic and copies ran while one was open for 0% of the time, Pallas kernels for 40%

profile of v7, /device:TPU:1, one launch (start us, length us, event | category | flops | bytes accessed | tf_op | source)
XLA Modules:
  0.0 89.4 jit_solution(8211229152362807360)
XLA Ops:
  0.0 2.0 %collective-permute-start = (bf16[256,2048]{1,0:T(8,128)(2,1)}, bf16[256,2048]{1,0:T(8,128)(2,1)S(1)}, u32[]{:S(2)}, u32[]{:S(2)}) collective-permute-start(bf16[256,2048]{1,0:T(8,128)(2,1)} %bitcast.14), channel_id=1, source_target_pairs={{1,0},{0,1},{3,2},{2,3},{5,4},{4,5},{7,6},{6,7},{9,8},{8,9},{11,10... | collective-permute-start | bytes 3145736 | tf_op jit(solution)/shard_map/ppermute | solution.py:496
  2.0 22.2 %load.1 = (bf16[3,4096,2048]{2,1,0:T(8,128)(2,1)S(1)}, f32[3,256,2048]{2,1,0:T(8,128)}, bf16[128,16384]{1,0:T(8,128)(2,1)}, bf16[128,16384]{1,0:T(8,128)(2,1)}) custom-call(s32[1]{0:T(128)} %bitcast.1.me_ref.member_ref, bf16[256,2048]{1,0:T(8,128)(2,1)} %bitcast.15, bf16[3,4096,2048]{2,1,0:T(8,128)(2,1)} %bitcast.13, f32[128,128]{1,0:T(8,128)} %bitcast.17), custom_call_target="tpu_custom_call" | custom-call | flops 6442450944 | bytes 50331648 | tf_op jit(solution)/shard_map/load/pallas_call | solution.py:154
  24.3 0.8 collective-permute-done.rest_0_
  25.1 0.0 copy-start.1
  25.1 1.0 %copy-done.1 = bf16[256,2048]{1,0:T(8,128)(2,1)} copy-done((bf16[256,2048]{1,0:T(8,128)(2,1)}, bf16[256,2048]{1,0:T(8,128)(2,1)S(1)}, u32[]{:S(2)}) %copy-start.1) | copy-done | bytes 1048600
  26.1 0.0 copy-start.2
  26.1 1.2 %copy-done.2 = bf16[256,2048]{1,0:T(8,128)(2,1)S(1)} copy-done((bf16[256,2048]{1,0:T(8,128)(2,1)S(1)}, bf16[256,2048]{1,0:T(8,128)(2,1)}, u32[]{:S(2)}) %copy-start.2) | copy-done | bytes 1048600
  27.3 22.8 %mixer.1.conv_ref = bf16[3,256,2048]{2,1,0:T(8,128)(2,1)S(1)} custom-call(s32[1]{0:T(128)} %bitcast.1.me_ref.member_ref, bf16[3,4096,2048]{2,1,0:T(8,128)(2,1)S(1)} %get-tuple-element.9.w_ref, f32[336,128]{1,0:T(8,128)} %bitcast.16, f32[1,2048]{1,0:T(1,128)} %skip_ref.1, bf16[256,2048]{1,0:T(8,128)(2,1)} %bitcast.10, ...), custom_call_target="tpu_custom_call" | custom-call | bytes 9437184 | tf_op jit(solution)/shard_map/mixer/pallas_call | solution.py:382
  50.1 3.5 %input_grad.4 = bf16[256,768]{1,0:T(8,128)(2,1)} custom-call(s32[1]{0:T(128)} %bitcast.member_ref, bf16[3,256,2048]{2,1,0:T(8,128)(2,1)S(1)} %mixer.1.conv_ref, bf16[3,4096,2048]{2,1,0:T(8,128)(2,1)S(1)} %get-tuple-element.9.w_ref), custom_call_target="tpu_custom_call" | custom-call | flops 1 | bytes 1 | tf_op jit(solution)/shard_map/input_grad/pallas_call | solution.py:434
  53.6 0.0 copy-start
  53.6 2.6 %collective-permute-start.1 = (bf16[256,768]{1,0:T(8,128)(2,1)}, bf16[256,768]{1,0:T(8,128)(2,1)S(1)}, u32[]{:S(2)}, u32[]{:S(2)}) collective-permute-start(bf16[256,768]{1,0:T(8,128)(2,1)} %input_grad.4), channel_id=1, source_target_pairs={{0,31},{1,30},{2,1},{3,0},{4,3},{5,2},{6,5},{7,4},{8,7},{9,6},{10,... | collective-permute-start | bytes 1179656 | tf_op jit(solution)/shard_map/ppermute | solution.py:516
  56.1 5.2 %input_grad.5 = bf16[256,1280]{1,0:T(8,128)(2,1)} custom-call(s32[1]{0:T(128)} %bitcast.member_ref, bf16[3,256,2048]{2,1,0:T(8,128)(2,1)S(1)} %mixer.1.conv_ref, bf16[3,4096,2048]{2,1,0:T(8,128)(2,1)S(1)} %get-tuple-element.9.w_ref), custom_call_target="tpu_custom_call" | custom-call | flops 1 | bytes 1 | tf_op jit(solution)/shard_map/input_grad/pallas_call | solution.py:434
  61.3 3.1 %collective-permute-start.2 = (bf16[256,1280]{1,0:T(8,128)(2,1)}, bf16[256,1280]{1,0:T(8,128)(2,1)S(1)}, u32[]{:S(2)}, u32[]{:S(2)}) collective-permute-start(bf16[256,1280]{1,0:T(8,128)(2,1)} %input_grad.5), channel_id=1, source_target_pairs={{0,31},{1,30},{2,1},{3,0},{4,3},{5,2},{6,5},{7,4},{8,7},{9,6},{10,... | collective-permute-start | bytes 1966088 | tf_op jit(solution)/shard_map/ppermute | solution.py:516
  64.4 0.0 copy-done
  64.4 5.2 %input_grad.6 = bf16[256,1280]{1,0:T(8,128)(2,1)} custom-call(s32[1]{0:T(128)} %bitcast.1.me_ref.member_ref, bf16[3,256,2048]{2,1,0:T(8,128)(2,1)S(1)} %mixer.1.conv_ref, bf16[3,4096,2048]{2,1,0:T(8,128)(2,1)S(1)} %get-tuple-element.9.w_ref, bf16[256,2048]{1,0:T(8,128)(2,1)S(1)} %bitcast.11), custom_call_target="tpu_custom_call" | custom-call | flops 1 | bytes 1 | tf_op jit(solution)/shard_map/input_grad/pallas_call | solution.py:434
  69.7 1.5 %collective-permute-start.3 = (bf16[256,1280]{1,0:T(8,128)(2,1)}, bf16[256,1280]{1,0:T(8,128)(2,1)S(1)}, u32[]{:S(2)}, u32[]{:S(2)}) collective-permute-start(bf16[256,1280]{1,0:T(8,128)(2,1)} %input_grad.6), channel_id=1, source_target_pairs={{0,30},{1,31},{2,0},{3,1},{4,2},{5,3},{6,4},{7,5},{8,6},{9,7},{10,... | collective-permute-start | bytes 1966088 | tf_op jit(solution)/shard_map/ppermute | solution.py:516
  71.2 1.2 %collective-permute-done.1.rest_1_.refs_0_ = bf16[256,768]{1,0:T(8,128)(2,1)S(1)} collective-permute-done((bf16[256,768]{1,0:T(8,128)(2,1)}, bf16[256,768]{1,0:T(8,128)(2,1)S(1)}, u32[]{:S(2)}, u32[]{:S(2)}) %collective-permute-start.1) | collective-permute-done | bytes 393248 | tf_op jit(solution)/shard_map/ppermute | solution.py:516
  72.4 3.5 %input_grad.7 = bf16[256,768]{1,0:T(8,128)(2,1)} custom-call(s32[1]{0:T(128)} %bitcast.1.me_ref.member_ref, bf16[3,256,2048]{2,1,0:T(8,128)(2,1)S(1)} %mixer.1.conv_ref, bf16[3,4096,2048]{2,1,0:T(8,128)(2,1)S(1)} %get-tuple-element.9.w_ref, bf16[256,2048]{1,0:T(8,128)(2,1)S(1)} %bitcast.12, bf16[256,768]{1,0:T(8,128)(2,1)S(1)} %collective-permute-done.1.rest_1_.refs_0_), custom_call_target="tpu_custom_call" | custom-call | flops 1 | bytes 1 | tf_op jit(solution)/shard_map/input_grad/pallas_call | solution.py:434
  76.0 0.0 collective-permute-start.4
  76.0 5.1 %collective-permute-done.2.refs_1_ = bf16[256,1280]{1,0:T(8,128)(2,1)S(1)} collective-permute-done((bf16[256,1280]{1,0:T(8,128)(2,1)}, bf16[256,1280]{1,0:T(8,128)(2,1)S(1)}, u32[]{:S(2)}, u32[]{:S(2)}) %collective-permute-start.2) | collective-permute-done | bytes 655392 | tf_op jit(solution)/shard_map/ppermute | solution.py:516
  81.1 2.9 %collective-permute-done.3.refs_2_ = bf16[256,1280]{1,0:T(8,128)(2,1)S(1)} collective-permute-done((bf16[256,1280]{1,0:T(8,128)(2,1)}, bf16[256,1280]{1,0:T(8,128)(2,1)S(1)}, u32[]{:S(2)}, u32[]{:S(2)}) %collective-permute-start.3) | collective-permute-done | bytes 655392 | tf_op jit(solution)/shard_map/ppermute | solution.py:516
  84.0 4.2 %collective-permute-done.4.refs_3_ = bf16[256,768]{1,0:T(8,128)(2,1)S(1)} collective-permute-done((bf16[256,768]{1,0:T(8,128)(2,1)}, bf16[256,768]{1,0:T(8,128)(2,1)S(1)}, u32[]{:S(2)}, u32[]{:S(2)}) %collective-permute-start.4) | collective-permute-done | bytes 393248 | tf_op jit(solution)/shard_map/ppermute | solution.py:516
  88.2 1.2 %join.1 = bf16[256,2048]{1,0:T(8,128)(2,1)} custom-call(bf16[256,768]{1,0:T(8,128)(2,1)S(1)} %collective-permute-done.1.rest_1_.refs_0_, bf16[256,1280]{1,0:T(8,128)(2,1)S(1)} %collective-permute-done.2.refs_1_, bf16[256,1280]{1,0:T(8,128)(2,1)S(1)} %collective-permute-done.3.refs_2_, bf16[256,768]{1,0:T(8,128)(2,1)S(1)} %collective-permute-done.4.refs_3_), custom_call_target="tpu_custom_call" | custom-call | bytes 3145728 | tf_op jit(solution)/shard_map/join/pallas_call | solution.py:460
Async XLA Ops:
  0.0 25.1 %collective-permute-start = (bf16[256,2048]{1,0:T(8,128)(2,1)}, bf16[256,2048]{1,0:T(8,128)(2,1)S(1)}, u32[]{:S(2)}, u32[]{:S(2)}) collective-permute-start(bf16[256,2048]{1,0:T(8,128)(2,1)} %bitcast.14), channel_id=1, source_target_pairs={{1,0},{0,1},{3,2},{2,3},{5,4},{4,5},{7,6},{6,7},{9,8},{8,9},{11,10... | collective-permute-start | bytes 3145736 | tf_op jit(solution)/shard_map/ppermute | solution.py:496
  25.1 1.0 %copy-start.1 = (bf16[256,2048]{1,0:T(8,128)(2,1)}, bf16[256,2048]{1,0:T(8,128)(2,1)S(1)}, u32[]{:S(2)}) copy-start(bf16[256,2048]{1,0:T(8,128)(2,1)S(1)} %collective-permute-done.rest_0_) | copy-start | bytes 3145732
  26.1 1.2 %copy-start.2 = (bf16[256,2048]{1,0:T(8,128)(2,1)S(1)}, bf16[256,2048]{1,0:T(8,128)(2,1)}, u32[]{:S(2)}) copy-start(bf16[256,2048]{1,0:T(8,128)(2,1)} %copy-done.1) | copy-start | bytes 3145732
  53.6 10.9 %copy-start = (bf16[1,2,128,2048]{3,2,1,0:T(8,128)(2,1)S(1)}, bf16[1,2,128,2048]{3,2,1,0:T(8,128)(2,1)}, u32[]{:S(2)}) copy-start(bf16[1,2,128,2048]{3,2,1,0:T(8,128)(2,1)} %param.7) | copy-start | bytes 3145732
  53.6 18.9 %collective-permute-start.1 = (bf16[256,768]{1,0:T(8,128)(2,1)}, bf16[256,768]{1,0:T(8,128)(2,1)S(1)}, u32[]{:S(2)}, u32[]{:S(2)}) collective-permute-start(bf16[256,768]{1,0:T(8,128)(2,1)} %input_grad.4), channel_id=1, source_target_pairs={{0,31},{1,30},{2,1},{3,0},{4,3},{5,2},{6,5},{7,4},{8,7},{9,6},{10,... | collective-permute-start | bytes 1179656 | tf_op jit(solution)/shard_map/ppermute | solution.py:516
  61.3 19.8 %collective-permute-start.2 = (bf16[256,1280]{1,0:T(8,128)(2,1)}, bf16[256,1280]{1,0:T(8,128)(2,1)S(1)}, u32[]{:S(2)}, u32[]{:S(2)}) collective-permute-start(bf16[256,1280]{1,0:T(8,128)(2,1)} %input_grad.5), channel_id=1, source_target_pairs={{0,31},{1,30},{2,1},{3,0},{4,3},{5,2},{6,5},{7,4},{8,7},{9,6},{10,... | collective-permute-start | bytes 1966088 | tf_op jit(solution)/shard_map/ppermute | solution.py:516
  69.7 14.3 %collective-permute-start.3 = (bf16[256,1280]{1,0:T(8,128)(2,1)}, bf16[256,1280]{1,0:T(8,128)(2,1)S(1)}, u32[]{:S(2)}, u32[]{:S(2)}) collective-permute-start(bf16[256,1280]{1,0:T(8,128)(2,1)} %input_grad.6), channel_id=1, source_target_pairs={{0,30},{1,31},{2,0},{3,1},{4,2},{5,3},{6,4},{7,5},{8,6},{9,7},{10,... | collective-permute-start | bytes 1966088 | tf_op jit(solution)/shard_map/ppermute | solution.py:516
  76.0 12.2 %collective-permute-start.4 = (bf16[256,768]{1,0:T(8,128)(2,1)}, bf16[256,768]{1,0:T(8,128)(2,1)S(1)}, u32[]{:S(2)}, u32[]{:S(2)}) collective-permute-start(bf16[256,768]{1,0:T(8,128)(2,1)} %input_grad.7), channel_id=1, source_target_pairs={{0,30},{1,31},{2,0},{3,1},{4,2},{5,3},{6,4},{7,5},{8,6},{9,7},{10,... | collective-permute-start | bytes 1179656 | tf_op jit(solution)/shard_map/ppermute | solution.py:516

commit v8 on v7

--- a/solution.py
+++ b/solution.py
@@ -196,7 +196,7 @@
 
 def mixer_kernel(
     me_ref, w_ref, taps_ref, skip_ref, grad_ref, so_far_ref, first_ref, second_ref, *rest,
-    members, micro, group, width
+    members, micro, group, width, wide
 ):
     x_refs = rest[: members - 1]
     (
@@ -212,40 +212,40 @@
     spread = LANES // group * length
     window = width // group * length
     blocks = channels // width
+    ratio = wide // width
     pairs = length // (2 * STRIP)
     margin = micro * STRIP
     masks = group_masks(group, micro * LANES)
 
-    def block_copies(n):
+    def so_far_copy(m):
+        lanes = pl.ds(pl.multiple_of(m * wide, wide), wide)
+        return pltpu.make_async_copy(so_far_ref.at[:, :, lanes], so_far, so_far_sem)
+
+    def grads_copy(n):
         slot = n % 2
         lanes = pl.ds(pl.multiple_of(n * width, width), width)
+        return pltpu.make_async_copy(grad_ref.at[:, lanes], grads.at[slot], grads_sem.at[slot])
+
+    def matrix_copies(n):
+        places = pl.ds(pl.multiple_of(n * window, window), window)
         return (
-            pltpu.make_async_copy(
-                so_far_ref.at[:, :, lanes], so_far.at[slot], so_far_sem.at[slot]
-            ),
-            pltpu.make_async_copy(grad_ref.at[:, lanes], grads.at[slot], grads_sem.at[slot]),
-        )
-
-    def matrix_copies(n):
-        wide = pl.ds(pl.multiple_of(n * window, window), window)
-        return (
-            pltpu.make_async_copy(first_ref.at[:, wide], first, first_sem),
-            pltpu.make_async_copy(second_ref.at[:, wide], second, second_sem),
+            pltpu.make_async_copy(first_ref.at[:, places], first, first_sem),
+            pltpu.make_async_copy(second_ref.at[:, places], second, second_sem),
         )
 
     def lanes_of(n, tile):
         return pl.ds(pl.multiple_of(n * width + tile * LANES, LANES), LANES)
 
-    def project(n):
-        lanes = pl.ds(pl.multiple_of(n * width, width), width)
+    def project(m):
+        lanes = pl.ds(pl.multiple_of(m * wide, wide), wide)
         for i in range(3):
-            total = so_far[n % 2, i]
+            total = so_far[i]
             for k, x_ref in enumerate(x_refs):
                 row = pl.multiple_of(lax.rem(me + k + 1, members) * depth, depth)
                 total = total + jnp.dot(
                     x_ref[...], w_ref[i, pl.ds(row, depth), lanes], preferred_element_type=F32
                 )
-            for tile in range(width // LANES):
+            for tile in range(wide // LANES):
                 for b in range(micro):
                     for start in range(0, length, STRIP):
                         first_row = margin + micro * start + b
@@ -256,7 +256,7 @@
 
     def forward(n, tile, taps):
         inner = slice(tile * LANES, (tile + 1) * LANES)
-        scratch = lagged.at[tile]
+        scratch = lagged.at[n % ratio * (width // LANES) + tile]
         for b in range(micro):
             place = slice(b * LANES, (b + 1) * LANES)
             for pair in range(pairs):
@@ -295,7 +295,7 @@
     def backward(n, tile, taps, mixed, product_grad):
         inner = slice(tile * LANES, (tile + 1) * LANES)
         lanes = lanes_of(n, tile)
-        scratch = lagged.at[tile]
+        scratch = lagged.at[n % ratio * (width // LANES) + tile]
         skip = jnp.broadcast_to(skip_ref[0:1, lanes], (STRIP, LANES))
         for b in range(micro):
             place = slice(b * LANES, (b + 1) * LANES)
@@ -330,22 +330,20 @@
                     ]
                     out_ref[i, span, lanes] = jnp.concatenate(strips, axis=0).astype(BF16)
 
-    for copy in block_copies(0):
-        copy.start()
-    zeros = jnp.zeros((width // LANES, 3, margin, LANES), F32)
+    so_far_copy(0).start()
+    grads_copy(0).start()
+    zeros = jnp.zeros((wide // LANES, 3, margin, LANES), F32)
     lagged[:, :, :margin, :] = zeros
     lagged[:, :, margin + micro * length :, :] = zeros
 
     def step(n, carry):
         @pl.when(n + 1 < blocks)
         def _():
-            for copy in block_copies(n + 1):
-                copy.start()
+            grads_copy(n + 1).start()
 
         for copy in matrix_copies(n):
             copy.start()
-        for copy in block_copies(n):
-            copy.wait()
+        grads_copy(n).wait()
         taps = []
         for tile in range(width // LANES):
             line = n * (width // LANES) + tile
@@ -358,7 +356,16 @@
                 ]
                 for i in range(3)
             ])
-        project(n)
+
+        @pl.when(n % ratio == 0)
+        def _():
+            so_far_copy(n // ratio).wait()
+            project(n // ratio)
+
+            @pl.when(n + ratio < blocks)
+            def _():
+                so_far_copy(n // ratio + 1).start()
+
         for tile in range(width // LANES):
             forward(n, tile, taps[tile])
         for copy in matrix_copies(n):
@@ -379,24 +386,25 @@
     width = min(256, channels)
     window = width // group * length
     tiles = width // LANES
+    wide = 2 * width if channels % (2 * width) == 0 else width
     return pl.pallas_call(
         functools.partial(
-            mixer_kernel, members=members, micro=micro, group=group, width=width
+            mixer_kernel, members=members, micro=micro, group=group, width=width, wide=wide
         ),
         in_specs=[IN_SMEM] + [IN_VMEM] * 3 + [ANYWHERE] * 4 + [IN_VMEM] * len(others),
         out_specs=IN_VMEM,
         out_shape=pltpu.VMEM(so_far.shape, BF16),
         scratch_shapes=[
-            pltpu.VMEM((2, 3, rows, width), F32),
+            pltpu.VMEM((3, rows, wide), F32),
             pltpu.VMEM((2, rows, width), BF16),
             pltpu.VMEM((length, window), BF16),
             pltpu.VMEM((length, window), BF16),
-            pltpu.VMEM((tiles, 3, micro * (length + 2 * STRIP), LANES), F32),
+            pltpu.VMEM((wide // LANES, 3, micro * (length + 2 * STRIP), LANES), F32),
             pltpu.VMEM((rows, width), F32),
             pltpu.VMEM((rows, width), F32),
             pltpu.VMEM((rows, width), F32),
             pltpu.VMEM((2, tiles, length, micro * LANES), BF16),
-            pltpu.SemaphoreType.DMA((2,)),
+            pltpu.SemaphoreType.DMA,
             pltpu.SemaphoreType.DMA((2,)),
             pltpu.SemaphoreType.DMA,
             pltpu.SemaphoreType.DMA,
@@ -441,7 +449,7 @@
         compiler_params=params(),
         cost_estimate=cost(1, 1),
         name="input_grad",
-    )(member, held(conv), held(weights), *map(held, operands[2:]), *map(held, after))
+    )(member, held(conv), held(weights), *operands[2:], *map(held, after))
 
 
 def join(pieces, depth):

time: 89.6 us -> 89.1 us (level)
  Pallas kernels: 63.6 us -> 67 us
  local copies, waits for them, and re-layouts: 2.2 us -> 0 us
  waiting for transfers between devices: 14.3 us -> 12.4 us
    pallas_call x4, Pallas kernels: 17.4 us -> 19.8 us  [input_grad(): pl.pallas_call(functools.partial(input_grad_kernel, first=first, depth=de...]
    unnamed x6 -> x0, local copies, waits for them, and re-layouts: 2.2 us -> none
    ppermute x4, waiting for transfers between devices: 13.5 us -> 11.6 us  [local(): pieces.append((first_column, lax.ppermute(share, ('section', 'tp'), pairs)))]
    pallas_call x1, Pallas kernels: 22.8 us -> 23.7 us  [mixer(): pl.pallas_call(functools.partial(mixer_kernel, members=members, micro=mic...]
  transfers between devices with their start and end apart: 5 -> 5, of which waited for: 5 -> 4; matrix products, arithmetic and copies ran while one was open for 0% -> 0% of each run, Pallas kernels for 40% -> 44%
where the time goes in v8:
time: 89.1 us; the launch traced here: 88.7 us
  Pallas kernels  67 us (75%)
  waiting for transfers between devices  12.4 us (14%)
  starting transfers between devices  9.28 us (10%)
    pallas_call x1, Pallas kernels, mixer(): pl.pallas_call(functools.partial(mixer_kernel, members=members, micro=mic...  23.7 us
    pallas_call x1, Pallas kernels, load(): pl.pallas_call(functools.partial(load_kernel, members=members, width=widt...  22.3 us
    pallas_call x4, Pallas kernels, input_grad(): pl.pallas_call(functools.partial(input_grad_kernel, first=first, depth=de...  19.8 us
    ppermute x4, waiting for transfers between devices, local(): pieces.append((first_column, lax.ppermute(share, ('section', 'tp'), pairs)))  11.6 us
    ppermute x4, starting transfers between devices, local(): pieces.append((first_column, lax.ppermute(share, ('section', 'tp'), pairs)))  7.24 us
    ppermute x1, starting transfers between devices, local(): others.append(lax.ppermute(x, 'tp', pairs))  2.04 us
  transfers between devices with their start and end apart: 5, of which 4 were waited for; matrix products, arithmetic and copies ran while one was open for 0% of the time, Pallas kernels for 44%

profile of v8, /device:TPU:1, one launch (start us, length us, event | category | flops | bytes accessed | tf_op | source)
XLA Modules:
  0.0 88.7 jit_solution(10180957556541441267)
XLA Ops:
  0.0 2.0 %collective-permute-start = (bf16[256,2048]{1,0:T(8,128)(2,1)}, bf16[256,2048]{1,0:T(8,128)(2,1)S(1)}, u32[]{:S(2)}, u32[]{:S(2)}) collective-permute-start(bf16[256,2048]{1,0:T(8,128)(2,1)} %bitcast.14), channel_id=1, source_target_pairs={{1,0},{0,1},{3,2},{2,3},{5,4},{4,5},{7,6},{6,7},{9,8},{8,9},{11,10... | collective-permute-start | bytes 3145736 | tf_op jit(solution)/shard_map/ppermute | solution.py:504
  2.0 22.3 %load.1 = (bf16[3,4096,2048]{2,1,0:T(8,128)(2,1)S(1)}, f32[3,256,2048]{2,1,0:T(8,128)}, bf16[128,16384]{1,0:T(8,128)(2,1)}, bf16[128,16384]{1,0:T(8,128)(2,1)}) custom-call(s32[1]{0:T(128)} %bitcast.1.me_ref.member_ref, bf16[256,2048]{1,0:T(8,128)(2,1)} %bitcast.15, bf16[3,4096,2048]{2,1,0:T(8,128)(2,1)} %bitcast.10, f32[128,128]{1,0:T(8,128)} %bitcast.17), custom_call_target="tpu_custom_call" | custom-call | flops 6442450944 | bytes 50331648 | tf_op jit(solution)/shard_map/load/pallas_call | solution.py:154
  24.3 0.8 collective-permute-done.rest_0_
  25.1 23.7 %mixer.1.conv_ref = bf16[3,256,2048]{2,1,0:T(8,128)(2,1)S(1)} custom-call(s32[1]{0:T(128)} %bitcast.1.me_ref.member_ref, bf16[3,4096,2048]{2,1,0:T(8,128)(2,1)S(1)} %get-tuple-element.9.w_ref, f32[336,128]{1,0:T(8,128)} %bitcast.16, f32[1,2048]{1,0:T(1,128)} %skip_ref.1, bf16[256,2048]{1,0:T(8,128)(2,1)} %bitcast.11, ...), custom_call_target="tpu_custom_call" | custom-call | bytes 9437184 | tf_op jit(solution)/shard_map/mixer/pallas_call | solution.py:390
  48.8 3.5 %input_grad.4 = bf16[256,768]{1,0:T(8,128)(2,1)} custom-call(s32[1]{0:T(128)} %bitcast.member_ref, bf16[3,256,2048]{2,1,0:T(8,128)(2,1)S(1)} %mixer.1.conv_ref, bf16[3,4096,2048]{2,1,0:T(8,128)(2,1)S(1)} %get-tuple-element.9.w_ref), custom_call_target="tpu_custom_call" | custom-call | flops 1 | bytes 1 | tf_op jit(solution)/shard_map/input_grad/pallas_call | solution.py:442
  52.3 2.6 %collective-permute-start.1 = (bf16[256,768]{1,0:T(8,128)(2,1)}, bf16[256,768]{1,0:T(8,128)(2,1)S(1)}, u32[]{:S(2)}, u32[]{:S(2)}) collective-permute-start(bf16[256,768]{1,0:T(8,128)(2,1)} %input_grad.4), channel_id=1, source_target_pairs={{0,31},{1,30},{2,1},{3,0},{4,3},{5,2},{6,5},{7,4},{8,7},{9,6},{10,... | collective-permute-start | bytes 1179656 | tf_op jit(solution)/shard_map/ppermute | solution.py:524
  54.8 5.2 %input_grad.5 = bf16[256,1280]{1,0:T(8,128)(2,1)} custom-call(s32[1]{0:T(128)} %bitcast.member_ref, bf16[3,256,2048]{2,1,0:T(8,128)(2,1)S(1)} %mixer.1.conv_ref, bf16[3,4096,2048]{2,1,0:T(8,128)(2,1)S(1)} %get-tuple-element.9.w_ref), custom_call_target="tpu_custom_call" | custom-call | flops 1 | bytes 1 | tf_op jit(solution)/shard_map/input_grad/pallas_call | solution.py:442
  60.0 3.1 %collective-permute-start.2 = (bf16[256,1280]{1,0:T(8,128)(2,1)}, bf16[256,1280]{1,0:T(8,128)(2,1)S(1)}, u32[]{:S(2)}, u32[]{:S(2)}) collective-permute-start(bf16[256,1280]{1,0:T(8,128)(2,1)} %input_grad.5), channel_id=1, source_target_pairs={{0,31},{1,30},{2,1},{3,0},{4,3},{5,2},{6,5},{7,4},{8,7},{9,6},{10,... | collective-permute-start | bytes 1966088 | tf_op jit(solution)/shard_map/ppermute | solution.py:524
  63.1 6.5 %input_grad.6 = bf16[256,1280]{1,0:T(8,128)(2,1)} custom-call(s32[1]{0:T(128)} %bitcast.1.me_ref.member_ref, bf16[3,256,2048]{2,1,0:T(8,128)(2,1)S(1)} %mixer.1.conv_ref, bf16[3,4096,2048]{2,1,0:T(8,128)(2,1)S(1)} %get-tuple-element.9.w_ref, bf16[256,2048]{1,0:T(8,128)(2,1)} %bitcast.12), custom_call_target="tpu_custom_call" | custom-call | flops 1 | bytes 1 | tf_op jit(solution)/shard_map/input_grad/pallas_call | solution.py:442
  69.6 1.5 %collective-permute-start.3 = (bf16[256,1280]{1,0:T(8,128)(2,1)}, bf16[256,1280]{1,0:T(8,128)(2,1)S(1)}, u32[]{:S(2)}, u32[]{:S(2)}) collective-permute-start(bf16[256,1280]{1,0:T(8,128)(2,1)} %input_grad.6), channel_id=1, source_target_pairs={{0,30},{1,31},{2,0},{3,1},{4,2},{5,3},{6,4},{7,5},{8,6},{9,7},{10,... | collective-permute-start | bytes 1966088 | tf_op jit(solution)/shard_map/ppermute | solution.py:524
  71.1 0.0 collective-permute-done.1.rest_1_.refs_0_
  71.2 4.7 %input_grad.7 = bf16[256,768]{1,0:T(8,128)(2,1)} custom-call(s32[1]{0:T(128)} %bitcast.1.me_ref.member_ref, bf16[3,256,2048]{2,1,0:T(8,128)(2,1)S(1)} %mixer.1.conv_ref, bf16[3,4096,2048]{2,1,0:T(8,128)(2,1)S(1)} %get-tuple-element.9.w_ref, bf16[256,2048]{1,0:T(8,128)(2,1)} %bitcast.13, bf16[256,768]{1,0:T(8,128)(2,1)S(1)} %collective-permute-done.1.rest_1_.refs_0_), custom_call_target="tpu_custom_call" | custom-call | flops 1 | bytes 1 | tf_op jit(solution)/shard_map/input_grad/pallas_call | solution.py:442
  75.9 0.0 collective-permute-start.4
  75.9 3.9 %collective-permute-done.2.refs_1_ = bf16[256,1280]{1,0:T(8,128)(2,1)S(1)} collective-permute-done((bf16[256,1280]{1,0:T(8,128)(2,1)}, bf16[256,1280]{1,0:T(8,128)(2,1)S(1)}, u32[]{:S(2)}, u32[]{:S(2)}) %collective-permute-start.2) | collective-permute-done | bytes 655392 | tf_op jit(solution)/shard_map/ppermute | solution.py:524
  79.8 3.5 %collective-permute-done.3.refs_2_ = bf16[256,1280]{1,0:T(8,128)(2,1)S(1)} collective-permute-done((bf16[256,1280]{1,0:T(8,128)(2,1)}, bf16[256,1280]{1,0:T(8,128)(2,1)S(1)}, u32[]{:S(2)}, u32[]{:S(2)}) %collective-permute-start.3) | collective-permute-done | bytes 655392 | tf_op jit(solution)/shard_map/ppermute | solution.py:524
  83.3 4.2 %collective-permute-done.4.refs_3_ = bf16[256,768]{1,0:T(8,128)(2,1)S(1)} collective-permute-done((bf16[256,768]{1,0:T(8,128)(2,1)}, bf16[256,768]{1,0:T(8,128)(2,1)S(1)}, u32[]{:S(2)}, u32[]{:S(2)}) %collective-permute-start.4) | collective-permute-done | bytes 393248 | tf_op jit(solution)/shard_map/ppermute | solution.py:524
  87.5 1.2 %join.1 = bf16[256,2048]{1,0:T(8,128)(2,1)} custom-call(bf16[256,768]{1,0:T(8,128)(2,1)S(1)} %collective-permute-done.1.rest_1_.refs_0_, bf16[256,1280]{1,0:T(8,128)(2,1)S(1)} %collective-permute-done.2.refs_1_, bf16[256,1280]{1,0:T(8,128)(2,1)S(1)} %collective-permute-done.3.refs_2_, bf16[256,768]{1,0:T(8,128)(2,1)S(1)} %collective-permute-done.4.refs_3_), custom_call_target="tpu_custom_call" | custom-call | bytes 3145728 | tf_op jit(solution)/shard_map/join/pallas_call | solution.py:468
Async XLA Ops:
  0.0 25.1 %collective-permute-start = (bf16[256,2048]{1,0:T(8,128)(2,1)}, bf16[256,2048]{1,0:T(8,128)(2,1)S(1)}, u32[]{:S(2)}, u32[]{:S(2)}) collective-permute-start(bf16[256,2048]{1,0:T(8,128)(2,1)} %bitcast.14), channel_id=1, source_target_pairs={{1,0},{0,1},{3,2},{2,3},{5,4},{4,5},{7,6},{6,7},{9,8},{8,9},{11,10... | collective-permute-start | bytes 3145736 | tf_op jit(solution)/shard_map/ppermute | solution.py:504
  52.3 18.9 %collective-permute-start.1 = (bf16[256,768]{1,0:T(8,128)(2,1)}, bf16[256,768]{1,0:T(8,128)(2,1)S(1)}, u32[]{:S(2)}, u32[]{:S(2)}) collective-permute-start(bf16[256,768]{1,0:T(8,128)(2,1)} %input_grad.4), channel_id=1, source_target_pairs={{0,31},{1,30},{2,1},{3,0},{4,3},{5,2},{6,5},{7,4},{8,7},{9,6},{10,... | collective-permute-start | bytes 1179656 | tf_op jit(solution)/shard_map/ppermute | solution.py:524
  60.0 19.8 %collective-permute-start.2 = (bf16[256,1280]{1,0:T(8,128)(2,1)}, bf16[256,1280]{1,0:T(8,128)(2,1)S(1)}, u32[]{:S(2)}, u32[]{:S(2)}) collective-permute-start(bf16[256,1280]{1,0:T(8,128)(2,1)} %input_grad.5), channel_id=1, source_target_pairs={{0,31},{1,30},{2,1},{3,0},{4,3},{5,2},{6,5},{7,4},{8,7},{9,6},{10,... | collective-permute-start | bytes 1966088 | tf_op jit(solution)/shard_map/ppermute | solution.py:524
  69.6 13.7 %collective-permute-start.3 = (bf16[256,1280]{1,0:T(8,128)(2,1)}, bf16[256,1280]{1,0:T(8,128)(2,1)S(1)}, u32[]{:S(2)}, u32[]{:S(2)}) collective-permute-start(bf16[256,1280]{1,0:T(8,128)(2,1)} %input_grad.6), channel_id=1, source_target_pairs={{0,30},{1,31},{2,0},{3,1},{4,2},{5,3},{6,4},{7,5},{8,6},{9,7},{10,... | collective-permute-start | bytes 1966088 | tf_op jit(solution)/shard_map/ppermute | solution.py:524
  75.9 11.6 %collective-permute-start.4 = (bf16[256,768]{1,0:T(8,128)(2,1)}, bf16[256,768]{1,0:T(8,128)(2,1)S(1)}, u32[]{:S(2)}, u32[]{:S(2)}) collective-permute-start(bf16[256,768]{1,0:T(8,128)(2,1)} %input_grad.7), channel_id=1, source_target_pairs={{0,30},{1,31},{2,0},{3,1},{4,2},{5,3},{6,4},{7,5},{8,6},{9,7},{10,... | collective-permute-start | bytes 1179656 | tf_op jit(solution)/shard_map/ppermute | solution.py:524

commit v9 on v7

--- a/solution.py
+++ b/solution.py
@@ -408,8 +408,14 @@
 
 
 def input_grad_kernel(member_ref, conv_ref, w_ref, *rest, first, depth, width, with_grad):
-    out_ref = rest[-1]
     start = member_ref[0] * depth + first
+    if with_grad:
+        out_ref, grad, grad_sem = rest[-3:]
+        columns = slice(first, first + out_ref.shape[1])
+        grad_copy = pltpu.make_async_copy(rest[0].at[:, columns], grad, grad_sem)
+        grad_copy.start()
+    else:
+        out_ref = rest[-1]
     for step in range(out_ref.shape[1] // width):
         place = slice(step * width, (step + 1) * width)
         row = pl.multiple_of(start + step * width, width)
@@ -424,7 +430,9 @@
             total = term if total is None else total + term
         total = total.T
         if with_grad:
-            total = total + rest[0][:, first + step * width : first + (step + 1) * width].astype(F32)
+            if step == 0:
+                grad_copy.wait()
+            total = total + grad[:, place].astype(F32)
         out_ref[:, place] = total.astype(BF16)
 
 
@@ -435,13 +443,18 @@
         functools.partial(
             input_grad_kernel, first=first, depth=depth, width=SPAN, with_grad=grad is not None
         ),
-        in_specs=[IN_SMEM] + [IN_VMEM] * (len(operands) + len(after)),
+        in_specs=[IN_SMEM, IN_VMEM, IN_VMEM]
+        + [ANYWHERE] * (len(operands) - 2)
+        + [IN_VMEM] * len(after),
         out_specs=IN_VMEM,
         out_shape=jax.ShapeDtypeStruct((rows, extent), BF16),
+        scratch_shapes=[]
+        if grad is None
+        else [pltpu.VMEM((rows, extent), BF16), pltpu.SemaphoreType.DMA],
         compiler_params=params(),
         cost_estimate=cost(1, 1),
         name="input_grad",
-    )(member, held(conv), held(weights), *map(held, operands[2:]), *map(held, after))
+    )(member, held(conv), held(weights), *operands[2:], *map(held, after))
 
 
 def join(pieces, depth):

time: 89.6 us -> 88 us (0.982)
  local copies, waits for them, and re-layouts: 2.2 us -> 0 us
  waiting for transfers between devices: 14.3 us -> 12.8 us
  Pallas kernels: 63.6 us -> 65 us
    unnamed x6 -> x0, local copies, waits for them, and re-layouts: 2.2 us -> none
    ppermute x4, waiting for transfers between devices: 13.5 us -> 12 us  [local(): pieces.append((first_column, lax.ppermute(share, ('section', 'tp'), pairs)))]
    pallas_call x4, Pallas kernels: 17.4 us -> 18.8 us  [input_grad(): pl.pallas_call(functools.partial(input_grad_kernel, first=first, depth=de...]
  transfers between devices with their start and end apart: 5 -> 5, of which waited for: 5 -> 4; matrix products, arithmetic and copies ran while one was open for 0% -> 0% of each run, Pallas kernels for 40% -> 43%
where the time goes in v9:
time: 88 us; the launch traced here: 87.8 us
  Pallas kernels  65 us (74%)
  waiting for transfers between devices  12.8 us (15%)
  starting transfers between devices  9.92 us (11%)
    pallas_call x1, Pallas kernels, mixer(): pl.pallas_call(functools.partial(mixer_kernel, members=members, micro=mic...  22.7 us
    pallas_call x1, Pallas kernels, load(): pl.pallas_call(functools.partial(load_kernel, members=members, width=widt...  22.3 us
    pallas_call x4, Pallas kernels, input_grad(): pl.pallas_call(functools.partial(input_grad_kernel, first=first, depth=de...  18.8 us
    ppermute x4, waiting for transfers between devices, local(): pieces.append((first_column, lax.ppermute(share, ('section', 'tp'), pairs)))  12 us
    ppermute x4, starting transfers between devices, local(): pieces.append((first_column, lax.ppermute(share, ('section', 'tp'), pairs)))  7.88 us
    ppermute x1, starting transfers between devices, local(): others.append(lax.ppermute(x, 'tp', pairs))  2.04 us
  transfers between devices with their start and end apart: 5, of which 4 were waited for; matrix products, arithmetic and copies ran while one was open for 0% of the time, Pallas kernels for 43%

profile of v9, /device:TPU:1, one launch (start us, length us, event | category | flops | bytes accessed | tf_op | source)
XLA Modules:
  0.0 87.8 jit_solution(17026693950450722308)
XLA Ops:
  0.0 2.0 %collective-permute-start = (bf16[256,2048]{1,0:T(8,128)(2,1)}, bf16[256,2048]{1,0:T(8,128)(2,1)S(1)}, u32[]{:S(2)}, u32[]{:S(2)}) collective-permute-start(bf16[256,2048]{1,0:T(8,128)(2,1)} %bitcast.14), channel_id=1, source_target_pairs={{1,0},{0,1},{3,2},{2,3},{5,4},{4,5},{7,6},{6,7},{9,8},{8,9},{11,10... | collective-permute-start | bytes 3145736 | tf_op jit(solution)/shard_map/ppermute | solution.py:509
  2.0 22.3 %load.1 = (bf16[3,4096,2048]{2,1,0:T(8,128)(2,1)S(1)}, f32[3,256,2048]{2,1,0:T(8,128)}, bf16[128,16384]{1,0:T(8,128)(2,1)}, bf16[128,16384]{1,0:T(8,128)(2,1)}) custom-call(s32[1]{0:T(128)} %bitcast.1.me_ref.member_ref, bf16[256,2048]{1,0:T(8,128)(2,1)} %bitcast.15, bf16[3,4096,2048]{2,1,0:T(8,128)(2,1)} %bitcast.10, f32[128,128]{1,0:T(8,128)} %bitcast.17), custom_call_target="tpu_custom_call" | custom-call | flops 6442450944 | bytes 50331648 | tf_op jit(solution)/shard_map/load/pallas_call | solution.py:154
  24.3 0.8 collective-permute-done.rest_0_
  25.1 22.7 %mixer.1.conv_ref = bf16[3,256,2048]{2,1,0:T(8,128)(2,1)S(1)} custom-call(s32[1]{0:T(128)} %bitcast.1.me_ref.member_ref, bf16[3,4096,2048]{2,1,0:T(8,128)(2,1)S(1)} %get-tuple-element.9.w_ref, f32[336,128]{1,0:T(8,128)} %bitcast.16, f32[1,2048]{1,0:T(1,128)} %skip_ref.1, bf16[256,2048]{1,0:T(8,128)(2,1)} %bitcast.11, ...), custom_call_target="tpu_custom_call" | custom-call | bytes 9437184 | tf_op jit(solution)/shard_map/mixer/pallas_call | solution.py:382
  47.9 3.5 %input_grad.4 = bf16[256,768]{1,0:T(8,128)(2,1)} custom-call(s32[1]{0:T(128)} %bitcast.member_ref, bf16[3,256,2048]{2,1,0:T(8,128)(2,1)S(1)} %mixer.1.conv_ref, bf16[3,4096,2048]{2,1,0:T(8,128)(2,1)S(1)} %get-tuple-element.9.w_ref), custom_call_target="tpu_custom_call" | custom-call | flops 1 | bytes 1 | tf_op jit(solution)/shard_map/input_grad/pallas_call | solution.py:442
  51.4 2.6 %collective-permute-start.1 = (bf16[256,768]{1,0:T(8,128)(2,1)}, bf16[256,768]{1,0:T(8,128)(2,1)S(1)}, u32[]{:S(2)}, u32[]{:S(2)}) collective-permute-start(bf16[256,768]{1,0:T(8,128)(2,1)} %input_grad.4), channel_id=1, source_target_pairs={{0,31},{1,30},{2,1},{3,0},{4,3},{5,2},{6,5},{7,4},{8,7},{9,6},{10,... | collective-permute-start | bytes 1179656 | tf_op jit(solution)/shard_map/ppermute | solution.py:529
  53.9 5.2 %input_grad.5 = bf16[256,1280]{1,0:T(8,128)(2,1)} custom-call(s32[1]{0:T(128)} %bitcast.member_ref, bf16[3,256,2048]{2,1,0:T(8,128)(2,1)S(1)} %mixer.1.conv_ref, bf16[3,4096,2048]{2,1,0:T(8,128)(2,1)S(1)} %get-tuple-element.9.w_ref), custom_call_target="tpu_custom_call" | custom-call | flops 1 | bytes 1 | tf_op jit(solution)/shard_map/input_grad/pallas_call | solution.py:442
  59.1 3.1 %collective-permute-start.2 = (bf16[256,1280]{1,0:T(8,128)(2,1)}, bf16[256,1280]{1,0:T(8,128)(2,1)S(1)}, u32[]{:S(2)}, u32[]{:S(2)}) collective-permute-start(bf16[256,1280]{1,0:T(8,128)(2,1)} %input_grad.5), channel_id=1, source_target_pairs={{0,31},{1,30},{2,1},{3,0},{4,3},{5,2},{6,5},{7,4},{8,7},{9,6},{10,... | collective-permute-start | bytes 1966088 | tf_op jit(solution)/shard_map/ppermute | solution.py:529
  62.2 6.4 %input_grad.6 = bf16[256,1280]{1,0:T(8,128)(2,1)} custom-call(s32[1]{0:T(128)} %bitcast.1.me_ref.member_ref, bf16[3,256,2048]{2,1,0:T(8,128)(2,1)S(1)} %mixer.1.conv_ref, bf16[3,4096,2048]{2,1,0:T(8,128)(2,1)S(1)} %get-tuple-element.9.w_ref, bf16[256,2048]{1,0:T(8,128)(2,1)} %bitcast.12), custom_call_target="tpu_custom_call" | custom-call | flops 1 | bytes 1 | tf_op jit(solution)/shard_map/input_grad/pallas_call | solution.py:442
  68.6 2.1 %collective-permute-start.3 = (bf16[256,1280]{1,0:T(8,128)(2,1)}, bf16[256,1280]{1,0:T(8,128)(2,1)S(1)}, u32[]{:S(2)}, u32[]{:S(2)}) collective-permute-start(bf16[256,1280]{1,0:T(8,128)(2,1)} %input_grad.6), channel_id=1, source_target_pairs={{0,30},{1,31},{2,0},{3,1},{4,2},{5,3},{6,4},{7,5},{8,6},{9,7},{10,... | collective-permute-start | bytes 1966088 | tf_op jit(solution)/shard_map/ppermute | solution.py:529
  70.7 0.0 collective-permute-done.1.rest_1_.refs_0_
  70.7 3.8 %input_grad.7 = bf16[256,768]{1,0:T(8,128)(2,1)} custom-call(s32[1]{0:T(128)} %bitcast.1.me_ref.member_ref, bf16[3,256,2048]{2,1,0:T(8,128)(2,1)S(1)} %mixer.1.conv_ref, bf16[3,4096,2048]{2,1,0:T(8,128)(2,1)S(1)} %get-tuple-element.9.w_ref, bf16[256,2048]{1,0:T(8,128)(2,1)} %bitcast.13, bf16[256,768]{1,0:T(8,128)(2,1)S(1)} %collective-permute-done.1.rest_1_.refs_0_), custom_call_target="tpu_custom_call" | custom-call | flops 1 | bytes 1 | tf_op jit(solution)/shard_map/input_grad/pallas_call | solution.py:442
  74.5 0.1 collective-permute-start.4
  74.6 4.3 %collective-permute-done.2.refs_1_ = bf16[256,1280]{1,0:T(8,128)(2,1)S(1)} collective-permute-done((bf16[256,1280]{1,0:T(8,128)(2,1)}, bf16[256,1280]{1,0:T(8,128)(2,1)S(1)}, u32[]{:S(2)}, u32[]{:S(2)}) %collective-permute-start.2) | collective-permute-done | bytes 655392 | tf_op jit(solution)/shard_map/ppermute | solution.py:529
  78.9 3.5 %collective-permute-done.3.refs_2_ = bf16[256,1280]{1,0:T(8,128)(2,1)S(1)} collective-permute-done((bf16[256,1280]{1,0:T(8,128)(2,1)}, bf16[256,1280]{1,0:T(8,128)(2,1)S(1)}, u32[]{:S(2)}, u32[]{:S(2)}) %collective-permute-start.3) | collective-permute-done | bytes 655392 | tf_op jit(solution)/shard_map/ppermute | solution.py:529
  82.4 4.2 %collective-permute-done.4.refs_3_ = bf16[256,768]{1,0:T(8,128)(2,1)S(1)} collective-permute-done((bf16[256,768]{1,0:T(8,128)(2,1)}, bf16[256,768]{1,0:T(8,128)(2,1)S(1)}, u32[]{:S(2)}, u32[]{:S(2)}) %collective-permute-start.4) | collective-permute-done | bytes 393248 | tf_op jit(solution)/shard_map/ppermute | solution.py:529
  86.6 1.2 %join.1 = bf16[256,2048]{1,0:T(8,128)(2,1)} custom-call(bf16[256,768]{1,0:T(8,128)(2,1)S(1)} %collective-permute-done.1.rest_1_.refs_0_, bf16[256,1280]{1,0:T(8,128)(2,1)S(1)} %collective-permute-done.2.refs_1_, bf16[256,1280]{1,0:T(8,128)(2,1)S(1)} %collective-permute-done.3.refs_2_, bf16[256,768]{1,0:T(8,128)(2,1)S(1)} %collective-permute-done.4.refs_3_), custom_call_target="tpu_custom_call" | custom-call | bytes 3145728 | tf_op jit(solution)/shard_map/join/pallas_call | solution.py:473
Async XLA Ops:
  0.0 25.1 %collective-permute-start = (bf16[256,2048]{1,0:T(8,128)(2,1)}, bf16[256,2048]{1,0:T(8,128)(2,1)S(1)}, u32[]{:S(2)}, u32[]{:S(2)}) collective-permute-start(bf16[256,2048]{1,0:T(8,128)(2,1)} %bitcast.14), channel_id=1, source_target_pairs={{1,0},{0,1},{3,2},{2,3},{5,4},{4,5},{7,6},{6,7},{9,8},{8,9},{11,10... | collective-permute-start | bytes 3145736 | tf_op jit(solution)/shard_map/ppermute | solution.py:509
  51.4 19.4 %collective-permute-start.1 = (bf16[256,768]{1,0:T(8,128)(2,1)}, bf16[256,768]{1,0:T(8,128)(2,1)S(1)}, u32[]{:S(2)}, u32[]{:S(2)}) collective-permute-start(bf16[256,768]{1,0:T(8,128)(2,1)} %input_grad.4), channel_id=1, source_target_pairs={{0,31},{1,30},{2,1},{3,0},{4,3},{5,2},{6,5},{7,4},{8,7},{9,6},{10,... | collective-permute-start | bytes 1179656 | tf_op jit(solution)/shard_map/ppermute | solution.py:529
  59.1 19.8 %collective-permute-start.2 = (bf16[256,1280]{1,0:T(8,128)(2,1)}, bf16[256,1280]{1,0:T(8,128)(2,1)S(1)}, u32[]{:S(2)}, u32[]{:S(2)}) collective-permute-start(bf16[256,1280]{1,0:T(8,128)(2,1)} %input_grad.5), channel_id=1, source_target_pairs={{0,31},{1,30},{2,1},{3,0},{4,3},{5,2},{6,5},{7,4},{8,7},{9,6},{10,... | collective-permute-start | bytes 1966088 | tf_op jit(solution)/shard_map/ppermute | solution.py:529
  68.6 13.8 %collective-permute-start.3 = (bf16[256,1280]{1,0:T(8,128)(2,1)}, bf16[256,1280]{1,0:T(8,128)(2,1)S(1)}, u32[]{:S(2)}, u32[]{:S(2)}) collective-permute-start(bf16[256,1280]{1,0:T(8,128)(2,1)} %input_grad.6), channel_id=1, source_target_pairs={{0,30},{1,31},{2,0},{3,1},{4,2},{5,3},{6,4},{7,5},{8,6},{9,7},{10,... | collective-permute-start | bytes 1966088 | tf_op jit(solution)/shard_map/ppermute | solution.py:529
  74.5 12.1 %collective-permute-start.4 = (bf16[256,768]{1,0:T(8,128)(2,1)}, bf16[256,768]{1,0:T(8,128)(2,1)S(1)}, u32[]{:S(2)}, u32[]{:S(2)}) collective-permute-start(bf16[256,768]{1,0:T(8,128)(2,1)} %input_grad.7), channel_id=1, source_target_pairs={{0,30},{1,31},{2,0},{3,1},{4,2},{5,3},{6,4},{7,5},{8,6},{9,7},{10,... | collective-permute-start | bytes 1179656 | tf_op jit(solution)/shard_map/ppermute | solution.py:529
